TPU v7x, 32 devices: a whole 2x2x4 slice. The times are simulated.
32 devices in a mesh: sub: 4 (over y, x), dom: 8 (over z, core).
Axes of the slice: x: 2, y: 2, z: 4, core: 2. Of those that a mesh axis runs over, the one named last changes fastest.
Arguments:
- reduced_basis: bfloat16 [8, 32, 3, 128, 128], P('dom', 'sub'), may hold values from -0.0690534 to 0.0690534
- gauss_stress: float32 [6, 8, 8, 32, 128], P(None, None, 'dom', 'sub'), may hold values from -6 to 6
- yield_flags: int32 [8, 8, 32, 128], P(None, 'dom', 'sub'), may hold values 0 or 1
- consolidation: float32 [8, 8, 32, 128], P(None, 'dom', 'sub'), may hold values from 0.5 to 3
- elastic_moduli: float32 [2, 8, 32, 128], P(None, 'dom', 'sub'), may hold values from 1 to 4
- element_sizes: float32 [3, 8, 32, 128], P(None, 'dom', 'sub'), may hold values from 0.5 to 2
Outputs:
- reduced_tangent: float32 [128, 128], replicated
- reduced_residual: float32 [128], replicated
All inputs are finite; a program needn't handle non-finite values. No bound on the sum of `yield_flags` on one device may be relied on, other than what follows from the above.
Results may differ from a plain program's by a relative error of at most 0.00055.
Values may be sent and summed in bfloat16 or wider, within the bound.
No kernel may reach another device: no remote copies, remote signals or barrier semaphores. Data moves between devices by JAX's collectives and lax.ppermute only.
A program may use at most 128 MiB of HBM per device.

v0:
```python
import functools

import jax
import jax.numpy as jnp
import numpy as np
from jax import lax
from jax.experimental import pallas as pl
from jax.experimental.pallas import tpu as pltpu
from jax.sharding import PartitionSpec as P

GAUSS_POINT = 0.5773502691896258
CRITICAL_SLOPE = 1.2
HARDENING = 0.5
VOIGT = ((0, 3, 5), (3, 1, 4), (5, 4, 2))
LINES = [(x, d) for x in range(2) for d in range(3)]
SAME_PAIRS = [(p, q) for p in range(6) for q in range(p, 6)]
NEXT_PAIRS = [(p, q) for p in range(6) for q in range(6)]
GROUP = 16


def corner_bits(corner):
    return (corner // 4, corner // 2 % 2, corner % 2)


def derivative_table():
    entries = np.zeros((8, 8, 3))
    for gauss_index in range(8):
        gauss_coords = [GAUSS_POINT * (2 * bit_value - 1) for bit_value in corner_bits(gauss_index)]
        for corner in range(8):
            corner_signs = [2 * bit_value - 1 for bit_value in corner_bits(corner)]
            for axis_index in range(3):
                entry_value = float(corner_signs[axis_index])
                for other_axis in range(3):
                    if other_axis != axis_index:
                        entry_value = (
                            entry_value
                            * (1.0 + corner_signs[other_axis] * gauss_coords[other_axis])
                            / 2.0
                        )
                entries[gauss_index, corner, axis_index] = entry_value
    return entries


TABLE = derivative_table()
MOMENTS = np.einsum("gad,gbe->adbe", TABLE, TABLE)


def combine(terms):
    total = None
    for constant, field in terms:
        if abs(constant) < 1e-14:
            continue
        term = field * np.float32(constant)
        total = term if total is None else total + term
    return total


def corner_sums(fields, gauss_index):
    scaled = {}

    def part(i, d, corner):
        constant = TABLE[gauss_index, corner, d]
        key = (i, d, round(abs(constant), 9))
        if key not in scaled:
            scaled[key] = fields[i][d] * np.float32(abs(constant))
        return scaled[key], constant > 0

    sums = []
    for corner in range(8):
        for i in range(3):
            pieces = sorted((part(i, d, corner) for d in range(3)), key=lambda piece: not piece[1])
            total = None
            for value, positive in pieces:
                if total is None:
                    total = value if positive else -value
                else:
                    total = total + value if positive else total - value
            sums.append(total)
    return sums


def stiffness_kernel(
    stress_ref, flags_ref, cons_ref, moduli_ref, sizes_ref, same_ref, next_ref, load_ref, v_ref, w_ref, f_ref
):
    columns, depth = sizes_ref.shape[2], sizes_ref.shape[3]
    sizes = [sizes_ref[d, 0] for d in range(3)]
    inverse = [1.0 / size for size in sizes]
    volume = sizes[0] * sizes[1] * sizes[2] * np.float32(0.125)
    bulk, shear = moduli_ref[0, 0], moduli_ref[1, 0]
    lame = bulk - np.float32(2.0 / 3.0) * shear
    slope = np.float32(3.0 / (CRITICAL_SLOPE * CRITICAL_SLOPE))

    for gauss_index in range(8):
        stress = [stress_ref[k, gauss_index, 0] for k in range(6)]
        cons = cons_ref[gauss_index, 0]
        pressure = (stress[0] + stress[1] + stress[2]) * np.float32(-1.0 / 3.0)
        volumetric = (2.0 * pressure - cons) * np.float32(1.0 / 3.0)
        normal = [slope * (stress[k] + pressure) - volumetric for k in range(3)]
        normal = normal + [(2.0 * slope) * stress[k] for k in range(3, 6)]
        trace = lame * (normal[0] + normal[1] + normal[2])
        twice = 2.0 * shear
        image = [trace + twice * normal[k] for k in range(3)]
        image = image + [shear * normal[k] for k in range(3, 6)]
        denominator = np.float32(HARDENING) * cons * cons
        for k in range(6):
            denominator = denominator + normal[k] * image[k]
        factor = flags_ref[gauss_index, 0].astype(jnp.float32) * volume / denominator
        fields = [[image[VOIGT[i][d]] * inverse[d] for d in range(3)] for i in range(3)]
        for index, value in enumerate(corner_sums(fields, gauss_index)):
            v_ref[gauss_index, index] = value
            w_ref[gauss_index, index] = value * factor
        fields = [[stress[VOIGT[i][d]] * (inverse[d] * volume) for d in range(3)] for i in range(3)]
        for index, value in enumerate(corner_sums(fields, gauss_index)):
            f_ref[index] = value if gauss_index == 0 else f_ref[index] + value

    pair_scale = {}
    for i in range(3):
        for j in range(i, 3):
            scale = volume * inverse[i] * inverse[j]
            pair_scale[i, j] = pair_scale[j, i] = (lame * scale, shear * scale)

    def entry(a, i, b, j):
        terms = [(MOMENTS[a, i, b, j], pair_scale[i, j][0])]
        if i == j:
            for d in range(3):
                weight = MOMENTS[a, d, b, d] + (MOMENTS[a, i, b, i] if d == i else 0.0)
                terms.append((weight, pair_scale[d, d][1]))
        else:
            terms.append((MOMENTS[a, j, b, i], pair_scale[i, j][1]))
        total = combine(terms)
        for gauss_index in range(8):
            term = w_ref[gauss_index, 3 * a + i] * v_ref[gauss_index, 3 * b + j]
            total = -term if total is None else total - term
        return total

    lane = lax.broadcasted_iota(jnp.int32, (columns, depth), 1)
    row = lax.broadcasted_iota(jnp.int32, (columns, depth), 0)

    def along(value):
        return jnp.where(lane == 0, 0.0, pltpu.roll(value, 1, 1))

    def diagonals(p, q, step, other, half):
        (ax, i), (bx, j) = LINES[p], LINES[q]
        a, b = 4 * ax + 2 * step, 4 * bx + 2 * other
        main = entry(a, i, b, j) + along(entry(a + 1, i, b + 1, j))
        after = along(entry(a, i, b + 1, j))
        if half:
            return [main * np.float32(0.5), after]
        return [main, after, entry(a + 1, i, b, j)]

    def store_rows(ref, index, first, second):
        moved = pltpu.roll(second, 1, 0)
        ref[index, 0:columns] = first + jnp.where(row == 0, 0.0, moved)
        ref[index, columns : columns + 1] = moved[0:1]

    index = 0
    for p, q in SAME_PAIRS:
        first = diagonals(p, q, 0, 0, p == q)
        second = diagonals(p, q, 1, 1, p == q)
        for low, high in zip(first, second):
            store_rows(same_ref, index, low, high)
            index += 1
    index = 0
    for p, q in NEXT_PAIRS:
        for value in diagonals(p, q, 0, 1, False):
            next_ref[index] = value
            index += 1
    for p, (x, d) in enumerate(LINES):
        parts = []
        for step in range(2):
            corner = 4 * x + 2 * step
            parts.append(f_ref[3 * corner + d] + along(f_ref[3 * corner + 3 + d]))
        store_rows(load_ref, p, *parts)


def contraction_kernel(
    own_ref, front_ref, side_ref, corner_ref, same_ref, next_ref, load_ref, out_ref,
    basis_ref, turned_ref, blocks_ref, rows_ref, sems,
):
    columns, plane_rows, modes = own_ref.shape
    depth = plane_rows // 3
    group_rows = 2 * plane_rows
    copies = []
    for index, (source, target) in enumerate(
        (
            (own_ref, basis_ref.at[0:columns, 0:plane_rows]),
            (front_ref, basis_ref.at[0:columns, plane_rows:group_rows]),
            (side_ref, basis_ref.at[columns : columns + 1, 0:plane_rows]),
            (corner_ref, basis_ref.at[columns : columns + 1, plane_rows:group_rows]),
        )
    ):
        copy = pltpu.make_async_copy(source, target, sems.at[index])
        copy.start()
        copies.append(copy)

    sub_index = lax.broadcasted_iota(jnp.int32, (GROUP, depth), 0)
    lane = lax.broadcasted_iota(jnp.int32, (GROUP, depth), 1)
    offset = lax.rem(lane - sub_index + depth, GROUP)
    is_main, is_after, is_before = offset == 0, offset == 1, offset == GROUP - 1
    keep = [
        jnp.where(jnp.abs(lane - sub_index - GROUP * r) <= 1, 1.0, 0.0).astype(jnp.bfloat16)
        for r in range(depth // GROUP)
    ]

    def build(row_at, column_at, main, after, before):
        if before is None:
            before = 0.0
        packed = jnp.where(is_main, main, jnp.where(is_after, after, jnp.where(is_before, before, 0.0)))
        packed = packed.astype(jnp.bfloat16)
        for r in range(depth // GROUP):
            blocks_ref[row_at + GROUP * r : row_at + GROUP * (r + 1), column_at : column_at + depth] = (
                packed * keep[r]
            )

    for p in range(6):
        for q in range(p):
            blocks_ref[p * depth : (p + 1) * depth, q * depth : (q + 1) * depth] = jnp.zeros(
                (depth, depth), jnp.bfloat16
            )
    rows_ref[modes : modes + GROUP, :] = jnp.zeros((GROUP, 2 * group_rows), jnp.bfloat16)
    for copy in copies:
        copy.wait()

    def group(y, with_next):
        turned_ref[...] = basis_ref[y].T
        index = 0
        for p, q in SAME_PAIRS:
            count = 2 if p == q else 3
            values = [same_ref[index + k, pl.ds(y, 1), :] for k in range(count)]
            build(p * depth, q * depth, *values, *([None] * (3 - count)))
            index += count
        for n in range(3):
            reach = 2 * (n + 1) * depth
            at = 2 * n * depth
            product = jnp.dot(
                turned_ref[:, 0:reach],
                blocks_ref[0:reach, at : at + 2 * depth],
                preferred_element_type=jnp.float32,
            )
            rows_ref[0:modes, at : at + 2 * depth] = product.astype(jnp.bfloat16)
        for p in range(6):
            value = load_ref[p, pl.ds(y, 1), :]
            leading = value.astype(jnp.bfloat16)
            rest = value - leading.astype(jnp.float32)
            which = lax.broadcasted_iota(jnp.int32, (GROUP, depth), 0)
            rows_ref[modes : modes + GROUP, p * depth : (p + 1) * depth] = jnp.where(
                which == 0, leading.astype(jnp.float32), jnp.where(which == 1, rest, 0.0)
            ).astype(jnp.bfloat16)
        total = jnp.dot(
            rows_ref[:, 0:group_rows], basis_ref[y], preferred_element_type=jnp.float32
        )
        if not with_next:
            return total
        index = 0
        for p, q in NEXT_PAIRS:
            values = [next_ref[index + k, pl.ds(y, 1), :] for k in range(3)]
            build(p * depth, group_rows + q * depth, *values)
            index += 3
        for n in range(3):
            at = group_rows + 2 * n * depth
            product = jnp.dot(
                turned_ref[...],
                blocks_ref[:, at : at + 2 * depth],
                preferred_element_type=jnp.float32,
            )
            rows_ref[0:modes, at : at + 2 * depth] = product.astype(jnp.bfloat16)
        return total + jnp.dot(
            rows_ref[:, group_rows:], basis_ref[y + 1], preferred_element_type=jnp.float32
        )

    out_ref[...] = jnp.zeros_like(out_ref)

    @pl.loop(0, columns)
    def _(y):
        out_ref[...] += group(y, True)

    total = out_ref[...] + group(columns, False)
    upper = total[0:modes]
    out_ref[0:modes] = upper + upper.T
    out_ref[modes:] = total[modes:]


def on_device(
    reduced_basis, gauss_stress, yield_flags, consolidation, elastic_moduli, element_sizes
):
    columns = reduced_basis.shape[1]
    depth, modes = reduced_basis.shape[3], reduced_basis.shape[4]
    plane_rows = 3 * depth
    own = reduced_basis.reshape(columns, plane_rows, modes)
    doms, subs = lax.axis_size("dom"), lax.axis_size("sub")
    front = lax.ppermute(own, "dom", [(s, s - 1) for s in range(1, doms)])
    side = lax.ppermute(own[0:1], "sub", [(s, s - 1) for s in range(1, subs)])
    corner = lax.ppermute(
        own[0:1],
        ("sub", "dom"),
        [(s * doms + t, (s - 1) * doms + t - 1) for s in range(1, subs) for t in range(1, doms)],
    )
    n_same = sum(2 if p == q else 3 for p, q in SAME_PAIRS)
    n_next = 3 * len(NEXT_PAIRS)
    same, following, loads = pl.pallas_call(
        stiffness_kernel,
        out_shape=(
            jax.ShapeDtypeStruct((n_same, 2 * columns, depth), jnp.float32),
            jax.ShapeDtypeStruct((n_next, columns, depth), jnp.float32),
            jax.ShapeDtypeStruct((6, 2 * columns, depth), jnp.float32),
        ),
        scratch_shapes=[
            pltpu.VMEM((8, 24, columns, depth), jnp.float32),
            pltpu.VMEM((8, 24, columns, depth), jnp.float32),
            pltpu.VMEM((24, columns, depth), jnp.float32),
        ],
        compiler_params=pltpu.CompilerParams(vmem_limit_bytes=24 * 2**20),
        cost_estimate=pl.CostEstimate(flops=20_000_000, bytes_accessed=1_500_000, transcendentals=0),
    )(gauss_stress, yield_flags, consolidation, elastic_moduli, element_sizes)
    any_spec = pl.BlockSpec(memory_space=pl.ANY)
    whole = pl.BlockSpec(memory_space=pltpu.VMEM)
    partial = pl.pallas_call(
        contraction_kernel,
        out_shape=jax.ShapeDtypeStruct((modes + GROUP, modes), jnp.float32),
        in_specs=[any_spec] * 4 + [whole] * 3,
        out_specs=whole,
        scratch_shapes=[
            pltpu.VMEM((columns + 1, 2 * plane_rows, modes), jnp.bfloat16),
            pltpu.VMEM((modes, 2 * plane_rows), jnp.bfloat16),
            pltpu.VMEM((2 * plane_rows, 4 * plane_rows), jnp.bfloat16),
            pltpu.VMEM((modes + GROUP, 4 * plane_rows), jnp.bfloat16),
            pltpu.SemaphoreType.DMA((4,)),
        ],
        compiler_params=pltpu.CompilerParams(vmem_limit_bytes=24 * 2**20),
        cost_estimate=pl.CostEstimate(flops=2_000_000_000, bytes_accessed=3_000_000, transcendentals=0),
    )(own, front, side, corner, same, following, loads)

    total = reduce_all(partial)
    return (total[0:modes], total[modes] + total[modes + 1])


def reduce_all(partial):
    subs, doms = lax.axis_size("sub"), lax.axis_size("dom")
    both = ("sub", "dom")
    count = subs * doms
    rows, modes = partial.shape
    short = -(-rows // count) * count
    padded = jnp.pad(partial, ((0, short - rows), (0, 0))).reshape(count, short // count, modes)
    parts = lax.all_to_all(padded, both, 0, 0)
    mine = jnp.sum(parts, axis=0, keepdims=True)
    gathered = lax.all_to_all(jnp.broadcast_to(mine, padded.shape), both, 0, 0)
    return gathered.reshape(short, modes)


def solution(mesh):
    return jax.shard_map(
        on_device,
        mesh=mesh,
        in_specs=(
            P("dom", "sub", None, None, None),
            P(None, None, "dom", "sub", None),
            P(None, "dom", "sub", None),
            P(None, "dom", "sub", None),
            P(None, "dom", "sub", None),
            P(None, "dom", "sub", None),
        ),
        out_specs=(P(), P()),
        check_vma=False,
    )
```

profile of v0, /device:TPU:0, one launch (start us, length us, event | category | flops | bytes accessed | tf_op | source)
XLA Modules:
  0.0 48.7 jit_solution(6535925660015255073)
XLA Ops:
  0.6 0.0 copy-start
  0.6 1.4 %collective-permute-start = (bf16[8,384,128]{2,1,0:T(8,128)(2,1)}, bf16[8,384,128]{2,1,0:T(8,128)(2,1)S(1)}, u32[]{:S(2)}, u32[]{:S(2)}) collective-permute-start(bf16[8,384,128]{2,1,0:T(8,128)(2,1)} %bitcast.4), channel_id=1, source_target_pairs={{1,0},{2,1},{3,2},{4,3},{5,4},{6,5},{7,6},{9,8},{10,9},{11,10},{12... | collective-permute-start | bytes 2359304 | tf_op jit(solution)/shard_map/ppermute | solution.py:291
  2.1 0.9 %slice.16 = bf16[1,1,3,128,128]{4,3,2,1,0:T(8,128)(2,1)S(1)} slice(bf16[1,8,3,128,128]{4,3,2,1,0:T(8,128)(2,1)} %param.6), slice={[0:1], [0:1], [0:3], [0:128], [0:128]} | slice | bytes 196608 | tf_op jit(solution)/shard_map/slice | solution.py:292
  3.0 1.3 %collective-permute-start.2 = (bf16[1,384,128]{2,1,0:T(8,128)(2,1)S(1)}, bf16[1,384,128]{2,1,0:T(8,128)(2,1)S(1)}, u32[]{:S(2)}, u32[]{:S(2)}) collective-permute-start(bf16[1,384,128]{2,1,0:T(8,128)(2,1)S(1)} %bitcast.6), channel_id=1, source_target_pairs={{9,0},{10,1},{11,2},{12,3},{13,4},{14,5},{15,6},{17,8},{18,9},{19,... | collective-permute-start | bytes 294920 | tf_op jit(solution)/shard_map/ppermute | solution.py:293
  4.3 1.3 %collective-permute-start.1 = (bf16[1,384,128]{2,1,0:T(8,128)(2,1)S(1)}, bf16[1,384,128]{2,1,0:T(8,128)(2,1)S(1)}, u32[]{:S(2)}, u32[]{:S(2)}) collective-permute-start(bf16[1,384,128]{2,1,0:T(8,128)(2,1)S(1)} %bitcast.7), channel_id=1, source_target_pairs={{8,0},{16,8},{24,16},{9,1},{17,9},{25,17},{10,2},{18,10},{26,18},{... | collective-permute-start | bytes 294920 | tf_op jit(solution)/shard_map/ppermute | solution.py:292
  5.6 0.0 copy-done
  5.6 0.0 copy-start.1
  5.6 0.7 %copy-done.1 = s32[8,1,8,128]{3,2,1,0:T(8,128)S(1)} copy-done((s32[8,1,8,128]{3,2,1,0:T(8,128)S(1)}, s32[8,1,8,128]{3,2,1,0:T(8,128)}, u32[]{:S(2)}) %copy-start.1) | copy-done | bytes 32792
  6.3 0.0 copy-start.2
  6.3 0.8 %copy-done.2 = f32[8,1,8,128]{3,2,1,0:T(8,128)S(1)} copy-done((f32[8,1,8,128]{3,2,1,0:T(8,128)S(1)}, f32[8,1,8,128]{3,2,1,0:T(8,128)}, u32[]{:S(2)}) %copy-start.2) | copy-done | bytes 32792
  7.1 0.0 copy-start.3
  7.1 0.7 %copy-done.3 = f32[3,1,8,128]{3,2,1,0:T(8,128)S(1)} copy-done((f32[3,1,8,128]{3,2,1,0:T(8,128)S(1)}, f32[3,1,8,128]{3,2,1,0:T(8,128)}, u32[]{:S(2)}) %copy-start.3) | copy-done | bytes 12312
  7.8 0.0 copy-start.5
  7.8 0.7 %copy-done.5 = f32[2,1,8,128]{3,2,1,0:T(8,128)S(1)} copy-done((f32[2,1,8,128]{3,2,1,0:T(8,128)S(1)}, f32[2,1,8,128]{3,2,1,0:T(8,128)}, u32[]{:S(2)}) %copy-start.5) | copy-done | bytes 8216
  8.5 1.1 %shard_map.77 = (f32[57,16,128]{2,1,0:T(8,128)S(1)}, f32[108,8,128]{2,1,0:T(8,128)S(1)}, f32[6,16,128]{2,1,0:T(8,128)S(1)}) custom-call(f32[6,8,1,8,128]{4,3,2,1,0:T(8,128)S(1)} %copy-done, s32[8,1,8,128]{3,2,1,0:T(8,128)S(1)} %copy-done.1, f32[8,1,8,128]{3,2,1,0:T(8,128)S(1)} %copy-done.2, f32[2,1,8,128]{3,2,1,0:T(8,128)S(1)} %copy-done.5, ...), custom_call_target="tpu_custom_call" | custom-call | flops 20000000 | bytes 1500000 | tf_op jit(solution)/shard_map/pallas_call | solution.py:300
  9.6 1.4 %collective-permute-done.2.corner_ref = bf16[1,384,128]{2,1,0:T(8,128)(2,1)S(1)} collective-permute-done((bf16[1,384,128]{2,1,0:T(8,128)(2,1)S(1)}, bf16[1,384,128]{2,1,0:T(8,128)(2,1)S(1)}, u32[]{:S(2)}, u32[]{:S(2)}) %collective-permute-start.2) | collective-permute-done | bytes 98336 | tf_op jit(solution)/shard_map/ppermute | solution.py:293
  11.0 1.0 %collective-permute-done.1.side_ref = bf16[1,384,128]{2,1,0:T(8,128)(2,1)S(1)} collective-permute-done((bf16[1,384,128]{2,1,0:T(8,128)(2,1)S(1)}, bf16[1,384,128]{2,1,0:T(8,128)(2,1)S(1)}, u32[]{:S(2)}, u32[]{:S(2)}) %collective-permute-start.1) | collective-permute-done | bytes 98336 | tf_op jit(solution)/shard_map/ppermute | solution.py:292
  12.1 0.0 collective-permute-done.front_ref
  12.1 0.0 copy-start.4
  12.1 1.1 %copy-done.4 = bf16[1,8,3,128,128]{4,3,2,1,0:T(8,128)(2,1)S(1)} copy-done((bf16[1,8,3,128,128]{4,3,2,1,0:T(8,128)(2,1)S(1)}, bf16[1,8,3,128,128]{4,3,2,1,0:T(8,128)(2,1)}, u32[]{:S(2)}) %copy-start.4) | copy-done | bytes 786456
  13.2 7.3 %shard_map.78 = f32[144,128]{1,0:T(8,128)S(1)} custom-call(bf16[8,384,128]{2,1,0:T(8,128)(2,1)S(1)} %bitcast.5, bf16[8,384,128]{2,1,0:T(8,128)(2,1)S(1)} %collective-permute-done.front_ref, bf16[1,384,128]{2,1,0:T(8,128)(2,1)S(1)} %collective-permute-done.1.side_ref, bf16[1,384,128]{2,1,0:T(8,128)(2,1)S(1)} %collective-permute-done.2.corner_ref, ...), custom_call_target="tpu_custom_call" | custom-call | flops 2000000000 | bytes 3000000 | tf_op jit(solution)/shard_map/pallas_call | solution.py:317
  20.5 17.1 %all_to_all.10 = f32[32,5,128]{2,1,0:T(8,128)S(1)} all-to-all(f32[32,5,128]{2,1,0:T(8,128)S(1)} %reshape.17), channel_id=1, replica_groups=mesh['sub'=4,'dom'=8] {'sub','dom'}, dimensions={0} | all-to-all | bytes 163840 | tf_op jit(solution)/shard_map/all_to_all | solution.py:344
  37.7 9.9 %all_to_all.11 = f32[32,5,128]{2,1,0:T(8,128)S(1)} all-to-all(f32[32,5,128]{2,1,0:T(8,128)S(1)} %broadcast_in_dim.2), channel_id=1, replica_groups=mesh['sub'=4,'dom'=8] {'sub','dom'}, dimensions={0} | all-to-all | bytes 163840 | tf_op jit(solution)/shard_map/all_to_all | solution.py:346
  47.6 0.5 %fusion = f32[128]{0:T(128)} fusion(f32[160,128]{1,0:T(8,128)S(1)} %reshape.18), kind=kLoop, calls=%fused_computation.1 | loop fusion | flops 128 | bytes 1536 | tf_op jit(solution)/shard_map/add | solution.py:334
  48.1 0.6 %slice.21 = f32[128,128]{1,0:T(8,128)} slice(f32[160,128]{1,0:T(8,128)S(1)} %reshape.18), slice={[0:128], [0:128]} | slice | bytes 131072 | tf_op jit(solution)/shard_map/slice | solution.py:334
  (5 shorter events, 0.1 us)
Async XLA Ops:
  0.6 4.9 %copy-start = (f32[6,8,1,8,128]{4,3,2,1,0:T(8,128)S(1)}, f32[6,8,1,8,128]{4,3,2,1,0:T(8,128)}, u32[]{:S(2)}) copy-start(f32[6,8,1,8,128]{4,3,2,1,0:T(8,128)} %stress_ref.1) | copy-start | bytes 589828
  0.6 11.4 %collective-permute-start = (bf16[8,384,128]{2,1,0:T(8,128)(2,1)}, bf16[8,384,128]{2,1,0:T(8,128)(2,1)S(1)}, u32[]{:S(2)}, u32[]{:S(2)}) collective-permute-start(bf16[8,384,128]{2,1,0:T(8,128)(2,1)} %bitcast.4), channel_id=1, source_target_pairs={{1,0},{2,1},{3,2},{4,3},{5,4},{6,5},{7,6},{9,8},{10,9},{11,10},{12... | collective-permute-start | bytes 2359304 | tf_op jit(solution)/shard_map/ppermute | solution.py:291
  3.0 8.1 %collective-permute-start.2 = (bf16[1,384,128]{2,1,0:T(8,128)(2,1)S(1)}, bf16[1,384,128]{2,1,0:T(8,128)(2,1)S(1)}, u32[]{:S(2)}, u32[]{:S(2)}) collective-permute-start(bf16[1,384,128]{2,1,0:T(8,128)(2,1)S(1)} %bitcast.6), channel_id=1, source_target_pairs={{9,0},{10,1},{11,2},{12,3},{13,4},{14,5},{15,6},{17,8},{18,9},{19,... | collective-permute-start | bytes 294920 | tf_op jit(solution)/shard_map/ppermute | solution.py:293
  4.3 7.8 %collective-permute-start.1 = (bf16[1,384,128]{2,1,0:T(8,128)(2,1)S(1)}, bf16[1,384,128]{2,1,0:T(8,128)(2,1)S(1)}, u32[]{:S(2)}, u32[]{:S(2)}) collective-permute-start(bf16[1,384,128]{2,1,0:T(8,128)(2,1)S(1)} %bitcast.7), channel_id=1, source_target_pairs={{8,0},{16,8},{24,16},{9,1},{17,9},{25,17},{10,2},{18,10},{26,18},{... | collective-permute-start | bytes 294920 | tf_op jit(solution)/shard_map/ppermute | solution.py:292
  5.6 0.8 %copy-start.1 = (s32[8,1,8,128]{3,2,1,0:T(8,128)S(1)}, s32[8,1,8,128]{3,2,1,0:T(8,128)}, u32[]{:S(2)}) copy-start(s32[8,1,8,128]{3,2,1,0:T(8,128)} %flags_ref.1) | copy-start | bytes 98308
  6.3 0.8 %copy-start.2 = (f32[8,1,8,128]{3,2,1,0:T(8,128)S(1)}, f32[8,1,8,128]{3,2,1,0:T(8,128)}, u32[]{:S(2)}) copy-start(f32[8,1,8,128]{3,2,1,0:T(8,128)} %cons_ref.1) | copy-start | bytes 98308
  7.1 0.7 %copy-start.3 = (f32[3,1,8,128]{3,2,1,0:T(8,128)S(1)}, f32[3,1,8,128]{3,2,1,0:T(8,128)}, u32[]{:S(2)}) copy-start(f32[3,1,8,128]{3,2,1,0:T(8,128)} %sizes_ref.1) | copy-start | bytes 36868
  7.8 0.7 %copy-start.5 = (f32[2,1,8,128]{3,2,1,0:T(8,128)S(1)}, f32[2,1,8,128]{3,2,1,0:T(8,128)}, u32[]{:S(2)}) copy-start(f32[2,1,8,128]{3,2,1,0:T(8,128)} %moduli_ref.1) | copy-start | bytes 24580
  12.1 1.1 %copy-start.4 = (bf16[1,8,3,128,128]{4,3,2,1,0:T(8,128)(2,1)S(1)}, bf16[1,8,3,128,128]{4,3,2,1,0:T(8,128)(2,1)}, u32[]{:S(2)}) copy-start(bf16[1,8,3,128,128]{4,3,2,1,0:T(8,128)(2,1)} %param.6) | copy-start | bytes 2359300
where the time goes:
time: 49.2 us; the launch traced here: 48.7 us
  blocking collectives  27 us (55%)
  Pallas kernels  8.36 us (17%)
  local copies, waits for them, and re-layouts  5.64 us (11%)
  starting transfers between devices  4 us (8%)
  waiting for transfers between devices  2.46 us (5%)
  between operations  0.72 us (1%)
  other arithmetic  0.55 us (1%)
    all_to_all x1, blocking collectives, reduce_all(): parts = lax.all_to_all(padded, both, 0, 0)  17.1 us
    all_to_all x1, blocking collectives, reduce_all(): gathered = lax.all_to_all(jnp.broadcast_to(mine, padded.shape), both, 0, 0)  9.88 us
    pallas_call x1, Pallas kernels, on_device(): pl.pallas_call(contraction_kernel, out_shape=jax.ShapeDtypeStruct((modes...  7.25 us
    unnamed x12, local copies, waits for them, and re-layouts  4.05 us
    ppermute x1, waiting for transfers between devices, on_device(): lax.ppermute(own[0:1], ('sub', 'dom'), [(s * doms + t, (s - 1) * doms + t...  1.44 us
    ppermute x1, starting transfers between devices, on_device(): front = lax.ppermute(own, 'dom', [(s, s - 1) for s in range(1, doms)])  1.42 us
    ppermute x1, starting transfers between devices, on_device(): side = lax.ppermute(own[0:1], 'sub', [(s, s - 1) for s in range(1, subs)])  1.29 us
    ppermute x1, starting transfers between devices, on_device(): lax.ppermute(own[0:1], ('sub', 'dom'), [(s * doms + t, (s - 1) * doms + t...  1.28 us
  transfers between devices with their start and end apart: 3, of which 2 were waited for; matrix products, arithmetic and copies ran while one was open for 2% of the time, Pallas kernels for 2%

commit v1 on v0

v1 whole, which is shorter than its diff:
```python
import functools

import jax
import jax.numpy as jnp
import numpy as np
from jax import lax
from jax.experimental import pallas as pl
from jax.experimental.pallas import tpu as pltpu
from jax.sharding import PartitionSpec as P

GAUSS_POINT = 0.5773502691896258
CRITICAL_SLOPE = 1.2
HARDENING = 0.5
VOIGT = ((0, 3, 5), (3, 1, 4), (5, 4, 2))
LINES = [(x, d) for x in range(2) for d in range(3)]
SLOTS = [
    [(0, 0), (0, 1), (0, 2), (0, 3)],
    [(0, 4), (0, 5), (1, 4), (1, 5)],
    [(1, 0), (1, 1), (1, 2), (1, 3)],
]
TILE = 16
PARTS = 4


def corner_bits(corner):
    return (corner // 4, corner // 2 % 2, corner % 2)


def derivative_table():
    entries = np.zeros((8, 8, 3))
    for gauss_index in range(8):
        gauss_coords = [GAUSS_POINT * (2 * bit_value - 1) for bit_value in corner_bits(gauss_index)]
        for corner in range(8):
            corner_signs = [2 * bit_value - 1 for bit_value in corner_bits(corner)]
            for axis_index in range(3):
                entry_value = float(corner_signs[axis_index])
                for other_axis in range(3):
                    if other_axis != axis_index:
                        entry_value = (
                            entry_value
                            * (1.0 + corner_signs[other_axis] * gauss_coords[other_axis])
                            / 2.0
                        )
                entries[gauss_index, corner, axis_index] = entry_value
    return entries


TABLE = derivative_table()
MOMENTS = np.einsum("gad,gbe->adbe", TABLE, TABLE)


def combine(terms):
    total = None
    for constant, field in terms:
        if abs(constant) < 1e-14:
            continue
        term = field * np.float32(constant)
        total = term if total is None else total + term
    return total


def corner_sums(fields, gauss_index):
    scaled = {}

    def part(i, d, corner):
        constant = TABLE[gauss_index, corner, d]
        key = (i, d, round(abs(constant), 9))
        if key not in scaled:
            scaled[key] = fields[i][d] * np.float32(abs(constant))
        return scaled[key], constant > 0

    sums = []
    for corner in range(8):
        for i in range(3):
            pieces = sorted((part(i, d, corner) for d in range(3)), key=lambda piece: not piece[1])
            total = None
            for value, positive in pieces:
                if total is None:
                    total = value if positive else -value
                else:
                    total = total + value if positive else total - value
            sums.append(total)
    return sums


def stiffness_kernel(
    state_ref, blocks_ref,
    v_ref, w_ref, f_ref, field_ref, load_ref, edge_ref,
):
    columns, depth = state_ref.shape[1:]
    flags_at, cons_at, moduli_at, sizes_at = 48, 56, 64, 66
    sizes = [state_ref[sizes_at + d] for d in range(3)]
    inverse = [1.0 / size for size in sizes]
    volume = sizes[0] * sizes[1] * sizes[2] * np.float32(0.125)
    bulk, shear = state_ref[moduli_at], state_ref[moduli_at + 1]
    lame = bulk - np.float32(2.0 / 3.0) * shear
    slope = np.float32(3.0 / (CRITICAL_SLOPE * CRITICAL_SLOPE))

    for gauss_index in range(8):
        stress = [state_ref[8 * k + gauss_index] for k in range(6)]
        cons = state_ref[cons_at + gauss_index]
        pressure = (stress[0] + stress[1] + stress[2]) * np.float32(-1.0 / 3.0)
        volumetric = (2.0 * pressure - cons) * np.float32(1.0 / 3.0)
        normal = [slope * (stress[k] + pressure) - volumetric for k in range(3)]
        normal = normal + [(2.0 * slope) * stress[k] for k in range(3, 6)]
        trace = lame * (normal[0] + normal[1] + normal[2])
        twice = 2.0 * shear
        image = [trace + twice * normal[k] for k in range(3)]
        image = image + [shear * normal[k] for k in range(3, 6)]
        denominator = np.float32(HARDENING) * cons * cons
        for k in range(6):
            denominator = denominator + normal[k] * image[k]
        factor = state_ref[flags_at + gauss_index] * volume / denominator
        fields = [[image[VOIGT[i][d]] * inverse[d] for d in range(3)] for i in range(3)]
        for index, value in enumerate(corner_sums(fields, gauss_index)):
            v_ref[gauss_index, index] = value
            w_ref[gauss_index, index] = value * factor
        fields = [[stress[VOIGT[i][d]] * (inverse[d] * volume) for d in range(3)] for i in range(3)]
        for index, value in enumerate(corner_sums(fields, gauss_index)):
            f_ref[index] = value if gauss_index == 0 else f_ref[index] + value

    pair_scale = {}
    for i in range(3):
        for j in range(i, 3):
            scale = volume * inverse[i] * inverse[j]
            pair_scale[i, j] = pair_scale[j, i] = (lame * scale, shear * scale)

    def entry(a, i, b, j):
        terms = [(MOMENTS[a, i, b, j], pair_scale[i, j][0])]
        if i == j:
            for d in range(3):
                weight = MOMENTS[a, d, b, d] + (MOMENTS[a, i, b, i] if d == i else 0.0)
                terms.append((weight, pair_scale[d, d][1]))
        else:
            terms.append((MOMENTS[a, j, b, i], pair_scale[i, j][1]))
        total = combine(terms)
        for gauss_index in range(8):
            term = w_ref[gauss_index, 3 * a + i] * v_ref[gauss_index, 3 * b + j]
            total = -term if total is None else total - term
        return total

    lane = lax.broadcasted_iota(jnp.int32, (columns, depth), 1)
    row = lax.broadcasted_iota(jnp.int32, (columns, depth), 0)
    zero = jnp.zeros((columns, depth), jnp.float32)
    span = depth // PARTS

    def along(value):
        return jnp.where(lane == 0, 0.0, pltpu.roll(value, 1, 1))

    def diagonals(p, q, step, other):
        (ax, i), (bx, j) = LINES[p], LINES[q]
        a, b = 4 * ax + 2 * step, 4 * bx + 2 * other
        main = entry(a, i, b, j) + along(entry(a + 1, i, b + 1, j))
        after = along(entry(a, i, b + 1, j))
        if step == other and p == q:
            return [main * np.float32(0.5), after, zero]
        return [main, after, jnp.where(lane == depth - 1, 0.0, entry(a + 1, i, b, j))]

    def all_rows(low, high):
        return low + jnp.where(row == 0, 0.0, pltpu.roll(high, 1, 0)), high

    part_of = lane // span

    def regrouped(values):
        moved = [values[0]] + [pltpu.roll(values[q], q * span, 1) for q in range(1, PARTS)]
        parts = []
        for part in range(PARTS):
            merged = moved[-part % PARTS]
            for at in range(1, PARTS):
                merged = jnp.where(part_of == at, moved[(at - part) % PARTS], merged)
            parts.append(pltpu.roll(merged, depth - part * span, 1) if part else merged)
        return parts

    def store(ref, at, kinds):
        for k, pairs in enumerate(kinds):
            firsts = regrouped([zero if pair is None else pair[0] for pair in pairs])
            for part in range(PARTS):
                ref[at + k, part, 0:columns] = firsts[part]
        if all(pair is None or pair[1] is None for pairs in kinds for pair in pairs):
            for k in range(len(kinds)):
                for part in range(PARTS):
                    ref[at + k, part, columns : columns + 1] = zero[0:1]
            return
        lasts = []
        for field in range(PARTS):
            merged = zero
            for k, pairs in enumerate(kinds):
                pair = pairs[field]
                if pair is not None and pair[1] is not None:
                    merged = jnp.where(row == k, pltpu.roll(pair[1], 1 + k, 0), merged)
            lasts.append(merged)
        lasts = regrouped(lasts)
        for k in range(len(kinds)):
            for part in range(PARTS):
                ref[at + k, part, columns : columns + 1] = lasts[part][k : k + 1]

    empty = set()
    for p in range(6):
        for g, slots in enumerate(SLOTS):
            kinds = [[], [], []]
            for following, q in slots:
                if following:
                    values = [(value, None) for value in diagonals(p, q, 0, 1)]
                elif q >= p:
                    low, high = diagonals(p, q, 0, 0), diagonals(p, q, 1, 1)
                    values = [all_rows(low[k], high[k]) for k in range(3)]
                else:
                    values = [None] * 3
                for k in range(3):
                    kinds[k].append(values[k])
            if all(value is None for value in kinds[0]):
                empty.add((p, g))
                continue
            store(field_ref, (p * 3 + g) * 3, kinds)
    loads = []
    for x, d in LINES:
        parts = [f_ref[12 * x + 6 * s + d] + along(f_ref[12 * x + 6 * s + 3 + d]) for s in range(2)]
        loads.append(all_rows(*parts))
    store(load_ref, 0, [loads[0:4], loads[4:6] + [None, None]])

    place = lax.rem(lax.broadcasted_iota(jnp.int32, (span, depth), 1), span)
    offset = (place - lax.broadcasted_iota(jnp.int32, (span, depth), 0)).astype(jnp.bfloat16)
    is_main, is_after, is_before = offset == 0, offset == 1, offset == -1
    begins = place[0:1] == 0
    ends = place[0:1] == span - 1
    tile_row = lax.broadcasted_iota(jnp.int32, (TILE, depth), 0)
    edge_at = 6 * span
    load_at = edge_at + TILE
    edge_ref[...] = jnp.zeros_like(edge_ref)

    @pl.loop(0, columns + 1, unroll=True)
    def _(y):
        for part in range(PARTS):
            at = y * PARTS + part
            for g in range(len(SLOTS)):
                lanes = slice(g * depth, (g + 1) * depth)
                for p in range(6):
                    rows = slice(p * span, (p + 1) * span)
                    if (p, g) in empty:
                        blocks_ref[at, rows, lanes] = jnp.zeros((span, depth), jnp.bfloat16)
                        continue
                    main, after, before = [
                        field_ref[(p * 3 + g) * 3 + k, part, pl.ds(y, 1), :] for k in range(3)
                    ]
                    main16, after16, before16 = [
                        jnp.broadcast_to(value, (TILE, depth)).astype(jnp.bfloat16)
                        for value in (main, after, before)
                    ]
                    for first in range(0, span, TILE):
                        here = slice(first, first + TILE)
                        blocks_ref[at, p * span + first : p * span + first + TILE, lanes] = jnp.where(
                            is_main[here],
                            main16,
                            jnp.where(
                                is_after[here],
                                after16,
                                jnp.where(is_before[here], before16, jnp.bfloat16(0)),
                            ),
                        )
                    edge_ref[p : p + 1, lanes] = jnp.where(begins, after, 0.0)
                    edge_ref[TILE // 2 + p : TILE // 2 + p + 1, lanes] = jnp.where(ends, before, 0.0)
                if g < 2:
                    value = load_ref[g, part, pl.ds(y, 1), :]
                    leading = value.astype(jnp.bfloat16).astype(jnp.float32)
                    blocks_ref[at, load_at : load_at + TILE, lanes] = jnp.where(
                        tile_row == 0, leading, jnp.where(tile_row == 1, value - leading, 0.0)
                    ).astype(jnp.bfloat16)
                else:
                    blocks_ref[at, load_at : load_at + TILE, lanes] = jnp.zeros((TILE, depth), jnp.bfloat16)
            blocks_ref[at, edge_at:load_at] = edge_ref[...].astype(jnp.bfloat16)


def contraction_kernel(
    own_ref, front_ref, side_ref, corner_ref, blocks_ref, mine_ref, other_ref,
    gather_ref, carry_ref, sum_ref, packed_ref,
):
    columns, plane_rows, modes = own_ref.shape
    depth = plane_rows // 3
    span = depth // PARTS
    carry_ref[...] = jnp.zeros_like(carry_ref)
    gather_ref[...] = jnp.zeros_like(gather_ref)
    sum_ref[...] = jnp.zeros_like(sum_ref)
    own_lanes = lax.broadcasted_iota(jnp.int32, (modes, depth), 1) < 2 * span
    nothing = jnp.zeros((8, modes), jnp.float32)

    def group(y, planes):
        def rows(p, first, count):
            ref, at = planes[p // 3]
            start = (p % 3) * depth + first
            return ref[at, start : start + count]

        for border in range(1, PARTS):
            for p in range(6):
                around = rows(p, border * span - TILE, 2 * TILE).astype(jnp.float32)
                at = ((border - 1) * 8 + p) * TILE
                gather_ref[at : at + TILE] = around[TILE // 2 : TILE + TILE // 2]
        total = sum_ref[...]
        for part in range(PARTS):
            before, after = nothing, nothing
            if part > 0:
                before = gather_ref[pl.ds((part - 1) * 8 * TILE + TILE // 2 - 1, 8, TILE)]
            if part < PARTS - 1:
                after = gather_ref[pl.ds(part * 8 * TILE + TILE // 2, 8, TILE)]
            edges = jnp.concatenate([before, after], 0).astype(jnp.bfloat16)
            here = jnp.concatenate([rows(p, part * span, span) for p in range(6)], 0)
            turned = jnp.concatenate([here, edges], 0).T
            at = y * PARTS + part
            product = jnp.dot(
                turned, blocks_ref[at, 0 : 6 * span + TILE], preferred_element_type=jnp.float32
            )
            first = product[:, 0:depth] + carry_ref[part, 0]
            middle = product[:, depth : 2 * depth]
            second = jnp.where(own_lanes, middle + carry_ref[part, 1], 0.0)
            carry_ref[part, 0] = product[:, 2 * depth :]
            carry_ref[part, 1] = pltpu.roll(middle, 2 * span, 1)
            factors = jnp.concatenate([first, second], 1).astype(jnp.bfloat16)
            factors = jnp.concatenate(
                [factors, blocks_ref[at, 6 * span + TILE : 6 * span + 2 * TILE, 0 : 2 * depth]], 0
            )
            total = total + jnp.dot(
                factors[:, 0 : 6 * span], here, preferred_element_type=jnp.float32
            )
        sum_ref[...] = total

    @pl.loop(0, columns, unroll=True)
    def _(y):
        group(y, ((own_ref, y), (front_ref, y)))

    group(columns, ((side_ref, 0), (corner_ref, 0)))
    total = sum_ref[...]
    upper = total[0:modes]
    tangent = upper + upper.T
    half, quarter, share = modes // 2, modes // 4, mine_ref.shape[0]
    packed_ref[0:half] = tangent[0:half]
    packed_ref[half : half + quarter] = jnp.concatenate(
        [tangent[half : half + quarter, half:], tangent[half + quarter :, half:]], 1
    )
    packed_ref[half + quarter :] = jnp.zeros_like(packed_ref[half + quarter :])
    packed_ref[half + quarter : half + quarter + 1] = (
        total[modes : modes + 1] + total[modes + 1 : modes + 2]
    )
    core = lax.rem(lax.axis_index("dom"), 2)
    mine_ref[...] = packed_ref[pl.ds(pl.multiple_of(core * share, 8), share)]
    other_ref[...] = packed_ref[pl.ds(pl.multiple_of((1 - core) * share, 8), share)]


def unpack_kernel(mine_ref, other_ref, tangent_ref, residual_ref, packed_ref):
    share = mine_ref.shape[0]
    modes = tangent_ref.shape[0]
    half, quarter = modes // 2, modes // 4
    core = lax.rem(lax.axis_index("dom"), 2)
    packed_ref[pl.ds(pl.multiple_of(core * share, 8), share)] = mine_ref[...]
    packed_ref[pl.ds(pl.multiple_of((1 - core) * share, 8), share)] = other_ref[...]
    tangent_ref[0:half] = packed_ref[0:half]
    low = packed_ref[half : half + quarter]
    corner = packed_ref[0:half, half:].T
    tangent_ref[half:, 0:half] = corner
    tangent_ref[half : half + quarter, half:] = low[:, 0:half]
    tangent_ref[half + quarter :, half:] = low[:, half:]
    residual_ref[...] = packed_ref[half + quarter : half + quarter + 1]


def on_device(
    reduced_basis, gauss_stress, yield_flags, consolidation, elastic_moduli, element_sizes
):
    columns = reduced_basis.shape[1]
    depth, modes = reduced_basis.shape[3], reduced_basis.shape[4]
    plane_rows = 3 * depth
    own = reduced_basis.reshape(columns, plane_rows, modes)
    doms, subs = lax.axis_size("dom"), lax.axis_size("sub")
    front = lax.ppermute(own, "dom", [(s, s - 1) for s in range(1, doms)])
    first = own[0:1]
    side = lax.ppermute(first, "sub", [(s, s - 1) for s in range(1, subs)])
    corner = lax.ppermute(
        first,
        ("sub", "dom"),
        [(s * doms + t, (s - 1) * doms + t - 1) for s in range(1, subs) for t in range(1, doms)],
    )
    shape = (columns, depth)
    block_rows = 6 * (depth // PARTS) + 2 * TILE
    blocks_shape = ((columns + 1) * PARTS, block_rows, len(SLOTS) * depth)
    fields = [
        value.astype(jnp.float32).reshape((-1,) + shape)
        for value in (gauss_stress, yield_flags, consolidation, elastic_moduli, element_sizes)
    ]
    count = sum(value.shape[0] for value in fields)
    state, at = 0.0, 0
    for value in fields:
        end = at + value.shape[0]
        state = state + jnp.pad(value, ((at, count - end), (0, 0), (0, 0)))
        at = end
    whole = pl.BlockSpec(memory_space=pltpu.VMEM)
    blocks = pl.pallas_call(
        stiffness_kernel,
        out_shape=jax.ShapeDtypeStruct(blocks_shape, jnp.bfloat16),
        in_specs=[whole],
        out_specs=whole,
        scratch_shapes=[
            pltpu.VMEM((8, 24) + shape, jnp.float32),
            pltpu.VMEM((8, 24) + shape, jnp.float32),
            pltpu.VMEM((24,) + shape, jnp.float32),
            pltpu.VMEM((9 * 6, PARTS, 2 * columns, depth), jnp.float32),
            pltpu.VMEM((2, PARTS, 2 * columns, depth), jnp.float32),
            pltpu.VMEM((TILE, len(SLOTS) * depth), jnp.float32),
        ],
        compiler_params=pltpu.CompilerParams(vmem_limit_bytes=24 * 2**20),
        cost_estimate=pl.CostEstimate(flops=20_000_000, bytes_accessed=8_000_000, transcendentals=0),
    )(state)
    packed_rows = -(-(modes // 2 + modes // 4 + 1) // 16) * 16
    share = jax.ShapeDtypeStruct((packed_rows // 2, modes), jnp.float32)
    mine, other = pl.pallas_call(
        contraction_kernel,
        out_shape=(share, share),
        in_specs=[whole] * 5,
        out_specs=(whole, whole),
        scratch_shapes=[
            pltpu.VMEM(((PARTS - 1) * 8 * TILE + TILE, modes), jnp.float32),
            pltpu.VMEM((PARTS, 2, modes, depth), jnp.float32),
            pltpu.VMEM((modes + TILE, modes), jnp.float32),
            pltpu.VMEM((packed_rows, modes), jnp.float32),
        ],
        compiler_params=pltpu.CompilerParams(vmem_limit_bytes=24 * 2**20),
        cost_estimate=pl.CostEstimate(flops=2_000_000_000, bytes_accessed=8_000_000, transcendentals=0),
    )(own, front, side, corner, blocks)

    mine = mine + exchanged(other, "dom", 1)
    for axis, first in (("dom", 2), ("sub", 1)):
        for stride, radix in stages(first, lax.axis_size(axis)):
            received = [exchanged(mine, axis, stride * k) for k in range(radix - 1, 0, -1)]
            mine = sum(received, mine)
    other = exchanged(mine, "dom", 1)
    tangent, residual = pl.pallas_call(
        unpack_kernel,
        out_shape=(
            jax.ShapeDtypeStruct((modes, modes), jnp.float32),
            jax.ShapeDtypeStruct((1, modes), jnp.float32),
        ),
        in_specs=[whole] * 2,
        out_specs=(whole, whole),
        scratch_shapes=[pltpu.VMEM((packed_rows, modes), jnp.float32)],
        compiler_params=pltpu.CompilerParams(vmem_limit_bytes=8 * 2**20),
    )(mine, other)
    return (tangent, residual.reshape(modes))


def exchanged(value, axis, distance):
    return lax.ppermute(value, axis, [(s, s ^ distance) for s in range(lax.axis_size(axis))])


def stages(stride, size):
    found = []
    while stride < size:
        radix = min(4, size // stride)
        found.append((stride, radix))
        stride *= radix
    return found


def solution(mesh):
    return jax.shard_map(
        on_device,
        mesh=mesh,
        in_specs=(
            P("dom", "sub", None, None, None),
            P(None, None, "dom", "sub", None),
            P(None, "dom", "sub", None),
            P(None, "dom", "sub", None),
            P(None, "dom", "sub", None),
            P(None, "dom", "sub", None),
        ),
        out_specs=(P(), P()),
        check_vma=False,
    )
```

time: 49.2 us -> 40.6 us (0.83)
  blocking collectives: 27 us -> 0 us
  starting transfers between devices: 4 us -> 18.1 us
  waiting for transfers between devices: 2.46 us -> 11.4 us
  local copies, waits for them, and re-layouts: 5.64 us -> 0.9 us
  other arithmetic: 0.55 us -> 1.8 us
  Pallas kernels: 8.36 us -> 7.37 us
    all_to_all x2 -> x0, blocking collectives: 27 us -> none  [the longest x1 17.1 us: reduce_all(): parts = lax.all_to_all(padded, both, 0, 0)]
    ppermute x2 -> x10, starting transfers between devices: 2.57 us -> 16.7 us  [the longest x8 14.1 us: exchanged(): lax.ppermute(value, axis, [(s, s ^ distance) for s in range(lax.axis_size...]
    ppermute x2 -> x10, waiting for transfers between devices: 2.45 us -> 11.4 us  [the longest x8 10.7 us: exchanged(): lax.ppermute(value, axis, [(s, s ^ distance) for s in range(lax.axis_size...]
    unnamed x12 -> x2, local copies, waits for them, and re-layouts: 4.05 us -> 0.01 us
    pallas_call x2 -> x3, Pallas kernels: 8.36 us -> 7.37 us  [the longest x1 4.08 us: on_device(): pl.pallas_call(stiffness_kernel, out_shape=jax.ShapeDtypeStruct(blocks_sh...]
    reshape x0 -> x1, other arithmetic: none -> 0.76 us  [on_device(): value.astype(jnp.float32).reshape((-1,) + shape)]
    slice x2 -> x1, local copies, waits for them, and re-layouts: 1.54 us -> 0.9 us  [on_device(): first = own[0:1]]
    add x1 -> x4, other arithmetic: 0.51 us -> 1.03 us  [the longest x1 1 us: on_device(): state = state + jnp.pad(value, ((at, count - end), (0, 0), (0, 0)))]
  transfers between devices with their start and end apart: 3 -> 11, of which waited for: 2 -> 7; matrix products, arithmetic and copies ran while one was open for 2% -> 7% of each run, Pallas kernels for 2% -> 10%
where the time goes in v1:
time: 40.6 us; the launch traced here: 40.3 us
  starting transfers between devices  18.1 us (45%)
  waiting for transfers between devices  11.4 us (28%)
  Pallas kernels  7.37 us (18%)
  other arithmetic  1.8 us (4%)
  local copies, waits for them, and re-layouts  0.9 us (2%)
  between operations  0.7 us (2%)
    ppermute x8, starting transfers between devices, exchanged(): lax.ppermute(value, axis, [(s, s ^ distance) for s in range(lax.axis_size...  14.1 us
    ppermute x8, waiting for transfers between devices, exchanged(): lax.ppermute(value, axis, [(s, s ^ distance) for s in range(lax.axis_size...  10.7 us
    pallas_call x1, Pallas kernels, on_device(): pl.pallas_call(stiffness_kernel, out_shape=jax.ShapeDtypeStruct(blocks_sh...  4.08 us
    pallas_call x1, Pallas kernels, on_device(): pl.pallas_call(contraction_kernel, out_shape=(share, share), in_specs=[wh...  2.5 us
    ppermute x1, starting transfers between devices, on_device(): front = lax.ppermute(own, 'dom', [(s, s - 1) for s in range(1, doms)])  1.42 us
    ppermute x1, starting transfers between devices, on_device(): side = lax.ppermute(first, 'sub', [(s, s - 1) for s in range(1, subs)])  1.29 us
    ppermute x1, starting transfers between devices, on_device(): lax.ppermute(first, ('sub', 'dom'), [(s * doms + t, (s - 1) * doms + t -...  1.28 us
    add x1, other arithmetic, on_device(): state = state + jnp.pad(value, ((at, count - end), (0, 0), (0, 0)))  1 us
  transfers between devices with their start and end apart: 11, of which 7 were waited for; matrix products, arithmetic and copies ran while one was open for 7% of the time, Pallas kernels for 10%

profile of v1, /device:TPU:0, one launch (start us, length us, event | category | flops | bytes accessed | tf_op | source)
XLA Modules:
  0.0 40.3 jit_solution(9977585490511037939)
XLA Ops:
  0.6 0.0 copy-start
  0.6 1.4 %collective-permute-start = (bf16[8,384,128]{2,1,0:T(8,128)(2,1)}, bf16[8,384,128]{2,1,0:T(8,128)(2,1)S(1)}, u32[]{:S(2)}, u32[]{:S(2)}) collective-permute-start(bf16[8,384,128]{2,1,0:T(8,128)(2,1)} %bitcast.13), channel_id=1, source_target_pairs={{1,0},{2,1},{3,2},{4,3},{5,4},{6,5},{7,6},{9,8},{10,9},{11,10},{12... | collective-permute-start | bytes 2359304 | tf_op jit(solution)/shard_map/ppermute | solution.py:371
  2.1 0.9 %slice.6 = bf16[1,1,3,128,128]{4,3,2,1,0:T(8,128)(2,1)S(1)} slice(bf16[1,8,3,128,128]{4,3,2,1,0:T(8,128)(2,1)} %param.6), slice={[0:1], [0:1], [0:3], [0:128], [0:128]} | slice | bytes 196608 | tf_op jit(solution)/shard_map/slice | solution.py:372
  3.0 1.3 %collective-permute-start.2 = (bf16[1,384,128]{2,1,0:T(8,128)(2,1)S(1)}, bf16[1,384,128]{2,1,0:T(8,128)(2,1)S(1)}, u32[]{:S(2)}, u32[]{:S(2)}) collective-permute-start(bf16[1,384,128]{2,1,0:T(8,128)(2,1)S(1)} %bitcast.16), channel_id=1, source_target_pairs={{9,0},{10,1},{11,2},{12,3},{13,4},{14,5},{15,6},{17,8},{18,9},{19,... | collective-permute-start | bytes 294920 | tf_op jit(solution)/shard_map/ppermute | solution.py:374
  4.3 1.3 %collective-permute-start.1 = (bf16[1,384,128]{2,1,0:T(8,128)(2,1)S(1)}, bf16[1,384,128]{2,1,0:T(8,128)(2,1)S(1)}, u32[]{:S(2)}, u32[]{:S(2)}) collective-permute-start(bf16[1,384,128]{2,1,0:T(8,128)(2,1)S(1)} %bitcast.17), channel_id=1, source_target_pairs={{8,0},{16,8},{24,16},{9,1},{17,9},{25,17},{10,2},{18,10},{26,18},{... | collective-permute-start | bytes 294920 | tf_op jit(solution)/shard_map/ppermute | solution.py:373
  5.6 0.8 %fusion = f32[8,8,128]{2,1,0:T(8,128)S(1)} fusion(s32[8,1,8,128]{3,2,1,0:T(8,128)} %param.8), kind=kLoop, calls=%fused_computation.2 | loop fusion | flops 8192 | bytes 65536 | tf_op jit(solution)/shard_map/reshape | solution.py:383
  6.3 1.0 %pad_add_fusion.state_ref = f32[69,8,128]{2,1,0:T(8,128)S(1)} fusion(f32[3,8,128]{2,1,0:T(8,128)} %bitcast.19, f32[2,8,128]{2,1,0:T(8,128)} %bitcast.20, f32[8,8,128]{2,1,0:T(8,128)} %bitcast.18, f32[8,8,128]{2,1,0:T(8,128)S(1)} %fusion, f32[48,8,128]{2,1,0:T(8,128)} %bitcast.15), kind=kLoop, calls=%fused_computation | loop fusion | flops 282624 | bytes 565248 | tf_op jit(solution)/shard_map/add | solution.py:390
  7.3 4.1 %shard_map.77.blocks_ref = bf16[36,224,384]{2,1,0:T(8,128)(2,1)S(1)} custom-call(f32[69,8,128]{2,1,0:T(8,128)S(1)} %pad_add_fusion.state_ref), custom_call_target="tpu_custom_call" | custom-call | flops 20000000 | bytes 8000000 | tf_op jit(solution)/shard_map/pallas_call | solution.py:393
  11.4 0.0 collective-permute-done.2.corner_ref
  11.4 0.6 %collective-permute-done.1.side_ref = bf16[1,384,128]{2,1,0:T(8,128)(2,1)S(1)} collective-permute-done((bf16[1,384,128]{2,1,0:T(8,128)(2,1)S(1)}, bf16[1,384,128]{2,1,0:T(8,128)(2,1)S(1)}, u32[]{:S(2)}, u32[]{:S(2)}) %collective-permute-start.1) | collective-permute-done | bytes 98336 | tf_op jit(solution)/shard_map/ppermute | solution.py:373
  12.1 0.0 collective-permute-done.front_ref
  12.1 0.0 copy-done
  12.1 2.5 %shard_map.78 = (f32[56,128]{1,0:T(8,128)S(1)}, f32[56,128]{1,0:T(8,128)S(1)}) custom-call(bf16[8,384,128]{2,1,0:T(8,128)(2,1)S(1)} %bitcast.14, bf16[8,384,128]{2,1,0:T(8,128)(2,1)S(1)} %collective-permute-done.front_ref, bf16[1,384,128]{2,1,0:T(8,128)(2,1)S(1)} %collective-permute-done.1.side_ref, ...), custom_call_target="tpu_custom_call" | custom-call | flops 2000000000 | bytes 8000000 | tf_op jit(solution)/shard_map/pallas_call | solution.py:411
  14.6 5.7 %collective-permute-start.3 = (f32[56,128]{1,0:T(8,128)S(1)}, f32[56,128]{1,0:T(8,128)S(1)}, u32[]{:S(2)}, u32[]{:S(2)}) collective-permute-start(f32[56,128]{1,0:T(8,128)S(1)} %get-tuple-element.7), channel_id=1, source_target_pairs={{0,1},{1,0},{2,3},{3,2},{4,5},{5,4},{6,7},{7,6},{8,9},{9,8},{10,11... | collective-permute-start | bytes 86024 | tf_op jit(solution)/shard_map/ppermute | solution.py:447
  20.3 0.9 %collective-permute-done.3 = f32[56,128]{1,0:T(8,128)S(1)} collective-permute-done((f32[56,128]{1,0:T(8,128)S(1)}, f32[56,128]{1,0:T(8,128)S(1)}, u32[]{:S(2)}, u32[]{:S(2)}) %collective-permute-start.3) | collective-permute-done | bytes 28704 | tf_op jit(solution)/shard_map/ppermute | solution.py:447
  21.1 1.6 %collective-permute-start.6 = (f32[56,128]{1,0:T(8,128)S(1)}, f32[56,128]{1,0:T(8,128)S(1)}, u32[]{:S(2)}, u32[]{:S(2)}) collective-permute-start(f32[56,128]{1,0:T(8,128)S(1)} %add.47), channel_id=1, source_target_pairs={{0,2},{1,3},{2,0},{3,1},{4,6},{5,7},{6,4},{7,5},{8,10},{9,11},{10,... | collective-permute-start | bytes 86024 | tf_op jit(solution)/shard_map/ppermute | solution.py:447
  22.7 1.1 %collective-permute-start.5 = (f32[56,128]{1,0:T(8,128)S(1)}, f32[56,128]{1,0:T(8,128)S(1)}, u32[]{:S(2)}, u32[]{:S(2)}) collective-permute-start(f32[56,128]{1,0:T(8,128)S(1)} %add.47), channel_id=1, source_target_pairs={{0,4},{1,5},{2,6},{3,7},{4,0},{5,1},{6,2},{7,3},{8,12},{9,13},{10,... | collective-permute-start | bytes 86024 | tf_op jit(solution)/shard_map/ppermute | solution.py:447
  23.8 1.7 %collective-permute-start.4 = (f32[56,128]{1,0:T(8,128)S(1)}, f32[56,128]{1,0:T(8,128)S(1)}, u32[]{:S(2)}, u32[]{:S(2)}) collective-permute-start(f32[56,128]{1,0:T(8,128)S(1)} %add.47), channel_id=1, source_target_pairs={{0,6},{1,7},{2,4},{3,5},{4,2},{5,3},{6,0},{7,1},{8,14},{9,15},{10,... | collective-permute-start | bytes 86024 | tf_op jit(solution)/shard_map/ppermute | solution.py:447
  25.5 0.0 collective-permute-done.6
  25.5 2.3 %collective-permute-done.5 = f32[56,128]{1,0:T(8,128)S(1)} collective-permute-done((f32[56,128]{1,0:T(8,128)S(1)}, f32[56,128]{1,0:T(8,128)S(1)}, u32[]{:S(2)}, u32[]{:S(2)}) %collective-permute-start.5) | collective-permute-done | bytes 28704 | tf_op jit(solution)/shard_map/ppermute | solution.py:447
  27.8 1.7 %collective-permute-done.4 = f32[56,128]{1,0:T(8,128)S(1)} collective-permute-done((f32[56,128]{1,0:T(8,128)S(1)}, f32[56,128]{1,0:T(8,128)S(1)}, u32[]{:S(2)}, u32[]{:S(2)}) %collective-permute-start.4) | collective-permute-done | bytes 28704 | tf_op jit(solution)/shard_map/ppermute | solution.py:447
  29.5 1.6 %collective-permute-start.9 = (f32[56,128]{1,0:T(8,128)S(1)}, f32[56,128]{1,0:T(8,128)S(1)}, u32[]{:S(2)}, u32[]{:S(2)}) collective-permute-start(f32[56,128]{1,0:T(8,128)S(1)} %add_add_fusion.1), channel_id=1, source_target_pairs={{0,8},{8,0},{16,24},{24,16},{1,9},{9,1},{17,25},{25,17},{2,10},{10... | collective-permute-start | bytes 86024 | tf_op jit(solution)/shard_map/ppermute | solution.py:447
  31.0 2.4 %collective-permute-start.8 = (f32[56,128]{1,0:T(8,128)S(1)}, f32[56,128]{1,0:T(8,128)S(1)}, u32[]{:S(2)}, u32[]{:S(2)}) collective-permute-start(f32[56,128]{1,0:T(8,128)S(1)} %add_add_fusion.1), channel_id=1, source_target_pairs={{0,16},{8,24},{16,0},{24,8},{1,17},{9,25},{17,1},{25,9},{2,18},{10... | collective-permute-start | bytes 86024 | tf_op jit(solution)/shard_map/ppermute | solution.py:447
  33.4 0.0 collective-permute-start.7
  33.4 0.0 collective-permute-done.9
  33.4 2.0 %collective-permute-done.8 = f32[56,128]{1,0:T(8,128)S(1)} collective-permute-done((f32[56,128]{1,0:T(8,128)S(1)}, f32[56,128]{1,0:T(8,128)S(1)}, u32[]{:S(2)}, u32[]{:S(2)}) %collective-permute-start.8) | collective-permute-done | bytes 28704 | tf_op jit(solution)/shard_map/ppermute | solution.py:447
  35.4 2.8 %collective-permute-done.7 = f32[56,128]{1,0:T(8,128)S(1)} collective-permute-done((f32[56,128]{1,0:T(8,128)S(1)}, f32[56,128]{1,0:T(8,128)S(1)}, u32[]{:S(2)}, u32[]{:S(2)}) %collective-permute-start.7) | collective-permute-done | bytes 28704 | tf_op jit(solution)/shard_map/ppermute | solution.py:447
  38.2 0.1 collective-permute-start.10
  38.3 1.2 %collective-permute-done.10.other_ref = f32[56,128]{1,0:T(8,128)S(1)} collective-permute-done((f32[56,128]{1,0:T(8,128)S(1)}, f32[56,128]{1,0:T(8,128)S(1)}, u32[]{:S(2)}, u32[]{:S(2)}) %collective-permute-start.10) | collective-permute-done | bytes 28704 | tf_op jit(solution)/shard_map/ppermute | solution.py:447
  39.5 0.8 %shard_map.79 = (f32[128,128]{1,0:T(8,128)}, f32[1,128]{1,0:T(1,128)}) custom-call(f32[56,128]{1,0:T(8,128)S(1)} %add_add_fusion.mine_ref, f32[56,128]{1,0:T(8,128)S(1)} %collective-permute-done.10.other_ref), custom_call_target="tpu_custom_call" | custom-call | tf_op jit(solution)/shard_map/pallas_call | solution.py:432
  (3 shorter events, 0.0 us)
Async XLA Ops:
  0.6 11.4 %copy-start = (bf16[1,8,3,128,128]{4,3,2,1,0:T(8,128)(2,1)S(1)}, bf16[1,8,3,128,128]{4,3,2,1,0:T(8,128)(2,1)}, u32[]{:S(2)}) copy-start(bf16[1,8,3,128,128]{4,3,2,1,0:T(8,128)(2,1)} %param.6) | copy-start | bytes 2359300
  0.6 11.4 %collective-permute-start = (bf16[8,384,128]{2,1,0:T(8,128)(2,1)}, bf16[8,384,128]{2,1,0:T(8,128)(2,1)S(1)}, u32[]{:S(2)}, u32[]{:S(2)}) collective-permute-start(bf16[8,384,128]{2,1,0:T(8,128)(2,1)} %bitcast.13), channel_id=1, source_target_pairs={{1,0},{2,1},{3,2},{4,3},{5,4},{6,5},{7,6},{9,8},{10,9},{11,10},{12... | collective-permute-start | bytes 2359304 | tf_op jit(solution)/shard_map/ppermute | solution.py:371
  3.0 8.4 %collective-permute-start.2 = (bf16[1,384,128]{2,1,0:T(8,128)(2,1)S(1)}, bf16[1,384,128]{2,1,0:T(8,128)(2,1)S(1)}, u32[]{:S(2)}, u32[]{:S(2)}) collective-permute-start(bf16[1,384,128]{2,1,0:T(8,128)(2,1)S(1)} %bitcast.16), channel_id=1, source_target_pairs={{9,0},{10,1},{11,2},{12,3},{13,4},{14,5},{15,6},{17,8},{18,9},{19,... | collective-permute-start | bytes 294920 | tf_op jit(solution)/shard_map/ppermute | solution.py:374
  4.3 7.8 %collective-permute-start.1 = (bf16[1,384,128]{2,1,0:T(8,128)(2,1)S(1)}, bf16[1,384,128]{2,1,0:T(8,128)(2,1)S(1)}, u32[]{:S(2)}, u32[]{:S(2)}) collective-permute-start(bf16[1,384,128]{2,1,0:T(8,128)(2,1)S(1)} %bitcast.17), channel_id=1, source_target_pairs={{8,0},{16,8},{24,16},{9,1},{17,9},{25,17},{10,2},{18,10},{26,18},{... | collective-permute-start | bytes 294920 | tf_op jit(solution)/shard_map/ppermute | solution.py:373
  14.6 6.5 %collective-permute-start.3 = (f32[56,128]{1,0:T(8,128)S(1)}, f32[56,128]{1,0:T(8,128)S(1)}, u32[]{:S(2)}, u32[]{:S(2)}) collective-permute-start(f32[56,128]{1,0:T(8,128)S(1)} %get-tuple-element.7), channel_id=1, source_target_pairs={{0,1},{1,0},{2,3},{3,2},{4,5},{5,4},{6,7},{7,6},{8,9},{9,8},{10,11... | collective-permute-start | bytes 86024 | tf_op jit(solution)/shard_map/ppermute | solution.py:447
  21.1 4.4 %collective-permute-start.6 = (f32[56,128]{1,0:T(8,128)S(1)}, f32[56,128]{1,0:T(8,128)S(1)}, u32[]{:S(2)}, u32[]{:S(2)}) collective-permute-start(f32[56,128]{1,0:T(8,128)S(1)} %add.47), channel_id=1, source_target_pairs={{0,2},{1,3},{2,0},{3,1},{4,6},{5,7},{6,4},{7,5},{8,10},{9,11},{10,... | collective-permute-start | bytes 86024 | tf_op jit(solution)/shard_map/ppermute | solution.py:447
  22.7 5.1 %collective-permute-start.5 = (f32[56,128]{1,0:T(8,128)S(1)}, f32[56,128]{1,0:T(8,128)S(1)}, u32[]{:S(2)}, u32[]{:S(2)}) collective-permute-start(f32[56,128]{1,0:T(8,128)S(1)} %add.47), channel_id=1, source_target_pairs={{0,4},{1,5},{2,6},{3,7},{4,0},{5,1},{6,2},{7,3},{8,12},{9,13},{10,... | collective-permute-start | bytes 86024 | tf_op jit(solution)/shard_map/ppermute | solution.py:447
  23.8 5.7 %collective-permute-start.4 = (f32[56,128]{1,0:T(8,128)S(1)}, f32[56,128]{1,0:T(8,128)S(1)}, u32[]{:S(2)}, u32[]{:S(2)}) collective-permute-start(f32[56,128]{1,0:T(8,128)S(1)} %add.47), channel_id=1, source_target_pairs={{0,6},{1,7},{2,4},{3,5},{4,2},{5,3},{6,0},{7,1},{8,14},{9,15},{10,... | collective-permute-start | bytes 86024 | tf_op jit(solution)/shard_map/ppermute | solution.py:447
  29.5 4.0 %collective-permute-start.9 = (f32[56,128]{1,0:T(8,128)S(1)}, f32[56,128]{1,0:T(8,128)S(1)}, u32[]{:S(2)}, u32[]{:S(2)}) collective-permute-start(f32[56,128]{1,0:T(8,128)S(1)} %add_add_fusion.1), channel_id=1, source_target_pairs={{0,8},{8,0},{16,24},{24,16},{1,9},{9,1},{17,25},{25,17},{2,10},{10... | collective-permute-start | bytes 86024 | tf_op jit(solution)/shard_map/ppermute | solution.py:447
  31.0 4.4 %collective-permute-start.8 = (f32[56,128]{1,0:T(8,128)S(1)}, f32[56,128]{1,0:T(8,128)S(1)}, u32[]{:S(2)}, u32[]{:S(2)}) collective-permute-start(f32[56,128]{1,0:T(8,128)S(1)} %add_add_fusion.1), channel_id=1, source_target_pairs={{0,16},{8,24},{16,0},{24,8},{1,17},{9,25},{17,1},{25,9},{2,18},{10... | collective-permute-start | bytes 86024 | tf_op jit(solution)/shard_map/ppermute | solution.py:447
  33.4 4.8 %collective-permute-start.7 = (f32[56,128]{1,0:T(8,128)S(1)}, f32[56,128]{1,0:T(8,128)S(1)}, u32[]{:S(2)}, u32[]{:S(2)}) collective-permute-start(f32[56,128]{1,0:T(8,128)S(1)} %add_add_fusion.1), channel_id=1, source_target_pairs={{0,24},{8,16},{16,8},{24,0},{1,25},{9,17},{17,9},{25,1},{2,26},{10... | collective-permute-start | bytes 86024 | tf_op jit(solution)/shard_map/ppermute | solution.py:447
  38.2 1.3 %collective-permute-start.10 = (f32[56,128]{1,0:T(8,128)S(1)}, f32[56,128]{1,0:T(8,128)S(1)}, u32[]{:S(2)}, u32[]{:S(2)}) collective-permute-start(f32[56,128]{1,0:T(8,128)S(1)} %add_add_fusion.mine_ref), channel_id=1, source_target_pairs={{0,1},{1,0},{2,3},{3,2},{4,5},{5,4},{6,7},{7,6},{8,9},{9,8},{10,11... | collective-permute-start | bytes 86024 | tf_op jit(solution)/shard_map/ppermute | solution.py:447

commit v2 on v1

--- a/solution.py
+++ b/solution.py
@@ -270,63 +270,78 @@
             blocks_ref[at, edge_at:load_at] = edge_ref[...].astype(jnp.bfloat16)
 
 
-def contraction_kernel(
-    own_ref, front_ref, side_ref, corner_ref, blocks_ref, mine_ref, other_ref,
-    gather_ref, carry_ref, sum_ref, packed_ref,
-):
+def contract(y, planes, depth, blocks_ref, gather_ref, carry_ref, sum_ref):
+    modes = sum_ref.shape[1]
+    span = depth // PARTS
+    own_lanes = lax.broadcasted_iota(jnp.int32, (modes, depth), 1) < 2 * span
+    nothing = jnp.zeros((8, modes), jnp.float32)
+
+    def rows(p, first, count):
+        ref, at = planes[p // 3]
+        start = (p % 3) * depth + first
+        return ref[at, start : start + count]
+
+    for border in range(1, PARTS):
+        for p in range(6):
+            around = rows(p, border * span - TILE, 2 * TILE).astype(jnp.float32)
+            at = ((border - 1) * 8 + p) * TILE
+            gather_ref[at : at + TILE] = around[TILE // 2 : TILE + TILE // 2]
+    total = sum_ref[...]
+    for part in range(PARTS):
+        before, after = nothing, nothing
+        if part > 0:
+            before = gather_ref[pl.ds((part - 1) * 8 * TILE + TILE // 2 - 1, 8, TILE)]
+        if part < PARTS - 1:
+            after = gather_ref[pl.ds(part * 8 * TILE + TILE // 2, 8, TILE)]
+        edges = jnp.concatenate([before, after], 0).astype(jnp.bfloat16)
+        here = jnp.concatenate([rows(p, part * span, span) for p in range(6)], 0)
+        turned = jnp.concatenate([here, edges], 0).T
+        at = y * PARTS + part
+        product = jnp.dot(
+            turned, blocks_ref[at, 0 : 6 * span + TILE], preferred_element_type=jnp.float32
+        )
+        first = product[:, 0:depth] + carry_ref[part, 0]
+        middle = product[:, depth : 2 * depth]
+        second = jnp.where(own_lanes, middle + carry_ref[part, 1], 0.0)
+        carry_ref[part, 0] = product[:, 2 * depth :]
+        carry_ref[part, 1] = pltpu.roll(middle, 2 * span, 1)
+        factors = jnp.concatenate([first, second], 1).astype(jnp.bfloat16)
+        factors = jnp.concatenate(
+            [factors, blocks_ref[at, 6 * span + TILE : 6 * span + 2 * TILE, 0 : 2 * depth]], 0
+        )
+        total = total + jnp.dot(
+            factors[:, 0 : 6 * span], here, preferred_element_type=jnp.float32
+        )
+    sum_ref[...] = total
+
+
+def contraction_kernel(own_ref, front_ref, blocks_ref, sum_ref, carry_ref, gather_ref):
     columns, plane_rows, modes = own_ref.shape
-    depth = plane_rows // 3
-    span = depth // PARTS
     carry_ref[...] = jnp.zeros_like(carry_ref)
     gather_ref[...] = jnp.zeros_like(gather_ref)
     sum_ref[...] = jnp.zeros_like(sum_ref)
-    own_lanes = lax.broadcasted_iota(jnp.int32, (modes, depth), 1) < 2 * span
-    nothing = jnp.zeros((8, modes), jnp.float32)
-
-    def group(y, planes):
-        def rows(p, first, count):
-            ref, at = planes[p // 3]
-            start = (p % 3) * depth + first
-            return ref[at, start : start + count]
-
-        for border in range(1, PARTS):
-            for p in range(6):
-                around = rows(p, border * span - TILE, 2 * TILE).astype(jnp.float32)
-                at = ((border - 1) * 8 + p) * TILE
-                gather_ref[at : at + TILE] = around[TILE // 2 : TILE + TILE // 2]
-        total = sum_ref[...]
-        for part in range(PARTS):
-            before, after = nothing, nothing
-            if part > 0:
-                before = gather_ref[pl.ds((part - 1) * 8 * TILE + TILE // 2 - 1, 8, TILE)]
-            if part < PARTS - 1:
-                after = gather_ref[pl.ds(part * 8 * TILE + TILE // 2, 8, TILE)]
-            edges = jnp.concatenate([before, after], 0).astype(jnp.bfloat16)
-            here = jnp.concatenate([rows(p, part * span, span) for p in range(6)], 0)
-            turned = jnp.concatenate([here, edges], 0).T
-            at = y * PARTS + part
-            product = jnp.dot(
-                turned, blocks_ref[at, 0 : 6 * span + TILE], preferred_element_type=jnp.float32
-            )
-            first = product[:, 0:depth] + carry_ref[part, 0]
-            middle = product[:, depth : 2 * depth]
-            second = jnp.where(own_lanes, middle + carry_ref[part, 1], 0.0)
-            carry_ref[part, 0] = product[:, 2 * depth :]
-            carry_ref[part, 1] = pltpu.roll(middle, 2 * span, 1)
-            factors = jnp.concatenate([first, second], 1).astype(jnp.bfloat16)
-            factors = jnp.concatenate(
-                [factors, blocks_ref[at, 6 * span + TILE : 6 * span + 2 * TILE, 0 : 2 * depth]], 0
-            )
-            total = total + jnp.dot(
-                factors[:, 0 : 6 * span], here, preferred_element_type=jnp.float32
-            )
-        sum_ref[...] = total
 
     @pl.loop(0, columns, unroll=True)
     def _(y):
-        group(y, ((own_ref, y), (front_ref, y)))
-
-    group(columns, ((side_ref, 0), (corner_ref, 0)))
+        planes = ((own_ref, y), (front_ref, y))
+        contract(y, planes, plane_rows // 3, blocks_ref, gather_ref, carry_ref, sum_ref)
+
+
+def last_kernel(
+    side_ref, corner_ref, blocks_ref, sum_in, carry_in, mine_ref, other_ref,
+    gather_ref, carry_ref, sum_ref, packed_ref, ends_ref,
+):
+    inside = lax.axis_index("sub") < lax.axis_size("sub") - 1
+    ends_ref[0:1] = jnp.where(inside, side_ref[...], jnp.bfloat16(0))
+    inside = inside & (lax.axis_index("dom") < lax.axis_size("dom") - 1)
+    ends_ref[1:2] = jnp.where(inside, corner_ref[...], jnp.bfloat16(0))
+    ignored, plane_rows, modes = side_ref.shape
+    columns = blocks_ref.shape[0] // PARTS - 1
+    carry_ref[...] = carry_in[...]
+    gather_ref[...] = jnp.zeros_like(gather_ref)
+    sum_ref[...] = sum_in[...]
+    planes = ((ends_ref, 0), (ends_ref, 1))
+    contract(columns, planes, plane_rows // 3, blocks_ref, gather_ref, carry_ref, sum_ref)
     total = sum_ref[...]
     upper = total[0:modes]
     tangent = upper + upper.T
@@ -370,24 +385,28 @@
     doms, subs = lax.axis_size("dom"), lax.axis_size("sub")
     front = lax.ppermute(own, "dom", [(s, s - 1) for s in range(1, doms)])
     first = own[0:1]
-    side = lax.ppermute(first, "sub", [(s, s - 1) for s in range(1, subs)])
     corner = lax.ppermute(
         first,
         ("sub", "dom"),
-        [(s * doms + t, (s - 1) * doms + t - 1) for s in range(1, subs) for t in range(1, doms)],
+        [
+            (s * doms + t, (s - 1) % subs * doms + (t - 1) % doms)
+            for s in range(subs)
+            for t in range(doms)
+        ],
     )
+    side = lax.ppermute(first, "sub", [(s, (s - 1) % subs) for s in range(subs)])
     shape = (columns, depth)
     block_rows = 6 * (depth // PARTS) + 2 * TILE
     blocks_shape = ((columns + 1) * PARTS, block_rows, len(SLOTS) * depth)
     fields = [
-        value.astype(jnp.float32).reshape((-1,) + shape)
+        value.reshape((-1,) + shape)
         for value in (gauss_stress, yield_flags, consolidation, elastic_moduli, element_sizes)
     ]
     count = sum(value.shape[0] for value in fields)
     state, at = 0.0, 0
     for value in fields:
         end = at + value.shape[0]
-        state = state + jnp.pad(value, ((at, count - end), (0, 0), (0, 0)))
+        state = state + jnp.pad(value, ((at, count - end), (0, 0), (0, 0))).astype(jnp.float32)
         at = end
     whole = pl.BlockSpec(memory_space=pltpu.VMEM)
     blocks = pl.pallas_call(
@@ -408,20 +427,33 @@
     )(state)
     packed_rows = -(-(modes // 2 + modes // 4 + 1) // 16) * 16
     share = jax.ShapeDtypeStruct((packed_rows // 2, modes), jnp.float32)
+    gather_scratch = pltpu.VMEM(((PARTS - 1) * 8 * TILE + TILE, modes), jnp.float32)
+    sum_shape = jax.ShapeDtypeStruct((modes + TILE, modes), jnp.float32)
+    carry_shape = jax.ShapeDtypeStruct((PARTS, 2, modes, depth), jnp.float32)
+    partial, carry = pl.pallas_call(
+        contraction_kernel,
+        out_shape=(sum_shape, carry_shape),
+        in_specs=[whole] * 3,
+        out_specs=(whole, whole),
+        scratch_shapes=[gather_scratch],
+        compiler_params=pltpu.CompilerParams(vmem_limit_bytes=24 * 2**20),
+        cost_estimate=pl.CostEstimate(flops=2_000_000_000, bytes_accessed=8_000_000, transcendentals=0),
+    )(own, front, blocks)
     mine, other = pl.pallas_call(
-        contraction_kernel,
+        last_kernel,
         out_shape=(share, share),
         in_specs=[whole] * 5,
         out_specs=(whole, whole),
         scratch_shapes=[
-            pltpu.VMEM(((PARTS - 1) * 8 * TILE + TILE, modes), jnp.float32),
-            pltpu.VMEM((PARTS, 2, modes, depth), jnp.float32),
-            pltpu.VMEM((modes + TILE, modes), jnp.float32),
+            gather_scratch,
+            pltpu.VMEM(carry_shape.shape, jnp.float32),
+            pltpu.VMEM(sum_shape.shape, jnp.float32),
             pltpu.VMEM((packed_rows, modes), jnp.float32),
+            pltpu.VMEM((2, plane_rows, modes), jnp.bfloat16),
         ],
         compiler_params=pltpu.CompilerParams(vmem_limit_bytes=24 * 2**20),
-        cost_estimate=pl.CostEstimate(flops=2_000_000_000, bytes_accessed=8_000_000, transcendentals=0),
-    )(own, front, side, corner, blocks)
+        cost_estimate=pl.CostEstimate(flops=200_000_000, bytes_accessed=1_000_000, transcendentals=0),
+    )(side, corner, blocks, partial, carry)
 
     mine = mine + exchanged(other, "dom", 1)
     for axis, first in (("dom", 2), ("sub", 1)):

time: 40.6 us -> 36 us (0.89)
  waiting for transfers between devices: 11.4 us -> 7.87 us
  other arithmetic: 1.8 us -> 1.05 us
  starting transfers between devices: 18.1 us -> 17.5 us
    ppermute x8, starting transfers between devices: 14.1 us -> 8.08 us  [exchanged(): lax.ppermute(value, axis, [(s, s ^ distance) for s in range(lax.axis_size...]
    ppermute x2, starting transfers between devices: 2.57 us -> 7.96 us  [the longest x1 4.07 us: on_device(): lax.ppermute(first, ('sub', 'dom'), [(s * doms + t, (s - 1) % subs * doms...]
    ppermute x8, waiting for transfers between devices: 10.7 us -> 7.86 us  [exchanged(): lax.ppermute(value, axis, [(s, s ^ distance) for s in range(lax.axis_size...]
    reshape x1 -> x0, other arithmetic: 0.76 us -> none  [on_device(): value.astype(jnp.float32).reshape((-1,) + shape)]
    ppermute x2, waiting for transfers between devices: 0.63 us -> 0.01 us  [the longest x1 0.01 us: on_device(): lax.ppermute(first, 'sub', [(s, (s - 1) % subs) for s in range(subs)])]
    pallas_call x1 -> x2, Pallas kernels: 2.5 us -> 2.89 us  [the longest x1 2.21 us: on_device(): pl.pallas_call(contraction_kernel, out_shape=(sum_shape, carry_shape), in...]
  transfers between devices with their start and end apart: 11 -> 11, of which waited for: 7 -> 8; matrix products, arithmetic and copies ran while one was open for 7% -> 5% of each run, Pallas kernels for 10% -> 18%
where the time goes in v2:
time: 36 us; the launch traced here: 35.8 us
  starting transfers between devices  17.5 us (49%)
  waiting for transfers between devices  7.87 us (22%)
  Pallas kernels  7.76 us (22%)
  other arithmetic  1.05 us (3%)
  local copies, waits for them, and re-layouts  0.9 us (2%)
  between operations  0.72 us (2%)
    ppermute x8, starting transfers between devices, exchanged(): lax.ppermute(value, axis, [(s, s ^ distance) for s in range(lax.axis_size...  8.08 us
    ppermute x8, waiting for transfers between devices, exchanged(): lax.ppermute(value, axis, [(s, s ^ distance) for s in range(lax.axis_size...  7.86 us
    pallas_call x1, Pallas kernels, on_device(): pl.pallas_call(stiffness_kernel, out_shape=jax.ShapeDtypeStruct(blocks_sh...  4.08 us
    ppermute x1, starting transfers between devices, on_device(): lax.ppermute(first, ('sub', 'dom'), [(s * doms + t, (s - 1) % subs * doms...  4.07 us
    ppermute x1, starting transfers between devices, on_device(): lax.ppermute(first, 'sub', [(s, (s - 1) % subs) for s in range(subs)])  3.89 us
    pallas_call x1, Pallas kernels, on_device(): pl.pallas_call(contraction_kernel, out_shape=(sum_shape, carry_shape), in...  2.21 us
    ppermute x1, starting transfers between devices, on_device(): front = lax.ppermute(own, 'dom', [(s, s - 1) for s in range(1, doms)])  1.42 us
    add x1, other arithmetic, on_device(): state + jnp.pad(value, ((at, count - end), (0, 0), (0, 0))).astype(jnp.fl...  1.02 us
  transfers between devices with their start and end apart: 11, of which 8 were waited for; matrix products, arithmetic and copies ran while one was open for 5% of the time, Pallas kernels for 18%

profile of v2, /device:TPU:0, one launch (start us, length us, event | category | flops | bytes accessed | tf_op | source)
XLA Modules:
  0.0 35.8 jit_solution(382623906299861238)
XLA Ops:
  0.6 0.0 copy-start
  0.6 1.4 %collective-permute-start.2 = (bf16[8,384,128]{2,1,0:T(8,128)(2,1)}, bf16[8,384,128]{2,1,0:T(8,128)(2,1)S(1)}, u32[]{:S(2)}, u32[]{:S(2)}) collective-permute-start(bf16[8,384,128]{2,1,0:T(8,128)(2,1)} %bitcast.8), channel_id=1, source_target_pairs={{1,0},{2,1},{3,2},{4,3},{5,4},{6,5},{7,6},{9,8},{10,9},{11,10},{12... | collective-permute-start | bytes 2359304 | tf_op jit(solution)/shard_map/ppermute | solution.py:386
  2.1 0.9 %slice.6 = bf16[1,1,3,128,128]{4,3,2,1,0:T(8,128)(2,1)S(1)} slice(bf16[1,8,3,128,128]{4,3,2,1,0:T(8,128)(2,1)} %param.6), slice={[0:1], [0:1], [0:3], [0:128], [0:128]} | slice | bytes 196608 | tf_op jit(solution)/shard_map/slice | solution.py:387
  3.0 3.9 %collective-permute-start = (bf16[1,384,128]{2,1,0:T(8,128)(2,1)S(1)}, bf16[1,384,128]{2,1,0:T(8,128)(2,1)S(1)}, u32[]{:S(2)}, u32[]{:S(2)}) collective-permute-start(bf16[1,384,128]{2,1,0:T(8,128)(2,1)S(1)} %bitcast.11), channel_id=1, source_target_pairs={{0,24},{8,0},{16,8},{24,16},{1,25},{9,1},{17,9},{25,17},{2,26},{10... | collective-permute-start | bytes 294920 | tf_op jit(solution)/shard_map/ppermute | solution.py:397
  6.9 4.1 %collective-permute-start.1 = (bf16[1,384,128]{2,1,0:T(8,128)(2,1)S(1)}, bf16[1,384,128]{2,1,0:T(8,128)(2,1)S(1)}, u32[]{:S(2)}, u32[]{:S(2)}) collective-permute-start(bf16[1,384,128]{2,1,0:T(8,128)(2,1)S(1)} %bitcast.12), channel_id=1, source_target_pairs={{0,31},{1,24},{2,25},{3,26},{4,27},{5,28},{6,29},{7,30},{8,7},{9,0... | collective-permute-start | bytes 294920 | tf_op jit(solution)/shard_map/ppermute | solution.py:388
  10.9 1.0 %pad_add_fusion.state_ref = f32[69,8,128]{2,1,0:T(8,128)S(1)} fusion(f32[3,8,128]{2,1,0:T(8,128)} %bitcast.15, f32[2,8,128]{2,1,0:T(8,128)} %bitcast.16, f32[8,8,128]{2,1,0:T(8,128)} %bitcast.13, s32[8,8,128]{2,1,0:T(8,128)} %bitcast.14, f32[48,8,128]{2,1,0:T(8,128)} %bitcast.10), kind=kLoop, calls=%fused_computation | loop fusion | flops 353280 | bytes 565248 | tf_op jit(solution)/shard_map/add | solution.py:409
  12.0 4.1 %shard_map.77.blocks_ref = bf16[36,224,384]{2,1,0:T(8,128)(2,1)S(1)} custom-call(f32[69,8,128]{2,1,0:T(8,128)S(1)} %pad_add_fusion.state_ref), custom_call_target="tpu_custom_call" | custom-call | flops 20000000 | bytes 8000000 | tf_op jit(solution)/shard_map/pallas_call | solution.py:412
  16.0 0.0 collective-permute-done.2.front_ref
  16.1 0.0 copy-done
  16.1 2.2 %shard_map.78 = (f32[144,128]{1,0:T(8,128)S(1)}, f32[4,2,128,128]{3,2,1,0:T(8,128)S(1)}) custom-call(bf16[8,384,128]{2,1,0:T(8,128)(2,1)S(1)} %bitcast.9, bf16[8,384,128]{2,1,0:T(8,128)(2,1)S(1)} %collective-permute-done.2.front_ref, bf16[36,224,384]{2,1,0:T(8,128)(2,1)S(1)} %shard_map.77.blocks_ref), custom_call_target="tpu_custom_call" | custom-call | flops 2000000000 | bytes 8000000 | tf_op jit(solution)/shard_map/pallas_call | solution.py:433
  18.3 0.0 collective-permute-done.side_ref
  18.3 0.0 collective-permute-done.1.corner_ref
  18.3 0.7 %shard_map.79 = (f32[56,128]{1,0:T(8,128)S(1)}, f32[56,128]{1,0:T(8,128)S(1)}) custom-call(bf16[1,384,128]{2,1,0:T(8,128)(2,1)S(1)} %collective-permute-done.side_ref, bf16[1,384,128]{2,1,0:T(8,128)(2,1)S(1)} %collective-permute-done.1.corner_ref, bf16[36,224,384]{2,1,0:T(8,128)(2,1)S(1)} %shard_map.77.blocks_ref, f32[144,128]{1,0:T(8,128)S(1)} %get-tuple-element.8.sum_in, ...), custom_call_target="tpu_custom_call" | custom-call | flops 200000000 | bytes 1000000 | tf_op jit(solution)/shard_map/pallas_call | solution.py:442
  19.0 0.1 collective-permute-start.3
  19.1 1.2 %collective-permute-done.3 = f32[56,128]{1,0:T(8,128)S(1)} collective-permute-done((f32[56,128]{1,0:T(8,128)S(1)}, f32[56,128]{1,0:T(8,128)S(1)}, u32[]{:S(2)}, u32[]{:S(2)}) %collective-permute-start.3) | collective-permute-done | bytes 28704 | tf_op jit(solution)/shard_map/ppermute | solution.py:479
  20.3 1.5 %collective-permute-start.4 = (f32[56,128]{1,0:T(8,128)S(1)}, f32[56,128]{1,0:T(8,128)S(1)}, u32[]{:S(2)}, u32[]{:S(2)}) collective-permute-start(f32[56,128]{1,0:T(8,128)S(1)} %add.47), channel_id=1, source_target_pairs={{0,6},{1,7},{2,4},{3,5},{4,2},{5,3},{6,0},{7,1},{8,14},{9,15},{10,... | collective-permute-start | bytes 86024 | tf_op jit(solution)/shard_map/ppermute | solution.py:479
  21.7 0.8 %collective-permute-start.5 = (f32[56,128]{1,0:T(8,128)S(1)}, f32[56,128]{1,0:T(8,128)S(1)}, u32[]{:S(2)}, u32[]{:S(2)}) collective-permute-start(f32[56,128]{1,0:T(8,128)S(1)} %add.47), channel_id=1, source_target_pairs={{0,4},{1,5},{2,6},{3,7},{4,0},{5,1},{6,2},{7,3},{8,12},{9,13},{10,... | collective-permute-start | bytes 86024 | tf_op jit(solution)/shard_map/ppermute | solution.py:479
  22.6 2.1 %collective-permute-start.6 = (f32[56,128]{1,0:T(8,128)S(1)}, f32[56,128]{1,0:T(8,128)S(1)}, u32[]{:S(2)}, u32[]{:S(2)}) collective-permute-start(f32[56,128]{1,0:T(8,128)S(1)} %add.47), channel_id=1, source_target_pairs={{0,2},{1,3},{2,0},{3,1},{4,6},{5,7},{6,4},{7,5},{8,10},{9,11},{10,... | collective-permute-start | bytes 86024 | tf_op jit(solution)/shard_map/ppermute | solution.py:479
  24.6 1.5 %collective-permute-done.4 = f32[56,128]{1,0:T(8,128)S(1)} collective-permute-done((f32[56,128]{1,0:T(8,128)S(1)}, f32[56,128]{1,0:T(8,128)S(1)}, u32[]{:S(2)}, u32[]{:S(2)}) %collective-permute-start.4) | collective-permute-done | bytes 28704 | tf_op jit(solution)/shard_map/ppermute | solution.py:479
  26.2 0.4 %collective-permute-done.5 = f32[56,128]{1,0:T(8,128)S(1)} collective-permute-done((f32[56,128]{1,0:T(8,128)S(1)}, f32[56,128]{1,0:T(8,128)S(1)}, u32[]{:S(2)}, u32[]{:S(2)}) %collective-permute-start.5) | collective-permute-done | bytes 28704 | tf_op jit(solution)/shard_map/ppermute | solution.py:479
  26.6 0.2 collective-permute-done.6
  26.8 2.5 %collective-permute-start.7 = (f32[56,128]{1,0:T(8,128)S(1)}, f32[56,128]{1,0:T(8,128)S(1)}, u32[]{:S(2)}, u32[]{:S(2)}) collective-permute-start(f32[56,128]{1,0:T(8,128)S(1)} %add_add_fusion.1), channel_id=1, source_target_pairs={{0,24},{8,16},{16,8},{24,0},{1,25},{9,17},{17,9},{25,1},{2,26},{10... | collective-permute-start | bytes 86024 | tf_op jit(solution)/shard_map/ppermute | solution.py:479
  29.3 0.6 %collective-permute-start.8 = (f32[56,128]{1,0:T(8,128)S(1)}, f32[56,128]{1,0:T(8,128)S(1)}, u32[]{:S(2)}, u32[]{:S(2)}) collective-permute-start(f32[56,128]{1,0:T(8,128)S(1)} %add_add_fusion.1), channel_id=1, source_target_pairs={{0,16},{8,24},{16,0},{24,8},{1,17},{9,25},{17,1},{25,9},{2,18},{10... | collective-permute-start | bytes 86024 | tf_op jit(solution)/shard_map/ppermute | solution.py:479
  29.8 0.5 %collective-permute-start.9 = (f32[56,128]{1,0:T(8,128)S(1)}, f32[56,128]{1,0:T(8,128)S(1)}, u32[]{:S(2)}, u32[]{:S(2)}) collective-permute-start(f32[56,128]{1,0:T(8,128)S(1)} %add_add_fusion.1), channel_id=1, source_target_pairs={{0,8},{8,0},{16,24},{24,16},{1,9},{9,1},{17,25},{25,17},{2,10},{10... | collective-permute-start | bytes 86024 | tf_op jit(solution)/shard_map/ppermute | solution.py:479
  30.4 1.3 %collective-permute-done.7 = f32[56,128]{1,0:T(8,128)S(1)} collective-permute-done((f32[56,128]{1,0:T(8,128)S(1)}, f32[56,128]{1,0:T(8,128)S(1)}, u32[]{:S(2)}, u32[]{:S(2)}) %collective-permute-start.7) | collective-permute-done | bytes 28704 | tf_op jit(solution)/shard_map/ppermute | solution.py:479
  31.6 1.5 %collective-permute-done.8 = f32[56,128]{1,0:T(8,128)S(1)} collective-permute-done((f32[56,128]{1,0:T(8,128)S(1)}, f32[56,128]{1,0:T(8,128)S(1)}, u32[]{:S(2)}, u32[]{:S(2)}) %collective-permute-start.8) | collective-permute-done | bytes 28704 | tf_op jit(solution)/shard_map/ppermute | solution.py:479
  33.1 0.6 %collective-permute-done.9 = f32[56,128]{1,0:T(8,128)S(1)} collective-permute-done((f32[56,128]{1,0:T(8,128)S(1)}, f32[56,128]{1,0:T(8,128)S(1)}, u32[]{:S(2)}, u32[]{:S(2)}) %collective-permute-start.9) | collective-permute-done | bytes 28704 | tf_op jit(solution)/shard_map/ppermute | solution.py:479
  33.7 0.1 collective-permute-start.10
  33.8 1.2 %collective-permute-done.10.other_ref = f32[56,128]{1,0:T(8,128)S(1)} collective-permute-done((f32[56,128]{1,0:T(8,128)S(1)}, f32[56,128]{1,0:T(8,128)S(1)}, u32[]{:S(2)}, u32[]{:S(2)}) %collective-permute-start.10) | collective-permute-done | bytes 28704 | tf_op jit(solution)/shard_map/ppermute | solution.py:479
  35.0 0.8 %shard_map.80 = (f32[128,128]{1,0:T(8,128)}, f32[1,128]{1,0:T(1,128)}) custom-call(f32[56,128]{1,0:T(8,128)S(1)} %add_add_fusion.mine_ref, f32[56,128]{1,0:T(8,128)S(1)} %collective-permute-done.10.other_ref), custom_call_target="tpu_custom_call" | custom-call | tf_op jit(solution)/shard_map/pallas_call | solution.py:464
  (3 shorter events, 0.0 us)
Async XLA Ops:
  0.6 15.4 %copy-start = (bf16[1,8,3,128,128]{4,3,2,1,0:T(8,128)(2,1)S(1)}, bf16[1,8,3,128,128]{4,3,2,1,0:T(8,128)(2,1)}, u32[]{:S(2)}) copy-start(bf16[1,8,3,128,128]{4,3,2,1,0:T(8,128)(2,1)} %param.6) | copy-start | bytes 2359300
  0.6 15.4 %collective-permute-start.2 = (bf16[8,384,128]{2,1,0:T(8,128)(2,1)}, bf16[8,384,128]{2,1,0:T(8,128)(2,1)S(1)}, u32[]{:S(2)}, u32[]{:S(2)}) collective-permute-start(bf16[8,384,128]{2,1,0:T(8,128)(2,1)} %bitcast.8), channel_id=1, source_target_pairs={{1,0},{2,1},{3,2},{4,3},{5,4},{6,5},{7,6},{9,8},{10,9},{11,10},{12... | collective-permute-start | bytes 2359304 | tf_op jit(solution)/shard_map/ppermute | solution.py:386
  3.0 15.3 %collective-permute-start = (bf16[1,384,128]{2,1,0:T(8,128)(2,1)S(1)}, bf16[1,384,128]{2,1,0:T(8,128)(2,1)S(1)}, u32[]{:S(2)}, u32[]{:S(2)}) collective-permute-start(bf16[1,384,128]{2,1,0:T(8,128)(2,1)S(1)} %bitcast.11), channel_id=1, source_target_pairs={{0,24},{8,0},{16,8},{24,16},{1,25},{9,1},{17,9},{25,17},{2,26},{10... | collective-permute-start | bytes 294920 | tf_op jit(solution)/shard_map/ppermute | solution.py:397
  6.9 11.4 %collective-permute-start.1 = (bf16[1,384,128]{2,1,0:T(8,128)(2,1)S(1)}, bf16[1,384,128]{2,1,0:T(8,128)(2,1)S(1)}, u32[]{:S(2)}, u32[]{:S(2)}) collective-permute-start(bf16[1,384,128]{2,1,0:T(8,128)(2,1)S(1)} %bitcast.12), channel_id=1, source_target_pairs={{0,31},{1,24},{2,25},{3,26},{4,27},{5,28},{6,29},{7,30},{8,7},{9,0... | collective-permute-start | bytes 294920 | tf_op jit(solution)/shard_map/ppermute | solution.py:388
  19.0 1.3 %collective-permute-start.3 = (f32[56,128]{1,0:T(8,128)S(1)}, f32[56,128]{1,0:T(8,128)S(1)}, u32[]{:S(2)}, u32[]{:S(2)}) collective-permute-start(f32[56,128]{1,0:T(8,128)S(1)} %get-tuple-element.11), channel_id=1, source_target_pairs={{0,1},{1,0},{2,3},{3,2},{4,5},{5,4},{6,7},{7,6},{8,9},{9,8},{10,11... | collective-permute-start | bytes 86024 | tf_op jit(solution)/shard_map/ppermute | solution.py:479
  20.3 5.9 %collective-permute-start.4 = (f32[56,128]{1,0:T(8,128)S(1)}, f32[56,128]{1,0:T(8,128)S(1)}, u32[]{:S(2)}, u32[]{:S(2)}) collective-permute-start(f32[56,128]{1,0:T(8,128)S(1)} %add.47), channel_id=1, source_target_pairs={{0,6},{1,7},{2,4},{3,5},{4,2},{5,3},{6,0},{7,1},{8,14},{9,15},{10,... | collective-permute-start | bytes 86024 | tf_op jit(solution)/shard_map/ppermute | solution.py:479
  21.7 4.8 %collective-permute-start.5 = (f32[56,128]{1,0:T(8,128)S(1)}, f32[56,128]{1,0:T(8,128)S(1)}, u32[]{:S(2)}, u32[]{:S(2)}) collective-permute-start(f32[56,128]{1,0:T(8,128)S(1)} %add.47), channel_id=1, source_target_pairs={{0,4},{1,5},{2,6},{3,7},{4,0},{5,1},{6,2},{7,3},{8,12},{9,13},{10,... | collective-permute-start | bytes 86024 | tf_op jit(solution)/shard_map/ppermute | solution.py:479
  22.6 4.2 %collective-permute-start.6 = (f32[56,128]{1,0:T(8,128)S(1)}, f32[56,128]{1,0:T(8,128)S(1)}, u32[]{:S(2)}, u32[]{:S(2)}) collective-permute-start(f32[56,128]{1,0:T(8,128)S(1)} %add.47), channel_id=1, source_target_pairs={{0,2},{1,3},{2,0},{3,1},{4,6},{5,7},{6,4},{7,5},{8,10},{9,11},{10,... | collective-permute-start | bytes 86024 | tf_op jit(solution)/shard_map/ppermute | solution.py:479
  26.8 4.8 %collective-permute-start.7 = (f32[56,128]{1,0:T(8,128)S(1)}, f32[56,128]{1,0:T(8,128)S(1)}, u32[]{:S(2)}, u32[]{:S(2)}) collective-permute-start(f32[56,128]{1,0:T(8,128)S(1)} %add_add_fusion.1), channel_id=1, source_target_pairs={{0,24},{8,16},{16,8},{24,0},{1,25},{9,17},{17,9},{25,1},{2,26},{10... | collective-permute-start | bytes 86024 | tf_op jit(solution)/shard_map/ppermute | solution.py:479
  29.3 3.9 %collective-permute-start.8 = (f32[56,128]{1,0:T(8,128)S(1)}, f32[56,128]{1,0:T(8,128)S(1)}, u32[]{:S(2)}, u32[]{:S(2)}) collective-permute-start(f32[56,128]{1,0:T(8,128)S(1)} %add_add_fusion.1), channel_id=1, source_target_pairs={{0,16},{8,24},{16,0},{24,8},{1,17},{9,25},{17,1},{25,9},{2,18},{10... | collective-permute-start | bytes 86024 | tf_op jit(solution)/shard_map/ppermute | solution.py:479
  29.8 3.9 %collective-permute-start.9 = (f32[56,128]{1,0:T(8,128)S(1)}, f32[56,128]{1,0:T(8,128)S(1)}, u32[]{:S(2)}, u32[]{:S(2)}) collective-permute-start(f32[56,128]{1,0:T(8,128)S(1)} %add_add_fusion.1), channel_id=1, source_target_pairs={{0,8},{8,0},{16,24},{24,16},{1,9},{9,1},{17,25},{25,17},{2,10},{10... | collective-permute-start | bytes 86024 | tf_op jit(solution)/shard_map/ppermute | solution.py:479
  33.7 1.3 %collective-permute-start.10 = (f32[56,128]{1,0:T(8,128)S(1)}, f32[56,128]{1,0:T(8,128)S(1)}, u32[]{:S(2)}, u32[]{:S(2)}) collective-permute-start(f32[56,128]{1,0:T(8,128)S(1)} %add_add_fusion.mine_ref), channel_id=1, source_target_pairs={{0,1},{1,0},{2,3},{3,2},{4,5},{5,4},{6,7},{7,6},{8,9},{9,8},{10,11... | collective-permute-start | bytes 86024 | tf_op jit(solution)/shard_map/ppermute | solution.py:479

commit v3 on v2

--- a/solution.py
+++ b/solution.py
@@ -143,6 +143,7 @@
     row = lax.broadcasted_iota(jnp.int32, (columns, depth), 0)
     zero = jnp.zeros((columns, depth), jnp.float32)
     span = depth // PARTS
+    live = jnp.where(lax.axis_index("dom") < lax.axis_size("dom") - 1, 1.0, 0.0)
 
     def along(value):
         return jnp.where(lane == 0, 0.0, pltpu.roll(value, 1, 1))
@@ -153,8 +154,10 @@
         main = entry(a, i, b, j) + along(entry(a + 1, i, b + 1, j))
         after = along(entry(a, i, b + 1, j))
         if step == other and p == q:
-            return [main * np.float32(0.5), after, zero]
-        return [main, after, jnp.where(lane == depth - 1, 0.0, entry(a + 1, i, b, j))]
+            found = [main * np.float32(0.5), after, zero]
+        else:
+            found = [main, after, jnp.where(lane == depth - 1, 0.0, entry(a + 1, i, b, j))]
+        return [value * live for value in found] if ax or bx else found
 
     def all_rows(low, high):
         return low + jnp.where(row == 0, 0.0, pltpu.roll(high, 1, 0)), high
@@ -215,7 +218,7 @@
     loads = []
     for x, d in LINES:
         parts = [f_ref[12 * x + 6 * s + d] + along(f_ref[12 * x + 6 * s + 3 + d]) for s in range(2)]
-        loads.append(all_rows(*parts))
+        loads.append(all_rows(*[part * live for part in parts] if x else parts))
     store(load_ref, 0, [loads[0:4], loads[4:6] + [None, None]])
 
     place = lax.rem(lax.broadcasted_iota(jnp.int32, (span, depth), 1), span)
@@ -328,8 +331,8 @@
 
 
 def last_kernel(
-    side_ref, corner_ref, blocks_ref, sum_in, carry_in, mine_ref, other_ref,
-    gather_ref, carry_ref, sum_ref, packed_ref, ends_ref,
+    side_ref, corner_ref, blocks_ref, sum_in, carry_in, packed_ref,
+    gather_ref, carry_ref, sum_ref, ends_ref,
 ):
     inside = lax.axis_index("sub") < lax.axis_size("sub") - 1
     ends_ref[0:1] = jnp.where(inside, side_ref[...], jnp.bfloat16(0))
@@ -345,34 +348,56 @@
     total = sum_ref[...]
     upper = total[0:modes]
     tangent = upper + upper.T
-    half, quarter, share = modes // 2, modes // 4, mine_ref.shape[0]
-    packed_ref[0:half] = tangent[0:half]
-    packed_ref[half : half + quarter] = jnp.concatenate(
-        [tangent[half : half + quarter, half:], tangent[half + quarter :, half:]], 1
+    packed_ref[...] = packed(tangent, total[modes : modes + 1] + total[modes + 1 : modes + 2])
+
+
+def rolled_rows(value, step):
+    row = lax.broadcasted_iota(jnp.int32, value.shape, 0)
+    result = value
+    for j in range(1, value.shape[0]):
+        result = jnp.where(row == j, pltpu.roll(value, j * step % value.shape[1], 1), result)
+    return result
+
+
+def packed(tangent, residual):
+    modes = tangent.shape[0]
+    size = modes // 4
+    lane = lax.broadcasted_iota(jnp.int32, (size, modes), 1)
+    first, second, third, fourth = [tangent[size * k : size * (k + 1)] for k in range(4)]
+    second = jnp.where(lane < size, pltpu.roll(fourth, size, 1), second)
+    folded = size // 2
+    third = jnp.where(
+        lane[:folded] < 2 * size, pltpu.roll(third[folded:], 2 * size, 1), third[:folded]
     )
-    packed_ref[half + quarter :] = jnp.zeros_like(packed_ref[half + quarter :])
-    packed_ref[half + quarter : half + quarter + 1] = (
-        total[modes : modes + 1] + total[modes + 1 : modes + 2]
+    count = 2 * modes // size
+    spread = rolled_rows(jnp.broadcast_to(residual, (count, modes)), modes - folded)
+    middle = jnp.where(lane[:count] < folded, spread, first[folded : folded + count])
+    return jnp.concatenate([first[:folded], middle, first[folded + count :], second, third], 0)
+
+
+def unpack_kernel(mine_ref, other_ref, tangent_ref, residual_ref, packed_ref):
+    modes = tangent_ref.shape[0]
+    size = modes // 4
+    folded = size // 2
+    count = 2 * modes // size
+    packed_ref[...] = mine_ref[...] + other_ref[...]
+    second, third = packed_ref[size : 2 * size], packed_ref[2 * size :]
+    upper = jnp.concatenate(
+        [
+            packed_ref[0 : 2 * size],
+            third,
+            pltpu.roll(third, 2 * size, 1),
+            pltpu.roll(second, modes - size, 1),
+        ],
+        0,
     )
-    core = lax.rem(lax.axis_index("dom"), 2)
-    mine_ref[...] = packed_ref[pl.ds(pl.multiple_of(core * share, 8), share)]
-    other_ref[...] = packed_ref[pl.ds(pl.multiple_of((1 - core) * share, 8), share)]
-
-
-def unpack_kernel(mine_ref, other_ref, tangent_ref, residual_ref, packed_ref):
-    share = mine_ref.shape[0]
-    modes = tangent_ref.shape[0]
-    half, quarter = modes // 2, modes // 4
-    core = lax.rem(lax.axis_index("dom"), 2)
-    packed_ref[pl.ds(pl.multiple_of(core * share, 8), share)] = mine_ref[...]
-    packed_ref[pl.ds(pl.multiple_of((1 - core) * share, 8), share)] = other_ref[...]
-    tangent_ref[0:half] = packed_ref[0:half]
-    low = packed_ref[half : half + quarter]
-    corner = packed_ref[0:half, half:].T
-    tangent_ref[half:, 0:half] = corner
-    tangent_ref[half : half + quarter, half:] = low[:, 0:half]
-    tangent_ref[half + quarter :, half:] = low[:, half:]
-    residual_ref[...] = packed_ref[half + quarter : half + quarter + 1]
+    lane = lax.broadcasted_iota(jnp.int32, (modes, modes), 1)
+    row = lax.broadcasted_iota(jnp.int32, (modes, modes), 0)
+    replaced = (row >= folded) & (row < folded + count) & (lane < folded)
+    tangent_ref[...] = jnp.where((row // size > lane // size) | replaced, upper.T, upper)
+    spread = rolled_rows(packed_ref[folded : folded + count], folded)
+    kept = lane[:count] // folded == row[:count]
+    residual_ref[...] = jnp.sum(jnp.where(kept, spread, 0.0), axis=0, keepdims=True)
 
 
 def on_device(
@@ -383,7 +408,7 @@
     plane_rows = 3 * depth
     own = reduced_basis.reshape(columns, plane_rows, modes)
     doms, subs = lax.axis_size("dom"), lax.axis_size("sub")
-    front = lax.ppermute(own, "dom", [(s, s - 1) for s in range(1, doms)])
+    front = lax.ppermute(own, "dom", [(s, (s - 1) % doms) for s in range(doms)])
     first = own[0:1]
     corner = lax.ppermute(
         first,
@@ -425,8 +450,7 @@
         compiler_params=pltpu.CompilerParams(vmem_limit_bytes=24 * 2**20),
         cost_estimate=pl.CostEstimate(flops=20_000_000, bytes_accessed=8_000_000, transcendentals=0),
     )(state)
-    packed_rows = -(-(modes // 2 + modes // 4 + 1) // 16) * 16
-    share = jax.ShapeDtypeStruct((packed_rows // 2, modes), jnp.float32)
+    packed_rows = modes * 5 // 8
     gather_scratch = pltpu.VMEM(((PARTS - 1) * 8 * TILE + TILE, modes), jnp.float32)
     sum_shape = jax.ShapeDtypeStruct((modes + TILE, modes), jnp.float32)
     carry_shape = jax.ShapeDtypeStruct((PARTS, 2, modes, depth), jnp.float32)
@@ -439,24 +463,22 @@
         compiler_params=pltpu.CompilerParams(vmem_limit_bytes=24 * 2**20),
         cost_estimate=pl.CostEstimate(flops=2_000_000_000, bytes_accessed=8_000_000, transcendentals=0),
     )(own, front, blocks)
-    mine, other = pl.pallas_call(
+    mine = pl.pallas_call(
         last_kernel,
-        out_shape=(share, share),
+        out_shape=jax.ShapeDtypeStruct((packed_rows, modes), jnp.float32),
         in_specs=[whole] * 5,
-        out_specs=(whole, whole),
+        out_specs=whole,
         scratch_shapes=[
             gather_scratch,
             pltpu.VMEM(carry_shape.shape, jnp.float32),
             pltpu.VMEM(sum_shape.shape, jnp.float32),
-            pltpu.VMEM((packed_rows, modes), jnp.float32),
             pltpu.VMEM((2, plane_rows, modes), jnp.bfloat16),
         ],
         compiler_params=pltpu.CompilerParams(vmem_limit_bytes=24 * 2**20),
         cost_estimate=pl.CostEstimate(flops=200_000_000, bytes_accessed=1_000_000, transcendentals=0),
     )(side, corner, blocks, partial, carry)
 
-    mine = mine + exchanged(other, "dom", 1)
-    for axis, first in (("dom", 2), ("sub", 1)):
+    for axis, first in (("sub", 1), ("dom", 2)):
         for stride, radix in stages(first, lax.axis_size(axis)):
             received = [exchanged(mine, axis, stride * k) for k in range(radix - 1, 0, -1)]
             mine = sum(received, mine)
@@ -480,6 +502,8 @@
 
 
 def stages(stride, size):
+    first = stride
+
     found = []
     while stride < size:
         radix = min(4, size // stride)

time: 36 us -> 33.8 us (0.939)
  starting transfers between devices: 17.5 us -> 15.6 us
    ppermute x1, starting transfers between devices: 4.07 us -> 0.35 us  [on_device(): lax.ppermute(first, ('sub', 'dom'), [(s * doms + t, (s - 1) % subs * doms...]
    ppermute x1, starting transfers between devices: 1.42 us -> 4.54 us  [on_device(): front = lax.ppermute(own, 'dom', [(s, (s - 1) % doms) for s in range(doms)])]
    ppermute x1, starting transfers between devices: 3.89 us -> 2.45 us  [on_device(): lax.ppermute(first, 'sub', [(s, (s - 1) % subs) for s in range(subs)])]
    ppermute x8 -> x7, waiting for transfers between devices: 7.86 us -> 6.61 us  [exchanged(): lax.ppermute(value, axis, [(s, s ^ distance) for s in range(lax.axis_size...]
    ppermute x1, waiting for transfers between devices: 0.01 us -> 0.92 us  [on_device(): front = lax.ppermute(own, 'dom', [(s, (s - 1) % doms) for s in range(doms)])]
    ppermute x8 -> x7, starting transfers between devices: 8.08 us -> 8.23 us  [exchanged(): lax.ppermute(value, axis, [(s, s ^ distance) for s in range(lax.axis_size...]
  transfers between devices with their start and end apart: 11 -> 10, of which waited for: 8 -> 7; matrix products, arithmetic and copies ran while one was open for 5% -> 6% of each run, Pallas kernels for 18% -> 19%
where the time goes in v3:
time: 33.8 us; the launch traced here: 33.6 us
  starting transfers between devices  15.6 us (46%)
  Pallas kernels  7.81 us (23%)
  waiting for transfers between devices  7.54 us (22%)
  other arithmetic  1.05 us (3%)
  local copies, waits for them, and re-layouts  0.94 us (3%)
  between operations  0.68 us (2%)
    ppermute x7, starting transfers between devices, exchanged(): lax.ppermute(value, axis, [(s, s ^ distance) for s in range(lax.axis_size...  8.23 us
    ppermute x7, waiting for transfers between devices, exchanged(): lax.ppermute(value, axis, [(s, s ^ distance) for s in range(lax.axis_size...  6.61 us
    ppermute x1, starting transfers between devices, on_device(): front = lax.ppermute(own, 'dom', [(s, (s - 1) % doms) for s in range(doms)])  4.54 us
    pallas_call x1, Pallas kernels, on_device(): pl.pallas_call(stiffness_kernel, out_shape=jax.ShapeDtypeStruct(blocks_sh...  4.14 us
    ppermute x1, starting transfers between devices, on_device(): lax.ppermute(first, 'sub', [(s, (s - 1) % subs) for s in range(subs)])  2.45 us
    pallas_call x1, Pallas kernels, on_device(): pl.pallas_call(contraction_kernel, out_shape=(sum_shape, carry_shape), in...  2.21 us
    add x1, other arithmetic, on_device(): state + jnp.pad(value, ((at, count - end), (0, 0), (0, 0))).astype(jnp.fl...  1.02 us
    slice x1, local copies, waits for them, and re-layouts, on_device(): first = own[0:1]  0.93 us
  transfers between devices with their start and end apart: 10, of which 7 were waited for; matrix products, arithmetic and copies ran while one was open for 6% of the time, Pallas kernels for 19%

profile of v3, /device:TPU:0, one launch (start us, length us, event | category | flops | bytes accessed | tf_op | source)
XLA Modules:
  0.0 33.6 jit_solution(3231443841039618661)
XLA Ops:
  0.6 0.0 copy-start
  0.6 4.5 %collective-permute-start.2 = (bf16[8,384,128]{2,1,0:T(8,128)(2,1)}, bf16[8,384,128]{2,1,0:T(8,128)(2,1)S(1)}, u32[]{:S(2)}, u32[]{:S(2)}) collective-permute-start(bf16[8,384,128]{2,1,0:T(8,128)(2,1)} %bitcast.8), channel_id=1, source_target_pairs={{0,7},{1,0},{2,1},{3,2},{4,3},{5,4},{6,5},{7,6},{8,15},{9,8},{10,9... | collective-permute-start | bytes 2359304 | tf_op jit(solution)/shard_map/ppermute | solution.py:411
  5.2 0.9 %slice.6 = bf16[1,1,3,128,128]{4,3,2,1,0:T(8,128)(2,1)S(1)} slice(bf16[1,8,3,128,128]{4,3,2,1,0:T(8,128)(2,1)} %param.6), slice={[0:1], [0:1], [0:3], [0:128], [0:128]} | slice | bytes 196608 | tf_op jit(solution)/shard_map/slice | solution.py:412
  6.1 2.4 %collective-permute-start = (bf16[1,384,128]{2,1,0:T(8,128)(2,1)S(1)}, bf16[1,384,128]{2,1,0:T(8,128)(2,1)S(1)}, u32[]{:S(2)}, u32[]{:S(2)}) collective-permute-start(bf16[1,384,128]{2,1,0:T(8,128)(2,1)S(1)} %bitcast.11), channel_id=1, source_target_pairs={{0,24},{8,0},{16,8},{24,16},{1,25},{9,1},{17,9},{25,17},{2,26},{10... | collective-permute-start | bytes 294920 | tf_op jit(solution)/shard_map/ppermute | solution.py:422
  8.6 0.3 %collective-permute-start.1 = (bf16[1,384,128]{2,1,0:T(8,128)(2,1)S(1)}, bf16[1,384,128]{2,1,0:T(8,128)(2,1)S(1)}, u32[]{:S(2)}, u32[]{:S(2)}) collective-permute-start(bf16[1,384,128]{2,1,0:T(8,128)(2,1)S(1)} %bitcast.12), channel_id=1, source_target_pairs={{0,31},{1,24},{2,25},{3,26},{4,27},{5,28},{6,29},{7,30},{8,7},{9,0... | collective-permute-start | bytes 294920 | tf_op jit(solution)/shard_map/ppermute | solution.py:413
  8.9 1.0 %pad_add_fusion.state_ref = f32[69,8,128]{2,1,0:T(8,128)S(1)} fusion(f32[3,8,128]{2,1,0:T(8,128)} %bitcast.15, f32[2,8,128]{2,1,0:T(8,128)} %bitcast.16, f32[8,8,128]{2,1,0:T(8,128)} %bitcast.13, s32[8,8,128]{2,1,0:T(8,128)} %bitcast.14, f32[48,8,128]{2,1,0:T(8,128)} %bitcast.10), kind=kLoop, calls=%fused_computation | loop fusion | flops 353280 | bytes 565248 | tf_op jit(solution)/shard_map/add | solution.py:434
  9.9 4.1 %shard_map.77.blocks_ref = bf16[36,224,384]{2,1,0:T(8,128)(2,1)S(1)} custom-call(f32[69,8,128]{2,1,0:T(8,128)S(1)} %pad_add_fusion.state_ref), custom_call_target="tpu_custom_call" | custom-call | flops 20000000 | bytes 8000000 | tf_op jit(solution)/shard_map/pallas_call | solution.py:437
  14.1 0.9 %collective-permute-done.2.front_ref = bf16[8,384,128]{2,1,0:T(8,128)(2,1)S(1)} collective-permute-done((bf16[8,384,128]{2,1,0:T(8,128)(2,1)}, bf16[8,384,128]{2,1,0:T(8,128)(2,1)S(1)}, u32[]{:S(2)}, u32[]{:S(2)}) %collective-permute-start.2) | collective-permute-done | bytes 786464 | tf_op jit(solution)/shard_map/ppermute | solution.py:411
  15.0 0.0 copy-done
  15.0 2.2 %shard_map.78 = (f32[144,128]{1,0:T(8,128)S(1)}, f32[4,2,128,128]{3,2,1,0:T(8,128)S(1)}) custom-call(bf16[8,384,128]{2,1,0:T(8,128)(2,1)S(1)} %bitcast.9, bf16[8,384,128]{2,1,0:T(8,128)(2,1)S(1)} %collective-permute-done.2.front_ref, bf16[36,224,384]{2,1,0:T(8,128)(2,1)S(1)} %shard_map.77.blocks_ref), custom_call_target="tpu_custom_call" | custom-call | flops 2000000000 | bytes 8000000 | tf_op jit(solution)/shard_map/pallas_call | solution.py:457
  17.2 0.0 collective-permute-done.side_ref
  17.2 0.0 collective-permute-done.1.corner_ref
  17.2 0.7 %shard_map.79 = f32[80,128]{1,0:T(8,128)S(1)} custom-call(bf16[1,384,128]{2,1,0:T(8,128)(2,1)S(1)} %collective-permute-done.side_ref, bf16[1,384,128]{2,1,0:T(8,128)(2,1)S(1)} %collective-permute-done.1.corner_ref, bf16[36,224,384]{2,1,0:T(8,128)(2,1)S(1)} %shard_map.77.blocks_ref, f32[144,128]{1,0:T(8,128)S(1)} %get-tuple-element.6.sum_in, ...), custom_call_target="tpu_custom_call" | custom-call | flops 200000000 | bytes 1000000 | tf_op jit(solution)/shard_map/pallas_call | solution.py:466
  17.9 2.5 %collective-permute-start.3 = (f32[80,128]{1,0:T(8,128)S(1)}, f32[80,128]{1,0:T(8,128)S(1)}, u32[]{:S(2)}, u32[]{:S(2)}) collective-permute-start(f32[80,128]{1,0:T(8,128)S(1)} %shard_map.79), channel_id=1, source_target_pairs={{0,24},{8,16},{16,8},{24,0},{1,25},{9,17},{17,9},{25,1},{2,26},{10... | collective-permute-start | bytes 122888 | tf_op jit(solution)/shard_map/ppermute | solution.py:501
  20.4 0.5 %collective-permute-start.4 = (f32[80,128]{1,0:T(8,128)S(1)}, f32[80,128]{1,0:T(8,128)S(1)}, u32[]{:S(2)}, u32[]{:S(2)}) collective-permute-start(f32[80,128]{1,0:T(8,128)S(1)} %shard_map.79), channel_id=1, source_target_pairs={{0,16},{8,24},{16,0},{24,8},{1,17},{9,25},{17,1},{25,9},{2,18},{10... | collective-permute-start | bytes 122888 | tf_op jit(solution)/shard_map/ppermute | solution.py:501
  20.9 0.5 %collective-permute-start.5 = (f32[80,128]{1,0:T(8,128)S(1)}, f32[80,128]{1,0:T(8,128)S(1)}, u32[]{:S(2)}, u32[]{:S(2)}) collective-permute-start(f32[80,128]{1,0:T(8,128)S(1)} %shard_map.79), channel_id=1, source_target_pairs={{0,8},{8,0},{16,24},{24,16},{1,9},{9,1},{17,25},{25,17},{2,10},{10... | collective-permute-start | bytes 122888 | tf_op jit(solution)/shard_map/ppermute | solution.py:501
  21.5 1.6 %collective-permute-done.3 = f32[80,128]{1,0:T(8,128)S(1)} collective-permute-done((f32[80,128]{1,0:T(8,128)S(1)}, f32[80,128]{1,0:T(8,128)S(1)}, u32[]{:S(2)}, u32[]{:S(2)}) %collective-permute-start.3) | collective-permute-done | bytes 40992 | tf_op jit(solution)/shard_map/ppermute | solution.py:501
  23.1 1.3 %collective-permute-done.4 = f32[80,128]{1,0:T(8,128)S(1)} collective-permute-done((f32[80,128]{1,0:T(8,128)S(1)}, f32[80,128]{1,0:T(8,128)S(1)}, u32[]{:S(2)}, u32[]{:S(2)}) %collective-permute-start.4) | collective-permute-done | bytes 40992 | tf_op jit(solution)/shard_map/ppermute | solution.py:501
  24.4 0.5 %collective-permute-done.5 = f32[80,128]{1,0:T(8,128)S(1)} collective-permute-done((f32[80,128]{1,0:T(8,128)S(1)}, f32[80,128]{1,0:T(8,128)S(1)}, u32[]{:S(2)}, u32[]{:S(2)}) %collective-permute-start.5) | collective-permute-done | bytes 40992 | tf_op jit(solution)/shard_map/ppermute | solution.py:501
  25.0 0.6 %collective-permute-start.6 = (f32[80,128]{1,0:T(8,128)S(1)}, f32[80,128]{1,0:T(8,128)S(1)}, u32[]{:S(2)}, u32[]{:S(2)}) collective-permute-start(f32[80,128]{1,0:T(8,128)S(1)} %add_add_fusion.1), channel_id=1, source_target_pairs={{0,6},{1,7},{2,4},{3,5},{4,2},{5,3},{6,0},{7,1},{8,14},{9,15},{10,... | collective-permute-start | bytes 122888 | tf_op jit(solution)/shard_map/ppermute | solution.py:501
  25.6 0.0 collective-permute-start.7
  25.6 3.8 %collective-permute-start.8 = (f32[80,128]{1,0:T(8,128)S(1)}, f32[80,128]{1,0:T(8,128)S(1)}, u32[]{:S(2)}, u32[]{:S(2)}) collective-permute-start(f32[80,128]{1,0:T(8,128)S(1)} %add_add_fusion.1), channel_id=1, source_target_pairs={{0,2},{1,3},{2,0},{3,1},{4,6},{5,7},{6,4},{7,5},{8,10},{9,11},{10,... | collective-permute-start | bytes 122888 | tf_op jit(solution)/shard_map/ppermute | solution.py:501
  29.4 1.5 %collective-permute-done.6 = f32[80,128]{1,0:T(8,128)S(1)} collective-permute-done((f32[80,128]{1,0:T(8,128)S(1)}, f32[80,128]{1,0:T(8,128)S(1)}, u32[]{:S(2)}, u32[]{:S(2)}) %collective-permute-start.6) | collective-permute-done | bytes 40992 | tf_op jit(solution)/shard_map/ppermute | solution.py:501
  30.9 0.6 %collective-permute-done.7 = f32[80,128]{1,0:T(8,128)S(1)} collective-permute-done((f32[80,128]{1,0:T(8,128)S(1)}, f32[80,128]{1,0:T(8,128)S(1)}, u32[]{:S(2)}, u32[]{:S(2)}) %collective-permute-start.7) | collective-permute-done | bytes 40992 | tf_op jit(solution)/shard_map/ppermute | solution.py:501
  31.5 0.0 collective-permute-done.8
  31.5 0.2 collective-permute-start.9
  31.7 1.1 %collective-permute-done.9.other_ref = f32[80,128]{1,0:T(8,128)S(1)} collective-permute-done((f32[80,128]{1,0:T(8,128)S(1)}, f32[80,128]{1,0:T(8,128)S(1)}, u32[]{:S(2)}, u32[]{:S(2)}) %collective-permute-start.9) | collective-permute-done | bytes 40992 | tf_op jit(solution)/shard_map/ppermute | solution.py:501
  32.8 0.8 %shard_map.80 = (f32[128,128]{1,0:T(8,128)}, f32[1,128]{1,0:T(1,128)}) custom-call(f32[80,128]{1,0:T(8,128)S(1)} %add_add_fusion.mine_ref, f32[80,128]{1,0:T(8,128)S(1)} %collective-permute-done.9.other_ref), custom_call_target="tpu_custom_call" | custom-call | tf_op jit(solution)/shard_map/pallas_call | solution.py:486
  (2 shorter events, 0.0 us)
Async XLA Ops:
  0.6 14.4 %copy-start = (bf16[1,8,3,128,128]{4,3,2,1,0:T(8,128)(2,1)S(1)}, bf16[1,8,3,128,128]{4,3,2,1,0:T(8,128)(2,1)}, u32[]{:S(2)}) copy-start(bf16[1,8,3,128,128]{4,3,2,1,0:T(8,128)(2,1)} %param.6) | copy-start | bytes 2359300
  0.6 14.4 %collective-permute-start.2 = (bf16[8,384,128]{2,1,0:T(8,128)(2,1)}, bf16[8,384,128]{2,1,0:T(8,128)(2,1)S(1)}, u32[]{:S(2)}, u32[]{:S(2)}) collective-permute-start(bf16[8,384,128]{2,1,0:T(8,128)(2,1)} %bitcast.8), channel_id=1, source_target_pairs={{0,7},{1,0},{2,1},{3,2},{4,3},{5,4},{6,5},{7,6},{8,15},{9,8},{10,9... | collective-permute-start | bytes 2359304 | tf_op jit(solution)/shard_map/ppermute | solution.py:411
  6.1 11.1 %collective-permute-start = (bf16[1,384,128]{2,1,0:T(8,128)(2,1)S(1)}, bf16[1,384,128]{2,1,0:T(8,128)(2,1)S(1)}, u32[]{:S(2)}, u32[]{:S(2)}) collective-permute-start(bf16[1,384,128]{2,1,0:T(8,128)(2,1)S(1)} %bitcast.11), channel_id=1, source_target_pairs={{0,24},{8,0},{16,8},{24,16},{1,25},{9,1},{17,9},{25,17},{2,26},{10... | collective-permute-start | bytes 294920 | tf_op jit(solution)/shard_map/ppermute | solution.py:422
  8.6 8.7 %collective-permute-start.1 = (bf16[1,384,128]{2,1,0:T(8,128)(2,1)S(1)}, bf16[1,384,128]{2,1,0:T(8,128)(2,1)S(1)}, u32[]{:S(2)}, u32[]{:S(2)}) collective-permute-start(bf16[1,384,128]{2,1,0:T(8,128)(2,1)S(1)} %bitcast.12), channel_id=1, source_target_pairs={{0,31},{1,24},{2,25},{3,26},{4,27},{5,28},{6,29},{7,30},{8,7},{9,0... | collective-permute-start | bytes 294920 | tf_op jit(solution)/shard_map/ppermute | solution.py:413
  17.9 5.2 %collective-permute-start.3 = (f32[80,128]{1,0:T(8,128)S(1)}, f32[80,128]{1,0:T(8,128)S(1)}, u32[]{:S(2)}, u32[]{:S(2)}) collective-permute-start(f32[80,128]{1,0:T(8,128)S(1)} %shard_map.79), channel_id=1, source_target_pairs={{0,24},{8,16},{16,8},{24,0},{1,25},{9,17},{17,9},{25,1},{2,26},{10... | collective-permute-start | bytes 122888 | tf_op jit(solution)/shard_map/ppermute | solution.py:501
  20.4 4.0 %collective-permute-start.4 = (f32[80,128]{1,0:T(8,128)S(1)}, f32[80,128]{1,0:T(8,128)S(1)}, u32[]{:S(2)}, u32[]{:S(2)}) collective-permute-start(f32[80,128]{1,0:T(8,128)S(1)} %shard_map.79), channel_id=1, source_target_pairs={{0,16},{8,24},{16,0},{24,8},{1,17},{9,25},{17,1},{25,9},{2,18},{10... | collective-permute-start | bytes 122888 | tf_op jit(solution)/shard_map/ppermute | solution.py:501
  20.9 4.0 %collective-permute-start.5 = (f32[80,128]{1,0:T(8,128)S(1)}, f32[80,128]{1,0:T(8,128)S(1)}, u32[]{:S(2)}, u32[]{:S(2)}) collective-permute-start(f32[80,128]{1,0:T(8,128)S(1)} %shard_map.79), channel_id=1, source_target_pairs={{0,8},{8,0},{16,24},{24,16},{1,9},{9,1},{17,25},{25,17},{2,10},{10... | collective-permute-start | bytes 122888 | tf_op jit(solution)/shard_map/ppermute | solution.py:501
  25.0 6.0 %collective-permute-start.6 = (f32[80,128]{1,0:T(8,128)S(1)}, f32[80,128]{1,0:T(8,128)S(1)}, u32[]{:S(2)}, u32[]{:S(2)}) collective-permute-start(f32[80,128]{1,0:T(8,128)S(1)} %add_add_fusion.1), channel_id=1, source_target_pairs={{0,6},{1,7},{2,4},{3,5},{4,2},{5,3},{6,0},{7,1},{8,14},{9,15},{10,... | collective-permute-start | bytes 122888 | tf_op jit(solution)/shard_map/ppermute | solution.py:501
  25.6 5.9 %collective-permute-start.7 = (f32[80,128]{1,0:T(8,128)S(1)}, f32[80,128]{1,0:T(8,128)S(1)}, u32[]{:S(2)}, u32[]{:S(2)}) collective-permute-start(f32[80,128]{1,0:T(8,128)S(1)} %add_add_fusion.1), channel_id=1, source_target_pairs={{0,4},{1,5},{2,6},{3,7},{4,0},{5,1},{6,2},{7,3},{8,12},{9,13},{10,... | collective-permute-start | bytes 122888 | tf_op jit(solution)/shard_map/ppermute | solution.py:501
  25.6 5.9 %collective-permute-start.8 = (f32[80,128]{1,0:T(8,128)S(1)}, f32[80,128]{1,0:T(8,128)S(1)}, u32[]{:S(2)}, u32[]{:S(2)}) collective-permute-start(f32[80,128]{1,0:T(8,128)S(1)} %add_add_fusion.1), channel_id=1, source_target_pairs={{0,2},{1,3},{2,0},{3,1},{4,6},{5,7},{6,4},{7,5},{8,10},{9,11},{10,... | collective-permute-start | bytes 122888 | tf_op jit(solution)/shard_map/ppermute | solution.py:501
  31.5 1.3 %collective-permute-start.9 = (f32[80,128]{1,0:T(8,128)S(1)}, f32[80,128]{1,0:T(8,128)S(1)}, u32[]{:S(2)}, u32[]{:S(2)}) collective-permute-start(f32[80,128]{1,0:T(8,128)S(1)} %add_add_fusion.mine_ref), channel_id=1, source_target_pairs={{0,1},{1,0},{2,3},{3,2},{4,5},{5,4},{6,7},{7,6},{8,9},{9,8},{10,11... | collective-permute-start | bytes 122888 | tf_op jit(solution)/shard_map/ppermute | solution.py:501

commit v4 on v3

--- a/solution.py
+++ b/solution.py
@@ -20,6 +20,7 @@
 ]
 TILE = 16
 PARTS = 4
+ORDERS = {2: (1,), 4: (2, 3, 1)}
 
 
 def corner_bits(corner):
@@ -480,7 +481,7 @@
 
     for axis, first in (("sub", 1), ("dom", 2)):
         for stride, radix in stages(first, lax.axis_size(axis)):
-            received = [exchanged(mine, axis, stride * k) for k in range(radix - 1, 0, -1)]
+            received = [exchanged(mine, axis, stride * k) for k in ORDERS[radix]]
             mine = sum(received, mine)
     other = exchanged(mine, "dom", 1)
     tangent, residual = pl.pallas_call(

time: 33.8 us -> 33.6 us (level)
  starting transfers between devices: 15.6 us -> 14.5 us
  waiting for transfers between devices: 7.54 us -> 8.37 us
    ppermute x7, starting transfers between devices: 8.23 us -> 7.17 us  [exchanged(): lax.ppermute(value, axis, [(s, s ^ distance) for s in range(lax.axis_size...]
    ppermute x7, waiting for transfers between devices: 6.61 us -> 7.44 us  [exchanged(): lax.ppermute(value, axis, [(s, s ^ distance) for s in range(lax.axis_size...]
  transfers between devices with their start and end apart: 10 -> 10, of which waited for: 7 -> 8; matrix products, arithmetic and copies ran while one was open for 6% -> 6% of each run, Pallas kernels for 19% -> 19%
where the time goes in v4:
time: 33.6 us; the launch traced here: 33.4 us
  starting transfers between devices  14.5 us (43%)
  waiting for transfers between devices  8.37 us (25%)
  Pallas kernels  7.81 us (23%)
  other arithmetic  1.05 us (3%)
  local copies, waits for them, and re-layouts  0.94 us (3%)
  between operations  0.7 us (2%)
    ppermute x7, waiting for transfers between devices, exchanged(): lax.ppermute(value, axis, [(s, s ^ distance) for s in range(lax.axis_size...  7.44 us
    ppermute x7, starting transfers between devices, exchanged(): lax.ppermute(value, axis, [(s, s ^ distance) for s in range(lax.axis_size...  7.17 us
    ppermute x1, starting transfers between devices, on_device(): front = lax.ppermute(own, 'dom', [(s, (s - 1) % doms) for s in range(doms)])  4.54 us
    pallas_call x1, Pallas kernels, on_device(): pl.pallas_call(stiffness_kernel, out_shape=jax.ShapeDtypeStruct(blocks_sh...  4.14 us
    ppermute x1, starting transfers between devices, on_device(): lax.ppermute(first, 'sub', [(s, (s - 1) % subs) for s in range(subs)])  2.45 us
    pallas_call x1, Pallas kernels, on_device(): pl.pallas_call(contraction_kernel, out_shape=(sum_shape, carry_shape), in...  2.21 us
    add x1, other arithmetic, on_device(): state + jnp.pad(value, ((at, count - end), (0, 0), (0, 0))).astype(jnp.fl...  1.02 us
    slice x1, local copies, waits for them, and re-layouts, on_device(): first = own[0:1]  0.93 us
  transfers between devices with their start and end apart: 10, of which 8 were waited for; matrix products, arithmetic and copies ran while one was open for 6% of the time, Pallas kernels for 19%

profile of v4, /device:TPU:0, one launch (start us, length us, event | category | flops | bytes accessed | tf_op | source)
XLA Modules:
  0.0 33.4 jit_solution(16968589998553839918)
XLA Ops:
  0.6 0.0 copy-start
  0.6 4.5 %collective-permute-start.2 = (bf16[8,384,128]{2,1,0:T(8,128)(2,1)}, bf16[8,384,128]{2,1,0:T(8,128)(2,1)S(1)}, u32[]{:S(2)}, u32[]{:S(2)}) collective-permute-start(bf16[8,384,128]{2,1,0:T(8,128)(2,1)} %bitcast.8), channel_id=1, source_target_pairs={{0,7},{1,0},{2,1},{3,2},{4,3},{5,4},{6,5},{7,6},{8,15},{9,8},{10,9... | collective-permute-start | bytes 2359304 | tf_op jit(solution)/shard_map/ppermute | solution.py:412
  5.2 0.9 %slice.6 = bf16[1,1,3,128,128]{4,3,2,1,0:T(8,128)(2,1)S(1)} slice(bf16[1,8,3,128,128]{4,3,2,1,0:T(8,128)(2,1)} %param.6), slice={[0:1], [0:1], [0:3], [0:128], [0:128]} | slice | bytes 196608 | tf_op jit(solution)/shard_map/slice | solution.py:413
  6.1 2.4 %collective-permute-start = (bf16[1,384,128]{2,1,0:T(8,128)(2,1)S(1)}, bf16[1,384,128]{2,1,0:T(8,128)(2,1)S(1)}, u32[]{:S(2)}, u32[]{:S(2)}) collective-permute-start(bf16[1,384,128]{2,1,0:T(8,128)(2,1)S(1)} %bitcast.11), channel_id=1, source_target_pairs={{0,24},{8,0},{16,8},{24,16},{1,25},{9,1},{17,9},{25,17},{2,26},{10... | collective-permute-start | bytes 294920 | tf_op jit(solution)/shard_map/ppermute | solution.py:423
  8.6 0.3 %collective-permute-start.1 = (bf16[1,384,128]{2,1,0:T(8,128)(2,1)S(1)}, bf16[1,384,128]{2,1,0:T(8,128)(2,1)S(1)}, u32[]{:S(2)}, u32[]{:S(2)}) collective-permute-start(bf16[1,384,128]{2,1,0:T(8,128)(2,1)S(1)} %bitcast.12), channel_id=1, source_target_pairs={{0,31},{1,24},{2,25},{3,26},{4,27},{5,28},{6,29},{7,30},{8,7},{9,0... | collective-permute-start | bytes 294920 | tf_op jit(solution)/shard_map/ppermute | solution.py:414
  8.9 1.0 %pad_add_fusion.state_ref = f32[69,8,128]{2,1,0:T(8,128)S(1)} fusion(f32[3,8,128]{2,1,0:T(8,128)} %bitcast.15, f32[2,8,128]{2,1,0:T(8,128)} %bitcast.16, f32[8,8,128]{2,1,0:T(8,128)} %bitcast.13, s32[8,8,128]{2,1,0:T(8,128)} %bitcast.14, f32[48,8,128]{2,1,0:T(8,128)} %bitcast.10), kind=kLoop, calls=%fused_computation | loop fusion | flops 353280 | bytes 565248 | tf_op jit(solution)/shard_map/add | solution.py:435
  9.9 4.1 %shard_map.77.blocks_ref = bf16[36,224,384]{2,1,0:T(8,128)(2,1)S(1)} custom-call(f32[69,8,128]{2,1,0:T(8,128)S(1)} %pad_add_fusion.state_ref), custom_call_target="tpu_custom_call" | custom-call | flops 20000000 | bytes 8000000 | tf_op jit(solution)/shard_map/pallas_call | solution.py:438
  14.1 0.9 %collective-permute-done.2.front_ref = bf16[8,384,128]{2,1,0:T(8,128)(2,1)S(1)} collective-permute-done((bf16[8,384,128]{2,1,0:T(8,128)(2,1)}, bf16[8,384,128]{2,1,0:T(8,128)(2,1)S(1)}, u32[]{:S(2)}, u32[]{:S(2)}) %collective-permute-start.2) | collective-permute-done | bytes 786464 | tf_op jit(solution)/shard_map/ppermute | solution.py:412
  15.0 0.0 copy-done
  15.0 2.2 %shard_map.78 = (f32[144,128]{1,0:T(8,128)S(1)}, f32[4,2,128,128]{3,2,1,0:T(8,128)S(1)}) custom-call(bf16[8,384,128]{2,1,0:T(8,128)(2,1)S(1)} %bitcast.9, bf16[8,384,128]{2,1,0:T(8,128)(2,1)S(1)} %collective-permute-done.2.front_ref, bf16[36,224,384]{2,1,0:T(8,128)(2,1)S(1)} %shard_map.77.blocks_ref), custom_call_target="tpu_custom_call" | custom-call | flops 2000000000 | bytes 8000000 | tf_op jit(solution)/shard_map/pallas_call | solution.py:458
  17.2 0.0 collective-permute-done.side_ref
  17.2 0.0 collective-permute-done.1.corner_ref
  17.2 0.7 %shard_map.79 = f32[80,128]{1,0:T(8,128)S(1)} custom-call(bf16[1,384,128]{2,1,0:T(8,128)(2,1)S(1)} %collective-permute-done.side_ref, bf16[1,384,128]{2,1,0:T(8,128)(2,1)S(1)} %collective-permute-done.1.corner_ref, bf16[36,224,384]{2,1,0:T(8,128)(2,1)S(1)} %shard_map.77.blocks_ref, f32[144,128]{1,0:T(8,128)S(1)} %get-tuple-element.6.sum_in, ...), custom_call_target="tpu_custom_call" | custom-call | flops 200000000 | bytes 1000000 | tf_op jit(solution)/shard_map/pallas_call | solution.py:467
  17.9 1.6 %collective-permute-start.3 = (f32[80,128]{1,0:T(8,128)S(1)}, f32[80,128]{1,0:T(8,128)S(1)}, u32[]{:S(2)}, u32[]{:S(2)}) collective-permute-start(f32[80,128]{1,0:T(8,128)S(1)} %shard_map.79), channel_id=1, source_target_pairs={{0,16},{8,24},{16,0},{24,8},{1,17},{9,25},{17,1},{25,9},{2,18},{10... | collective-permute-start | bytes 122888 | tf_op jit(solution)/shard_map/ppermute | solution.py:502
  19.5 1.4 %collective-permute-start.4 = (f32[80,128]{1,0:T(8,128)S(1)}, f32[80,128]{1,0:T(8,128)S(1)}, u32[]{:S(2)}, u32[]{:S(2)}) collective-permute-start(f32[80,128]{1,0:T(8,128)S(1)} %shard_map.79), channel_id=1, source_target_pairs={{0,24},{8,16},{16,8},{24,0},{1,25},{9,17},{17,9},{25,1},{2,26},{10... | collective-permute-start | bytes 122888 | tf_op jit(solution)/shard_map/ppermute | solution.py:502
  20.9 0.5 %collective-permute-start.5 = (f32[80,128]{1,0:T(8,128)S(1)}, f32[80,128]{1,0:T(8,128)S(1)}, u32[]{:S(2)}, u32[]{:S(2)}) collective-permute-start(f32[80,128]{1,0:T(8,128)S(1)} %shard_map.79), channel_id=1, source_target_pairs={{0,8},{8,0},{16,24},{24,16},{1,9},{9,1},{17,25},{25,17},{2,10},{10... | collective-permute-start | bytes 122888 | tf_op jit(solution)/shard_map/ppermute | solution.py:502
  21.5 0.8 %collective-permute-done.3 = f32[80,128]{1,0:T(8,128)S(1)} collective-permute-done((f32[80,128]{1,0:T(8,128)S(1)}, f32[80,128]{1,0:T(8,128)S(1)}, u32[]{:S(2)}, u32[]{:S(2)}) %collective-permute-start.3) | collective-permute-done | bytes 40992 | tf_op jit(solution)/shard_map/ppermute | solution.py:502
  22.3 2.1 %collective-permute-done.4 = f32[80,128]{1,0:T(8,128)S(1)} collective-permute-done((f32[80,128]{1,0:T(8,128)S(1)}, f32[80,128]{1,0:T(8,128)S(1)}, u32[]{:S(2)}, u32[]{:S(2)}) %collective-permute-start.4) | collective-permute-done | bytes 40992 | tf_op jit(solution)/shard_map/ppermute | solution.py:502
  24.4 0.5 %collective-permute-done.5 = f32[80,128]{1,0:T(8,128)S(1)} collective-permute-done((f32[80,128]{1,0:T(8,128)S(1)}, f32[80,128]{1,0:T(8,128)S(1)}, u32[]{:S(2)}, u32[]{:S(2)}) %collective-permute-start.5) | collective-permute-done | bytes 40992 | tf_op jit(solution)/shard_map/ppermute | solution.py:502
  25.0 0.1 collective-permute-start.6
  25.0 1.1 %collective-permute-start.7 = (f32[80,128]{1,0:T(8,128)S(1)}, f32[80,128]{1,0:T(8,128)S(1)}, u32[]{:S(2)}, u32[]{:S(2)}) collective-permute-start(f32[80,128]{1,0:T(8,128)S(1)} %add_add_fusion.1), channel_id=1, source_target_pairs={{0,6},{1,7},{2,4},{3,5},{4,2},{5,3},{6,0},{7,1},{8,14},{9,15},{10,... | collective-permute-start | bytes 122888 | tf_op jit(solution)/shard_map/ppermute | solution.py:502
  26.2 2.4 %collective-permute-start.8 = (f32[80,128]{1,0:T(8,128)S(1)}, f32[80,128]{1,0:T(8,128)S(1)}, u32[]{:S(2)}, u32[]{:S(2)}) collective-permute-start(f32[80,128]{1,0:T(8,128)S(1)} %add_add_fusion.1), channel_id=1, source_target_pairs={{0,2},{1,3},{2,0},{3,1},{4,6},{5,7},{6,4},{7,5},{8,10},{9,11},{10,... | collective-permute-start | bytes 122888 | tf_op jit(solution)/shard_map/ppermute | solution.py:502
  28.5 1.7 %collective-permute-done.6 = f32[80,128]{1,0:T(8,128)S(1)} collective-permute-done((f32[80,128]{1,0:T(8,128)S(1)}, f32[80,128]{1,0:T(8,128)S(1)}, u32[]{:S(2)}, u32[]{:S(2)}) %collective-permute-start.6) | collective-permute-done | bytes 40992 | tf_op jit(solution)/shard_map/ppermute | solution.py:502
  30.2 0.8 %collective-permute-done.7 = f32[80,128]{1,0:T(8,128)S(1)} collective-permute-done((f32[80,128]{1,0:T(8,128)S(1)}, f32[80,128]{1,0:T(8,128)S(1)}, u32[]{:S(2)}, u32[]{:S(2)}) %collective-permute-start.7) | collective-permute-done | bytes 40992 | tf_op jit(solution)/shard_map/ppermute | solution.py:502
  31.0 0.2 collective-permute-done.8
  31.3 0.1 collective-permute-start.9
  31.4 1.2 %collective-permute-done.9.other_ref = f32[80,128]{1,0:T(8,128)S(1)} collective-permute-done((f32[80,128]{1,0:T(8,128)S(1)}, f32[80,128]{1,0:T(8,128)S(1)}, u32[]{:S(2)}, u32[]{:S(2)}) %collective-permute-start.9) | collective-permute-done | bytes 40992 | tf_op jit(solution)/shard_map/ppermute | solution.py:502
  32.6 0.8 %shard_map.80 = (f32[128,128]{1,0:T(8,128)}, f32[1,128]{1,0:T(1,128)}) custom-call(f32[80,128]{1,0:T(8,128)S(1)} %add_add_fusion.mine_ref, f32[80,128]{1,0:T(8,128)S(1)} %collective-permute-done.9.other_ref), custom_call_target="tpu_custom_call" | custom-call | tf_op jit(solution)/shard_map/pallas_call | solution.py:487
  (2 shorter events, 0.0 us)
Async XLA Ops:
  0.6 14.4 %copy-start = (bf16[1,8,3,128,128]{4,3,2,1,0:T(8,128)(2,1)S(1)}, bf16[1,8,3,128,128]{4,3,2,1,0:T(8,128)(2,1)}, u32[]{:S(2)}) copy-start(bf16[1,8,3,128,128]{4,3,2,1,0:T(8,128)(2,1)} %param.6) | copy-start | bytes 2359300
  0.6 14.4 %collective-permute-start.2 = (bf16[8,384,128]{2,1,0:T(8,128)(2,1)}, bf16[8,384,128]{2,1,0:T(8,128)(2,1)S(1)}, u32[]{:S(2)}, u32[]{:S(2)}) collective-permute-start(bf16[8,384,128]{2,1,0:T(8,128)(2,1)} %bitcast.8), channel_id=1, source_target_pairs={{0,7},{1,0},{2,1},{3,2},{4,3},{5,4},{6,5},{7,6},{8,15},{9,8},{10,9... | collective-permute-start | bytes 2359304 | tf_op jit(solution)/shard_map/ppermute | solution.py:412
  6.1 11.1 %collective-permute-start = (bf16[1,384,128]{2,1,0:T(8,128)(2,1)S(1)}, bf16[1,384,128]{2,1,0:T(8,128)(2,1)S(1)}, u32[]{:S(2)}, u32[]{:S(2)}) collective-permute-start(bf16[1,384,128]{2,1,0:T(8,128)(2,1)S(1)} %bitcast.11), channel_id=1, source_target_pairs={{0,24},{8,0},{16,8},{24,16},{1,25},{9,1},{17,9},{25,17},{2,26},{10... | collective-permute-start | bytes 294920 | tf_op jit(solution)/shard_map/ppermute | solution.py:423
  8.6 8.7 %collective-permute-start.1 = (bf16[1,384,128]{2,1,0:T(8,128)(2,1)S(1)}, bf16[1,384,128]{2,1,0:T(8,128)(2,1)S(1)}, u32[]{:S(2)}, u32[]{:S(2)}) collective-permute-start(bf16[1,384,128]{2,1,0:T(8,128)(2,1)S(1)} %bitcast.12), channel_id=1, source_target_pairs={{0,31},{1,24},{2,25},{3,26},{4,27},{5,28},{6,29},{7,30},{8,7},{9,0... | collective-permute-start | bytes 294920 | tf_op jit(solution)/shard_map/ppermute | solution.py:414
  17.9 4.4 %collective-permute-start.3 = (f32[80,128]{1,0:T(8,128)S(1)}, f32[80,128]{1,0:T(8,128)S(1)}, u32[]{:S(2)}, u32[]{:S(2)}) collective-permute-start(f32[80,128]{1,0:T(8,128)S(1)} %shard_map.79), channel_id=1, source_target_pairs={{0,16},{8,24},{16,0},{24,8},{1,17},{9,25},{17,1},{25,9},{2,18},{10... | collective-permute-start | bytes 122888 | tf_op jit(solution)/shard_map/ppermute | solution.py:502
  19.5 4.9 %collective-permute-start.4 = (f32[80,128]{1,0:T(8,128)S(1)}, f32[80,128]{1,0:T(8,128)S(1)}, u32[]{:S(2)}, u32[]{:S(2)}) collective-permute-start(f32[80,128]{1,0:T(8,128)S(1)} %shard_map.79), channel_id=1, source_target_pairs={{0,24},{8,16},{16,8},{24,0},{1,25},{9,17},{17,9},{25,1},{2,26},{10... | collective-permute-start | bytes 122888 | tf_op jit(solution)/shard_map/ppermute | solution.py:502
  20.9 4.0 %collective-permute-start.5 = (f32[80,128]{1,0:T(8,128)S(1)}, f32[80,128]{1,0:T(8,128)S(1)}, u32[]{:S(2)}, u32[]{:S(2)}) collective-permute-start(f32[80,128]{1,0:T(8,128)S(1)} %shard_map.79), channel_id=1, source_target_pairs={{0,8},{8,0},{16,24},{24,16},{1,9},{9,1},{17,25},{25,17},{2,10},{10... | collective-permute-start | bytes 122888 | tf_op jit(solution)/shard_map/ppermute | solution.py:502
  25.0 5.3 %collective-permute-start.6 = (f32[80,128]{1,0:T(8,128)S(1)}, f32[80,128]{1,0:T(8,128)S(1)}, u32[]{:S(2)}, u32[]{:S(2)}) collective-permute-start(f32[80,128]{1,0:T(8,128)S(1)} %add_add_fusion.1), channel_id=1, source_target_pairs={{0,4},{1,5},{2,6},{3,7},{4,0},{5,1},{6,2},{7,3},{8,12},{9,13},{10,... | collective-permute-start | bytes 122888 | tf_op jit(solution)/shard_map/ppermute | solution.py:502
  25.0 6.0 %collective-permute-start.7 = (f32[80,128]{1,0:T(8,128)S(1)}, f32[80,128]{1,0:T(8,128)S(1)}, u32[]{:S(2)}, u32[]{:S(2)}) collective-permute-start(f32[80,128]{1,0:T(8,128)S(1)} %add_add_fusion.1), channel_id=1, source_target_pairs={{0,6},{1,7},{2,4},{3,5},{4,2},{5,3},{6,0},{7,1},{8,14},{9,15},{10,... | collective-permute-start | bytes 122888 | tf_op jit(solution)/shard_map/ppermute | solution.py:502
  26.2 5.1 %collective-permute-start.8 = (f32[80,128]{1,0:T(8,128)S(1)}, f32[80,128]{1,0:T(8,128)S(1)}, u32[]{:S(2)}, u32[]{:S(2)}) collective-permute-start(f32[80,128]{1,0:T(8,128)S(1)} %add_add_fusion.1), channel_id=1, source_target_pairs={{0,2},{1,3},{2,0},{3,1},{4,6},{5,7},{6,4},{7,5},{8,10},{9,11},{10,... | collective-permute-start | bytes 122888 | tf_op jit(solution)/shard_map/ppermute | solution.py:502
  31.3 1.3 %collective-permute-start.9 = (f32[80,128]{1,0:T(8,128)S(1)}, f32[80,128]{1,0:T(8,128)S(1)}, u32[]{:S(2)}, u32[]{:S(2)}) collective-permute-start(f32[80,128]{1,0:T(8,128)S(1)} %add_add_fusion.mine_ref), channel_id=1, source_target_pairs={{0,1},{1,0},{2,3},{3,2},{4,5},{5,4},{6,7},{7,6},{8,9},{9,8},{10,11... | collective-permute-start | bytes 122888 | tf_op jit(solution)/shard_map/ppermute | solution.py:502

commit v5 on v3

--- a/solution.py
+++ b/solution.py
@@ -20,6 +20,7 @@
 ]
 TILE = 16
 PARTS = 4
+ORDERS = {("sub", 2): (1,), ("sub", 4): (3, 1, 2), ("dom", 2): (1,), ("dom", 4): (2, 3, 1)}
 
 
 def corner_bits(corner):
@@ -273,8 +274,8 @@
             blocks_ref[at, edge_at:load_at] = edge_ref[...].astype(jnp.bfloat16)
 
 
-def contract(y, planes, depth, blocks_ref, gather_ref, carry_ref, sum_ref):
-    modes = sum_ref.shape[1]
+def contract(y, planes, depth, blocks_ref, gather_ref, carry_in, carry_out, total):
+    modes = total.shape[1]
     span = depth // PARTS
     own_lanes = lax.broadcasted_iota(jnp.int32, (modes, depth), 1) < 2 * span
     nothing = jnp.zeros((8, modes), jnp.float32)
@@ -289,7 +290,6 @@
             around = rows(p, border * span - TILE, 2 * TILE).astype(jnp.float32)
             at = ((border - 1) * 8 + p) * TILE
             gather_ref[at : at + TILE] = around[TILE // 2 : TILE + TILE // 2]
-    total = sum_ref[...]
     for part in range(PARTS):
         before, after = nothing, nothing
         if part > 0:
@@ -303,11 +303,15 @@
         product = jnp.dot(
             turned, blocks_ref[at, 0 : 6 * span + TILE], preferred_element_type=jnp.float32
         )
-        first = product[:, 0:depth] + carry_ref[part, 0]
-        middle = product[:, depth : 2 * depth]
-        second = jnp.where(own_lanes, middle + carry_ref[part, 1], 0.0)
-        carry_ref[part, 0] = product[:, 2 * depth :]
-        carry_ref[part, 1] = pltpu.roll(middle, 2 * span, 1)
+        first = product[:, 0:depth]
+        middle = second = product[:, depth : 2 * depth]
+        if carry_in is not None:
+            first = first + carry_in[part, 0]
+            second = second + carry_in[part, 1]
+        second = jnp.where(own_lanes, second, 0.0)
+        if carry_out is not None:
+            carry_out[part, 0] = product[:, 2 * depth :]
+            carry_out[part, 1] = pltpu.roll(middle, 2 * span, 1)
         factors = jnp.concatenate([first, second], 1).astype(jnp.bfloat16)
         factors = jnp.concatenate(
             [factors, blocks_ref[at, 6 * span + TILE : 6 * span + 2 * TILE, 0 : 2 * depth]], 0
@@ -315,24 +319,25 @@
         total = total + jnp.dot(
             factors[:, 0 : 6 * span], here, preferred_element_type=jnp.float32
         )
-    sum_ref[...] = total
+    return total
 
 
 def contraction_kernel(own_ref, front_ref, blocks_ref, sum_ref, carry_ref, gather_ref):
     columns, plane_rows, modes = own_ref.shape
-    carry_ref[...] = jnp.zeros_like(carry_ref)
     gather_ref[...] = jnp.zeros_like(gather_ref)
-    sum_ref[...] = jnp.zeros_like(sum_ref)
-
-    @pl.loop(0, columns, unroll=True)
-    def _(y):
+    total = jnp.zeros(sum_ref.shape, jnp.float32)
+    for y in range(columns):
         planes = ((own_ref, y), (front_ref, y))
-        contract(y, planes, plane_rows // 3, blocks_ref, gather_ref, carry_ref, sum_ref)
+        carried = carry_ref if y else None
+        total = contract(
+            y, planes, plane_rows // 3, blocks_ref, gather_ref, carried, carry_ref, total
+        )
+    sum_ref[...] = total
 
 
 def last_kernel(
     side_ref, corner_ref, blocks_ref, sum_in, carry_in, packed_ref,
-    gather_ref, carry_ref, sum_ref, ends_ref,
+    gather_ref, ends_ref,
 ):
     inside = lax.axis_index("sub") < lax.axis_size("sub") - 1
     ends_ref[0:1] = jnp.where(inside, side_ref[...], jnp.bfloat16(0))
@@ -340,12 +345,11 @@
     ends_ref[1:2] = jnp.where(inside, corner_ref[...], jnp.bfloat16(0))
     ignored, plane_rows, modes = side_ref.shape
     columns = blocks_ref.shape[0] // PARTS - 1
-    carry_ref[...] = carry_in[...]
     gather_ref[...] = jnp.zeros_like(gather_ref)
-    sum_ref[...] = sum_in[...]
     planes = ((ends_ref, 0), (ends_ref, 1))
-    contract(columns, planes, plane_rows // 3, blocks_ref, gather_ref, carry_ref, sum_ref)
-    total = sum_ref[...]
+    total = contract(
+        columns, planes, plane_rows // 3, blocks_ref, gather_ref, carry_in, None, sum_in[...]
+    )
     upper = total[0:modes]
     tangent = upper + upper.T
     packed_ref[...] = packed(tangent, total[modes : modes + 1] + total[modes + 1 : modes + 2])
@@ -470,8 +474,6 @@
         out_specs=whole,
         scratch_shapes=[
             gather_scratch,
-            pltpu.VMEM(carry_shape.shape, jnp.float32),
-            pltpu.VMEM(sum_shape.shape, jnp.float32),
             pltpu.VMEM((2, plane_rows, modes), jnp.bfloat16),
         ],
         compiler_params=pltpu.CompilerParams(vmem_limit_bytes=24 * 2**20),
@@ -480,7 +482,7 @@
 
     for axis, first in (("sub", 1), ("dom", 2)):
         for stride, radix in stages(first, lax.axis_size(axis)):
-            received = [exchanged(mine, axis, stride * k) for k in range(radix - 1, 0, -1)]
+            received = [exchanged(mine, axis, stride * k) for k in ORDERS[axis, radix]]
             mine = sum(received, mine)
     other = exchanged(mine, "dom", 1)
     tangent, residual = pl.pallas_call(

time: 33.8 us -> 33.5 us (level)
  starting transfers between devices: 15.6 us -> 14.5 us
  waiting for transfers between devices: 7.54 us -> 8.39 us
    ppermute x7, starting transfers between devices: 8.23 us -> 7.17 us  [exchanged(): lax.ppermute(value, axis, [(s, s ^ distance) for s in range(lax.axis_size...]
    ppermute x7, waiting for transfers between devices: 6.61 us -> 7.47 us  [exchanged(): lax.ppermute(value, axis, [(s, s ^ distance) for s in range(lax.axis_size...]
  transfers between devices with their start and end apart: 10 -> 10, of which waited for: 7 -> 8; matrix products, arithmetic and copies ran while one was open for 6% -> 6% of each run, Pallas kernels for 19% -> 19%
where the time goes in v5:
time: 33.5 us; the launch traced here: 33.3 us
  starting transfers between devices  14.5 us (43%)
  waiting for transfers between devices  8.39 us (25%)
  Pallas kernels  7.73 us (23%)
  other arithmetic  1.05 us (3%)
  local copies, waits for them, and re-layouts  0.94 us (3%)
  between operations  0.7 us (2%)
    ppermute x7, waiting for transfers between devices, exchanged(): lax.ppermute(value, axis, [(s, s ^ distance) for s in range(lax.axis_size...  7.47 us
    ppermute x7, starting transfers between devices, exchanged(): lax.ppermute(value, axis, [(s, s ^ distance) for s in range(lax.axis_size...  7.17 us
    ppermute x1, starting transfers between devices, on_device(): front = lax.ppermute(own, 'dom', [(s, (s - 1) % doms) for s in range(doms)])  4.54 us
    pallas_call x1, Pallas kernels, on_device(): pl.pallas_call(stiffness_kernel, out_shape=jax.ShapeDtypeStruct(blocks_sh...  4.14 us
    ppermute x1, starting transfers between devices, on_device(): lax.ppermute(first, 'sub', [(s, (s - 1) % subs) for s in range(subs)])  2.45 us
    pallas_call x1, Pallas kernels, on_device(): pl.pallas_call(contraction_kernel, out_shape=(sum_shape, carry_shape), in...  2.2 us
    add x1, other arithmetic, on_device(): state + jnp.pad(value, ((at, count - end), (0, 0), (0, 0))).astype(jnp.fl...  1.02 us
    slice x1, local copies, waits for them, and re-layouts, on_device(): first = own[0:1]  0.93 us
  transfers between devices with their start and end apart: 10, of which 8 were waited for; matrix products, arithmetic and copies ran while one was open for 6% of the time, Pallas kernels for 19%

profile of v5, /device:TPU:0, one launch (start us, length us, event | category | flops | bytes accessed | tf_op | source)
XLA Modules:
  0.0 33.3 jit_solution(4820112522652632024)
XLA Ops:
  0.6 0.0 copy-start
  0.6 4.5 %collective-permute-start.2 = (bf16[8,384,128]{2,1,0:T(8,128)(2,1)}, bf16[8,384,128]{2,1,0:T(8,128)(2,1)S(1)}, u32[]{:S(2)}, u32[]{:S(2)}) collective-permute-start(bf16[8,384,128]{2,1,0:T(8,128)(2,1)} %bitcast.8), channel_id=1, source_target_pairs={{0,7},{1,0},{2,1},{3,2},{4,3},{5,4},{6,5},{7,6},{8,15},{9,8},{10,9... | collective-permute-start | bytes 2359304 | tf_op jit(solution)/shard_map/ppermute | solution.py:415
  5.2 0.9 %slice.6 = bf16[1,1,3,128,128]{4,3,2,1,0:T(8,128)(2,1)S(1)} slice(bf16[1,8,3,128,128]{4,3,2,1,0:T(8,128)(2,1)} %param.6), slice={[0:1], [0:1], [0:3], [0:128], [0:128]} | slice | bytes 196608 | tf_op jit(solution)/shard_map/slice | solution.py:416
  6.1 2.4 %collective-permute-start = (bf16[1,384,128]{2,1,0:T(8,128)(2,1)S(1)}, bf16[1,384,128]{2,1,0:T(8,128)(2,1)S(1)}, u32[]{:S(2)}, u32[]{:S(2)}) collective-permute-start(bf16[1,384,128]{2,1,0:T(8,128)(2,1)S(1)} %bitcast.11), channel_id=1, source_target_pairs={{0,24},{8,0},{16,8},{24,16},{1,25},{9,1},{17,9},{25,17},{2,26},{10... | collective-permute-start | bytes 294920 | tf_op jit(solution)/shard_map/ppermute | solution.py:426
  8.6 0.3 %collective-permute-start.1 = (bf16[1,384,128]{2,1,0:T(8,128)(2,1)S(1)}, bf16[1,384,128]{2,1,0:T(8,128)(2,1)S(1)}, u32[]{:S(2)}, u32[]{:S(2)}) collective-permute-start(bf16[1,384,128]{2,1,0:T(8,128)(2,1)S(1)} %bitcast.12), channel_id=1, source_target_pairs={{0,31},{1,24},{2,25},{3,26},{4,27},{5,28},{6,29},{7,30},{8,7},{9,0... | collective-permute-start | bytes 294920 | tf_op jit(solution)/shard_map/ppermute | solution.py:417
  8.9 1.0 %pad_add_fusion.state_ref = f32[69,8,128]{2,1,0:T(8,128)S(1)} fusion(f32[3,8,128]{2,1,0:T(8,128)} %bitcast.15, f32[2,8,128]{2,1,0:T(8,128)} %bitcast.16, f32[8,8,128]{2,1,0:T(8,128)} %bitcast.13, s32[8,8,128]{2,1,0:T(8,128)} %bitcast.14, f32[48,8,128]{2,1,0:T(8,128)} %bitcast.10), kind=kLoop, calls=%fused_computation | loop fusion | flops 353280 | bytes 565248 | tf_op jit(solution)/shard_map/add | solution.py:438
  9.9 4.1 %shard_map.77.blocks_ref = bf16[36,224,384]{2,1,0:T(8,128)(2,1)S(1)} custom-call(f32[69,8,128]{2,1,0:T(8,128)S(1)} %pad_add_fusion.state_ref), custom_call_target="tpu_custom_call" | custom-call | flops 20000000 | bytes 8000000 | tf_op jit(solution)/shard_map/pallas_call | solution.py:441
  14.1 0.9 %collective-permute-done.2.front_ref = bf16[8,384,128]{2,1,0:T(8,128)(2,1)S(1)} collective-permute-done((bf16[8,384,128]{2,1,0:T(8,128)(2,1)}, bf16[8,384,128]{2,1,0:T(8,128)(2,1)S(1)}, u32[]{:S(2)}, u32[]{:S(2)}) %collective-permute-start.2) | collective-permute-done | bytes 786464 | tf_op jit(solution)/shard_map/ppermute | solution.py:415
  15.0 0.0 copy-done
  15.0 2.2 %shard_map.78 = (f32[144,128]{1,0:T(8,128)S(1)}, f32[4,2,128,128]{3,2,1,0:T(8,128)S(1)}) custom-call(bf16[8,384,128]{2,1,0:T(8,128)(2,1)S(1)} %bitcast.9, bf16[8,384,128]{2,1,0:T(8,128)(2,1)S(1)} %collective-permute-done.2.front_ref, bf16[36,224,384]{2,1,0:T(8,128)(2,1)S(1)} %shard_map.77.blocks_ref), custom_call_target="tpu_custom_call" | custom-call | flops 2000000000 | bytes 8000000 | tf_op jit(solution)/shard_map/pallas_call | solution.py:461
  17.2 0.0 collective-permute-done.side_ref
  17.2 0.0 collective-permute-done.1.corner_ref
  17.2 0.6 %shard_map.79 = f32[80,128]{1,0:T(8,128)S(1)} custom-call(bf16[1,384,128]{2,1,0:T(8,128)(2,1)S(1)} %collective-permute-done.side_ref, bf16[1,384,128]{2,1,0:T(8,128)(2,1)S(1)} %collective-permute-done.1.corner_ref, bf16[36,224,384]{2,1,0:T(8,128)(2,1)S(1)} %shard_map.77.blocks_ref, f32[144,128]{1,0:T(8,128)S(1)} %get-tuple-element.6.sum_in, ...), custom_call_target="tpu_custom_call" | custom-call | flops 200000000 | bytes 1000000 | tf_op jit(solution)/shard_map/pallas_call | solution.py:470
  17.8 2.5 %collective-permute-start.3 = (f32[80,128]{1,0:T(8,128)S(1)}, f32[80,128]{1,0:T(8,128)S(1)}, u32[]{:S(2)}, u32[]{:S(2)}) collective-permute-start(f32[80,128]{1,0:T(8,128)S(1)} %shard_map.79), channel_id=1, source_target_pairs={{0,24},{8,16},{16,8},{24,0},{1,25},{9,17},{17,9},{25,1},{2,26},{10... | collective-permute-start | bytes 122888 | tf_op jit(solution)/shard_map/ppermute | solution.py:503
  20.4 0.5 %collective-permute-start.4 = (f32[80,128]{1,0:T(8,128)S(1)}, f32[80,128]{1,0:T(8,128)S(1)}, u32[]{:S(2)}, u32[]{:S(2)}) collective-permute-start(f32[80,128]{1,0:T(8,128)S(1)} %shard_map.79), channel_id=1, source_target_pairs={{0,8},{8,0},{16,24},{24,16},{1,9},{9,1},{17,25},{25,17},{2,10},{10... | collective-permute-start | bytes 122888 | tf_op jit(solution)/shard_map/ppermute | solution.py:503
  20.9 0.5 %collective-permute-start.5 = (f32[80,128]{1,0:T(8,128)S(1)}, f32[80,128]{1,0:T(8,128)S(1)}, u32[]{:S(2)}, u32[]{:S(2)}) collective-permute-start(f32[80,128]{1,0:T(8,128)S(1)} %shard_map.79), channel_id=1, source_target_pairs={{0,16},{8,24},{16,0},{24,8},{1,17},{9,25},{17,1},{25,9},{2,18},{10... | collective-permute-start | bytes 122888 | tf_op jit(solution)/shard_map/ppermute | solution.py:503
  21.4 1.5 %collective-permute-done.3 = f32[80,128]{1,0:T(8,128)S(1)} collective-permute-done((f32[80,128]{1,0:T(8,128)S(1)}, f32[80,128]{1,0:T(8,128)S(1)}, u32[]{:S(2)}, u32[]{:S(2)}) %collective-permute-start.3) | collective-permute-done | bytes 40992 | tf_op jit(solution)/shard_map/ppermute | solution.py:503
  22.9 1.5 %collective-permute-done.4 = f32[80,128]{1,0:T(8,128)S(1)} collective-permute-done((f32[80,128]{1,0:T(8,128)S(1)}, f32[80,128]{1,0:T(8,128)S(1)}, u32[]{:S(2)}, u32[]{:S(2)}) %collective-permute-start.4) | collective-permute-done | bytes 40992 | tf_op jit(solution)/shard_map/ppermute | solution.py:503
  24.4 0.5 %collective-permute-done.5 = f32[80,128]{1,0:T(8,128)S(1)} collective-permute-done((f32[80,128]{1,0:T(8,128)S(1)}, f32[80,128]{1,0:T(8,128)S(1)}, u32[]{:S(2)}, u32[]{:S(2)}) %collective-permute-start.5) | collective-permute-done | bytes 40992 | tf_op jit(solution)/shard_map/ppermute | solution.py:503
  24.9 0.1 collective-permute-start.6
  25.0 1.1 %collective-permute-start.7 = (f32[80,128]{1,0:T(8,128)S(1)}, f32[80,128]{1,0:T(8,128)S(1)}, u32[]{:S(2)}, u32[]{:S(2)}) collective-permute-start(f32[80,128]{1,0:T(8,128)S(1)} %add_add_fusion.1), channel_id=1, source_target_pairs={{0,6},{1,7},{2,4},{3,5},{4,2},{5,3},{6,0},{7,1},{8,14},{9,15},{10,... | collective-permute-start | bytes 122888 | tf_op jit(solution)/shard_map/ppermute | solution.py:503
  26.1 2.4 %collective-permute-start.8 = (f32[80,128]{1,0:T(8,128)S(1)}, f32[80,128]{1,0:T(8,128)S(1)}, u32[]{:S(2)}, u32[]{:S(2)}) collective-permute-start(f32[80,128]{1,0:T(8,128)S(1)} %add_add_fusion.1), channel_id=1, source_target_pairs={{0,2},{1,3},{2,0},{3,1},{4,6},{5,7},{6,4},{7,5},{8,10},{9,11},{10,... | collective-permute-start | bytes 122888 | tf_op jit(solution)/shard_map/ppermute | solution.py:503
  28.5 1.7 %collective-permute-done.6 = f32[80,128]{1,0:T(8,128)S(1)} collective-permute-done((f32[80,128]{1,0:T(8,128)S(1)}, f32[80,128]{1,0:T(8,128)S(1)}, u32[]{:S(2)}, u32[]{:S(2)}) %collective-permute-start.6) | collective-permute-done | bytes 40992 | tf_op jit(solution)/shard_map/ppermute | solution.py:503
  30.2 0.8 %collective-permute-done.7 = f32[80,128]{1,0:T(8,128)S(1)} collective-permute-done((f32[80,128]{1,0:T(8,128)S(1)}, f32[80,128]{1,0:T(8,128)S(1)}, u32[]{:S(2)}, u32[]{:S(2)}) %collective-permute-start.7) | collective-permute-done | bytes 40992 | tf_op jit(solution)/shard_map/ppermute | solution.py:503
  31.0 0.2 collective-permute-done.8
  31.2 0.1 collective-permute-start.9
  31.3 1.2 %collective-permute-done.9.other_ref = f32[80,128]{1,0:T(8,128)S(1)} collective-permute-done((f32[80,128]{1,0:T(8,128)S(1)}, f32[80,128]{1,0:T(8,128)S(1)}, u32[]{:S(2)}, u32[]{:S(2)}) %collective-permute-start.9) | collective-permute-done | bytes 40992 | tf_op jit(solution)/shard_map/ppermute | solution.py:503
  32.5 0.8 %shard_map.80 = (f32[128,128]{1,0:T(8,128)}, f32[1,128]{1,0:T(1,128)}) custom-call(f32[80,128]{1,0:T(8,128)S(1)} %add_add_fusion.mine_ref, f32[80,128]{1,0:T(8,128)S(1)} %collective-permute-done.9.other_ref), custom_call_target="tpu_custom_call" | custom-call | tf_op jit(solution)/shard_map/pallas_call | solution.py:488
  (2 shorter events, 0.0 us)
Async XLA Ops:
  0.6 14.4 %copy-start = (bf16[1,8,3,128,128]{4,3,2,1,0:T(8,128)(2,1)S(1)}, bf16[1,8,3,128,128]{4,3,2,1,0:T(8,128)(2,1)}, u32[]{:S(2)}) copy-start(bf16[1,8,3,128,128]{4,3,2,1,0:T(8,128)(2,1)} %param.6) | copy-start | bytes 2359300
  0.6 14.4 %collective-permute-start.2 = (bf16[8,384,128]{2,1,0:T(8,128)(2,1)}, bf16[8,384,128]{2,1,0:T(8,128)(2,1)S(1)}, u32[]{:S(2)}, u32[]{:S(2)}) collective-permute-start(bf16[8,384,128]{2,1,0:T(8,128)(2,1)} %bitcast.8), channel_id=1, source_target_pairs={{0,7},{1,0},{2,1},{3,2},{4,3},{5,4},{6,5},{7,6},{8,15},{9,8},{10,9... | collective-permute-start | bytes 2359304 | tf_op jit(solution)/shard_map/ppermute | solution.py:415
  6.1 11.1 %collective-permute-start = (bf16[1,384,128]{2,1,0:T(8,128)(2,1)S(1)}, bf16[1,384,128]{2,1,0:T(8,128)(2,1)S(1)}, u32[]{:S(2)}, u32[]{:S(2)}) collective-permute-start(bf16[1,384,128]{2,1,0:T(8,128)(2,1)S(1)} %bitcast.11), channel_id=1, source_target_pairs={{0,24},{8,0},{16,8},{24,16},{1,25},{9,1},{17,9},{25,17},{2,26},{10... | collective-permute-start | bytes 294920 | tf_op jit(solution)/shard_map/ppermute | solution.py:426
  8.6 8.7 %collective-permute-start.1 = (bf16[1,384,128]{2,1,0:T(8,128)(2,1)S(1)}, bf16[1,384,128]{2,1,0:T(8,128)(2,1)S(1)}, u32[]{:S(2)}, u32[]{:S(2)}) collective-permute-start(bf16[1,384,128]{2,1,0:T(8,128)(2,1)S(1)} %bitcast.12), channel_id=1, source_target_pairs={{0,31},{1,24},{2,25},{3,26},{4,27},{5,28},{6,29},{7,30},{8,7},{9,0... | collective-permute-start | bytes 294920 | tf_op jit(solution)/shard_map/ppermute | solution.py:417
  17.8 5.0 %collective-permute-start.3 = (f32[80,128]{1,0:T(8,128)S(1)}, f32[80,128]{1,0:T(8,128)S(1)}, u32[]{:S(2)}, u32[]{:S(2)}) collective-permute-start(f32[80,128]{1,0:T(8,128)S(1)} %shard_map.79), channel_id=1, source_target_pairs={{0,24},{8,16},{16,8},{24,0},{1,25},{9,17},{17,9},{25,1},{2,26},{10... | collective-permute-start | bytes 122888 | tf_op jit(solution)/shard_map/ppermute | solution.py:503
  20.4 4.0 %collective-permute-start.4 = (f32[80,128]{1,0:T(8,128)S(1)}, f32[80,128]{1,0:T(8,128)S(1)}, u32[]{:S(2)}, u32[]{:S(2)}) collective-permute-start(f32[80,128]{1,0:T(8,128)S(1)} %shard_map.79), channel_id=1, source_target_pairs={{0,8},{8,0},{16,24},{24,16},{1,9},{9,1},{17,25},{25,17},{2,10},{10... | collective-permute-start | bytes 122888 | tf_op jit(solution)/shard_map/ppermute | solution.py:503
  20.9 4.0 %collective-permute-start.5 = (f32[80,128]{1,0:T(8,128)S(1)}, f32[80,128]{1,0:T(8,128)S(1)}, u32[]{:S(2)}, u32[]{:S(2)}) collective-permute-start(f32[80,128]{1,0:T(8,128)S(1)} %shard_map.79), channel_id=1, source_target_pairs={{0,16},{8,24},{16,0},{24,8},{1,17},{9,25},{17,1},{25,9},{2,18},{10... | collective-permute-start | bytes 122888 | tf_op jit(solution)/shard_map/ppermute | solution.py:503
  24.9 5.3 %collective-permute-start.6 = (f32[80,128]{1,0:T(8,128)S(1)}, f32[80,128]{1,0:T(8,128)S(1)}, u32[]{:S(2)}, u32[]{:S(2)}) collective-permute-start(f32[80,128]{1,0:T(8,128)S(1)} %add_add_fusion.1), channel_id=1, source_target_pairs={{0,4},{1,5},{2,6},{3,7},{4,0},{5,1},{6,2},{7,3},{8,12},{9,13},{10,... | collective-permute-start | bytes 122888 | tf_op jit(solution)/shard_map/ppermute | solution.py:503
  25.0 6.0 %collective-permute-start.7 = (f32[80,128]{1,0:T(8,128)S(1)}, f32[80,128]{1,0:T(8,128)S(1)}, u32[]{:S(2)}, u32[]{:S(2)}) collective-permute-start(f32[80,128]{1,0:T(8,128)S(1)} %add_add_fusion.1), channel_id=1, source_target_pairs={{0,6},{1,7},{2,4},{3,5},{4,2},{5,3},{6,0},{7,1},{8,14},{9,15},{10,... | collective-permute-start | bytes 122888 | tf_op jit(solution)/shard_map/ppermute | solution.py:503
  26.1 5.1 %collective-permute-start.8 = (f32[80,128]{1,0:T(8,128)S(1)}, f32[80,128]{1,0:T(8,128)S(1)}, u32[]{:S(2)}, u32[]{:S(2)}) collective-permute-start(f32[80,128]{1,0:T(8,128)S(1)} %add_add_fusion.1), channel_id=1, source_target_pairs={{0,2},{1,3},{2,0},{3,1},{4,6},{5,7},{6,4},{7,5},{8,10},{9,11},{10,... | collective-permute-start | bytes 122888 | tf_op jit(solution)/shard_map/ppermute | solution.py:503
  31.2 1.3 %collective-permute-start.9 = (f32[80,128]{1,0:T(8,128)S(1)}, f32[80,128]{1,0:T(8,128)S(1)}, u32[]{:S(2)}, u32[]{:S(2)}) collective-permute-start(f32[80,128]{1,0:T(8,128)S(1)} %add_add_fusion.mine_ref), channel_id=1, source_target_pairs={{0,1},{1,0},{2,3},{3,2},{4,5},{5,4},{6,7},{7,6},{8,9},{9,8},{10,11... | collective-permute-start | bytes 122888 | tf_op jit(solution)/shard_map/ppermute | solution.py:503

commit v6 on v5

--- a/solution.py
+++ b/solution.py
@@ -322,8 +322,8 @@
     return total
 
 
-def contraction_kernel(own_ref, front_ref, blocks_ref, sum_ref, carry_ref, gather_ref):
-    columns, plane_rows, modes = own_ref.shape
+def contract_all(own_ref, front_ref, blocks_ref, sum_ref, carry_ref, gather_ref):
+    columns, plane_rows, ignored = own_ref.shape
     gather_ref[...] = jnp.zeros_like(gather_ref)
     total = jnp.zeros(sum_ref.shape, jnp.float32)
     for y in range(columns):
@@ -333,6 +333,29 @@
             y, planes, plane_rows // 3, blocks_ref, gather_ref, carried, carry_ref, total
         )
     sum_ref[...] = total
+
+
+def on_last_layer():
+    return lax.axis_index("dom") == lax.axis_size("dom") - 1
+
+
+def early_kernel(own_ref, blocks_ref, sum_ref, carry_ref, gather_ref):
+    @pl.when(on_last_layer())
+    def _():
+        contract_all(own_ref, own_ref, blocks_ref, sum_ref, carry_ref, gather_ref)
+
+
+def contraction_kernel(
+    own_ref, front_ref, blocks_ref, sum_early, carry_early, sum_ref, carry_ref, gather_ref
+):
+    @pl.when(on_last_layer())
+    def _():
+        sum_ref[...] = sum_early[...]
+        carry_ref[...] = carry_early[...]
+
+    @pl.when(jnp.logical_not(on_last_layer()))
+    def _():
+        contract_all(own_ref, front_ref, blocks_ref, sum_ref, carry_ref, gather_ref)
 
 
 def last_kernel(
@@ -458,15 +481,19 @@
     gather_scratch = pltpu.VMEM(((PARTS - 1) * 8 * TILE + TILE, modes), jnp.float32)
     sum_shape = jax.ShapeDtypeStruct((modes + TILE, modes), jnp.float32)
     carry_shape = jax.ShapeDtypeStruct((PARTS, 2, modes, depth), jnp.float32)
-    partial, carry = pl.pallas_call(
-        contraction_kernel,
-        out_shape=(sum_shape, carry_shape),
-        in_specs=[whole] * 3,
-        out_specs=(whole, whole),
-        scratch_shapes=[gather_scratch],
-        compiler_params=pltpu.CompilerParams(vmem_limit_bytes=24 * 2**20),
-        cost_estimate=pl.CostEstimate(flops=2_000_000_000, bytes_accessed=8_000_000, transcendentals=0),
-    )(own, front, blocks)
+    settings = {
+        "out_shape": (sum_shape, carry_shape),
+        "out_specs": (whole, whole),
+        "scratch_shapes": [gather_scratch],
+        "compiler_params": pltpu.CompilerParams(vmem_limit_bytes=24 * 2**20),
+        "cost_estimate": pl.CostEstimate(
+            flops=2_000_000_000, bytes_accessed=8_000_000, transcendentals=0
+        ),
+    }
+    early = pl.pallas_call(early_kernel, in_specs=[whole] * 2, **settings)(own, blocks)
+    partial, carry = pl.pallas_call(contraction_kernel, in_specs=[whole] * 5, **settings)(
+        own, front, blocks, *early
+    )
     mine = pl.pallas_call(
         last_kernel,
         out_shape=jax.ShapeDtypeStruct((packed_rows, modes), jnp.float32),

time: 33.5 us -> 33.5 us (level)
    pallas_call x1 -> x2, Pallas kernels: 2.2 us -> 2.21 us  [the longest x1 2.2 us: on_device(): pl.pallas_call(contraction_kernel, in_specs=[whole] * 5, **settings)]
  transfers between devices with their start and end apart: 10 -> 10, of which waited for: 8 -> 7; matrix products, arithmetic and copies ran while one was open for 6% -> 6% of each run, Pallas kernels for 19% -> 19%
where the time goes in v6:
time: 33.5 us; the launch traced here: 33.3 us
  starting transfers between devices  14.5 us (43%)
  waiting for transfers between devices  8.33 us (25%)
  Pallas kernels  7.75 us (23%)
  other arithmetic  1.05 us (3%)
  local copies, waits for them, and re-layouts  0.94 us (3%)
  between operations  0.72 us (2%)
    ppermute x7, waiting for transfers between devices, exchanged(): lax.ppermute(value, axis, [(s, s ^ distance) for s in range(lax.axis_size...  7.44 us
    ppermute x7, starting transfers between devices, exchanged(): lax.ppermute(value, axis, [(s, s ^ distance) for s in range(lax.axis_size...  7.17 us
    ppermute x1, starting transfers between devices, on_device(): front = lax.ppermute(own, 'dom', [(s, (s - 1) % doms) for s in range(doms)])  4.54 us
    pallas_call x1, Pallas kernels, on_device(): pl.pallas_call(stiffness_kernel, out_shape=jax.ShapeDtypeStruct(blocks_sh...  4.14 us
    ppermute x1, starting transfers between devices, on_device(): lax.ppermute(first, 'sub', [(s, (s - 1) % subs) for s in range(subs)])  2.45 us
    pallas_call x1, Pallas kernels, on_device(): pl.pallas_call(contraction_kernel, in_specs=[whole] * 5, **settings)  2.2 us
    add x1, other arithmetic, on_device(): state + jnp.pad(value, ((at, count - end), (0, 0), (0, 0))).astype(jnp.fl...  1.02 us
    slice x1, local copies, waits for them, and re-layouts, on_device(): first = own[0:1]  0.93 us
  transfers between devices with their start and end apart: 10, of which 7 were waited for; matrix products, arithmetic and copies ran while one was open for 6% of the time, Pallas kernels for 19%

profile of v6, /device:TPU:0, one launch (start us, length us, event | category | flops | bytes accessed | tf_op | source)
XLA Modules:
  0.0 33.3 jit_solution(15612487165331266081)
XLA Ops:
  0.6 0.0 copy-start
  0.6 4.5 %collective-permute-start.2 = (bf16[8,384,128]{2,1,0:T(8,128)(2,1)}, bf16[8,384,128]{2,1,0:T(8,128)(2,1)S(1)}, u32[]{:S(2)}, u32[]{:S(2)}) collective-permute-start(bf16[8,384,128]{2,1,0:T(8,128)(2,1)} %bitcast.8), channel_id=1, source_target_pairs={{0,7},{1,0},{2,1},{3,2},{4,3},{5,4},{6,5},{7,6},{8,15},{9,8},{10,9... | collective-permute-start | bytes 2359304 | tf_op jit(solution)/shard_map/ppermute | solution.py:438
  5.2 0.9 %slice.6 = bf16[1,1,3,128,128]{4,3,2,1,0:T(8,128)(2,1)S(1)} slice(bf16[1,8,3,128,128]{4,3,2,1,0:T(8,128)(2,1)} %param.6), slice={[0:1], [0:1], [0:3], [0:128], [0:128]} | slice | bytes 196608 | tf_op jit(solution)/shard_map/slice | solution.py:439
  6.1 2.4 %collective-permute-start = (bf16[1,384,128]{2,1,0:T(8,128)(2,1)S(1)}, bf16[1,384,128]{2,1,0:T(8,128)(2,1)S(1)}, u32[]{:S(2)}, u32[]{:S(2)}) collective-permute-start(bf16[1,384,128]{2,1,0:T(8,128)(2,1)S(1)} %bitcast.12), channel_id=1, source_target_pairs={{0,24},{8,0},{16,8},{24,16},{1,25},{9,1},{17,9},{25,17},{2,26},{10... | collective-permute-start | bytes 294920 | tf_op jit(solution)/shard_map/ppermute | solution.py:449
  8.6 0.3 %collective-permute-start.1 = (bf16[1,384,128]{2,1,0:T(8,128)(2,1)S(1)}, bf16[1,384,128]{2,1,0:T(8,128)(2,1)S(1)}, u32[]{:S(2)}, u32[]{:S(2)}) collective-permute-start(bf16[1,384,128]{2,1,0:T(8,128)(2,1)S(1)} %bitcast.13), channel_id=1, source_target_pairs={{0,31},{1,24},{2,25},{3,26},{4,27},{5,28},{6,29},{7,30},{8,7},{9,0... | collective-permute-start | bytes 294920 | tf_op jit(solution)/shard_map/ppermute | solution.py:440
  8.9 1.0 %pad_add_fusion.state_ref = f32[69,8,128]{2,1,0:T(8,128)S(1)} fusion(f32[3,8,128]{2,1,0:T(8,128)} %bitcast.16, f32[2,8,128]{2,1,0:T(8,128)} %bitcast.17, f32[8,8,128]{2,1,0:T(8,128)} %bitcast.14, s32[8,8,128]{2,1,0:T(8,128)} %bitcast.15, f32[48,8,128]{2,1,0:T(8,128)} %bitcast.11), kind=kLoop, calls=%fused_computation | loop fusion | flops 353280 | bytes 565248 | tf_op jit(solution)/shard_map/add | solution.py:461
  9.9 4.1 %shard_map.77.blocks_ref = bf16[36,224,384]{2,1,0:T(8,128)(2,1)S(1)} custom-call(f32[69,8,128]{2,1,0:T(8,128)S(1)} %pad_add_fusion.state_ref), custom_call_target="tpu_custom_call" | custom-call | flops 20000000 | bytes 8000000 | tf_op jit(solution)/shard_map/pallas_call | solution.py:464
  14.1 0.0 copy-done
  14.1 0.9 %collective-permute-done.2.front_ref = bf16[8,384,128]{2,1,0:T(8,128)(2,1)S(1)} collective-permute-done((bf16[8,384,128]{2,1,0:T(8,128)(2,1)}, bf16[8,384,128]{2,1,0:T(8,128)(2,1)S(1)}, u32[]{:S(2)}, u32[]{:S(2)}) %collective-permute-start.2) | collective-permute-done | bytes 786464 | tf_op jit(solution)/shard_map/ppermute | solution.py:438
  15.0 2.2 %shard_map.79 = (f32[144,128]{1,0:T(8,128)S(1)}, f32[4,2,128,128]{3,2,1,0:T(8,128)S(1)}) custom-call(bf16[8,384,128]{2,1,0:T(8,128)(2,1)S(1)} %bitcast.10, bf16[8,384,128]{2,1,0:T(8,128)(2,1)S(1)} %collective-permute-done.2.front_ref, bf16[36,224,384]{2,1,0:T(8,128)(2,1)S(1)} %shard_map.77.blocks_ref, f32[144,128]{1,0:T(8,128)S(1)} %get-tuple-element.8.sum_early, ...), custom_call_target="tpu_custom_call" | custom-call | flops 2000000000 | bytes 8000000 | tf_op jit(solution)/shard_map/pallas_call | solution.py:494
  17.2 0.0 collective-permute-done.side_ref
  17.2 0.0 collective-permute-done.1.corner_ref
  17.2 0.6 %shard_map.80 = f32[80,128]{1,0:T(8,128)S(1)} custom-call(bf16[1,384,128]{2,1,0:T(8,128)(2,1)S(1)} %collective-permute-done.side_ref, bf16[1,384,128]{2,1,0:T(8,128)(2,1)S(1)} %collective-permute-done.1.corner_ref, bf16[36,224,384]{2,1,0:T(8,128)(2,1)S(1)} %shard_map.77.blocks_ref, f32[144,128]{1,0:T(8,128)S(1)} %get-tuple-element.10.sum_in, ...), custom_call_target="tpu_custom_call" | custom-call | flops 200000000 | bytes 1000000 | tf_op jit(solution)/shard_map/pallas_call | solution.py:497
  17.9 2.5 %collective-permute-start.3 = (f32[80,128]{1,0:T(8,128)S(1)}, f32[80,128]{1,0:T(8,128)S(1)}, u32[]{:S(2)}, u32[]{:S(2)}) collective-permute-start(f32[80,128]{1,0:T(8,128)S(1)} %shard_map.80), channel_id=1, source_target_pairs={{0,24},{8,16},{16,8},{24,0},{1,25},{9,17},{17,9},{25,1},{2,26},{10... | collective-permute-start | bytes 122888 | tf_op jit(solution)/shard_map/ppermute | solution.py:530
  20.4 0.5 %collective-permute-start.4 = (f32[80,128]{1,0:T(8,128)S(1)}, f32[80,128]{1,0:T(8,128)S(1)}, u32[]{:S(2)}, u32[]{:S(2)}) collective-permute-start(f32[80,128]{1,0:T(8,128)S(1)} %shard_map.80), channel_id=1, source_target_pairs={{0,8},{8,0},{16,24},{24,16},{1,9},{9,1},{17,25},{25,17},{2,10},{10... | collective-permute-start | bytes 122888 | tf_op jit(solution)/shard_map/ppermute | solution.py:530
  20.9 0.5 %collective-permute-start.5 = (f32[80,128]{1,0:T(8,128)S(1)}, f32[80,128]{1,0:T(8,128)S(1)}, u32[]{:S(2)}, u32[]{:S(2)}) collective-permute-start(f32[80,128]{1,0:T(8,128)S(1)} %shard_map.80), channel_id=1, source_target_pairs={{0,16},{8,24},{16,0},{24,8},{1,17},{9,25},{17,1},{25,9},{2,18},{10... | collective-permute-start | bytes 122888 | tf_op jit(solution)/shard_map/ppermute | solution.py:530
  21.4 1.5 %collective-permute-done.3 = f32[80,128]{1,0:T(8,128)S(1)} collective-permute-done((f32[80,128]{1,0:T(8,128)S(1)}, f32[80,128]{1,0:T(8,128)S(1)}, u32[]{:S(2)}, u32[]{:S(2)}) %collective-permute-start.3) | collective-permute-done | bytes 40992 | tf_op jit(solution)/shard_map/ppermute | solution.py:530
  22.9 1.4 %collective-permute-done.4 = f32[80,128]{1,0:T(8,128)S(1)} collective-permute-done((f32[80,128]{1,0:T(8,128)S(1)}, f32[80,128]{1,0:T(8,128)S(1)}, u32[]{:S(2)}, u32[]{:S(2)}) %collective-permute-start.4) | collective-permute-done | bytes 40992 | tf_op jit(solution)/shard_map/ppermute | solution.py:530
  24.4 0.5 %collective-permute-done.5 = f32[80,128]{1,0:T(8,128)S(1)} collective-permute-done((f32[80,128]{1,0:T(8,128)S(1)}, f32[80,128]{1,0:T(8,128)S(1)}, u32[]{:S(2)}, u32[]{:S(2)}) %collective-permute-start.5) | collective-permute-done | bytes 40992 | tf_op jit(solution)/shard_map/ppermute | solution.py:530
  24.9 0.1 collective-permute-start.6
  25.0 1.1 %collective-permute-start.7 = (f32[80,128]{1,0:T(8,128)S(1)}, f32[80,128]{1,0:T(8,128)S(1)}, u32[]{:S(2)}, u32[]{:S(2)}) collective-permute-start(f32[80,128]{1,0:T(8,128)S(1)} %add_add_fusion.1), channel_id=1, source_target_pairs={{0,6},{1,7},{2,4},{3,5},{4,2},{5,3},{6,0},{7,1},{8,14},{9,15},{10,... | collective-permute-start | bytes 122888 | tf_op jit(solution)/shard_map/ppermute | solution.py:530
  26.1 2.4 %collective-permute-start.8 = (f32[80,128]{1,0:T(8,128)S(1)}, f32[80,128]{1,0:T(8,128)S(1)}, u32[]{:S(2)}, u32[]{:S(2)}) collective-permute-start(f32[80,128]{1,0:T(8,128)S(1)} %add_add_fusion.1), channel_id=1, source_target_pairs={{0,2},{1,3},{2,0},{3,1},{4,6},{5,7},{6,4},{7,5},{8,10},{9,11},{10,... | collective-permute-start | bytes 122888 | tf_op jit(solution)/shard_map/ppermute | solution.py:530
  28.5 1.8 %collective-permute-done.6 = f32[80,128]{1,0:T(8,128)S(1)} collective-permute-done((f32[80,128]{1,0:T(8,128)S(1)}, f32[80,128]{1,0:T(8,128)S(1)}, u32[]{:S(2)}, u32[]{:S(2)}) %collective-permute-start.6) | collective-permute-done | bytes 40992 | tf_op jit(solution)/shard_map/ppermute | solution.py:530
  30.3 0.9 %collective-permute-done.7 = f32[80,128]{1,0:T(8,128)S(1)} collective-permute-done((f32[80,128]{1,0:T(8,128)S(1)}, f32[80,128]{1,0:T(8,128)S(1)}, u32[]{:S(2)}, u32[]{:S(2)}) %collective-permute-start.7) | collective-permute-done | bytes 40992 | tf_op jit(solution)/shard_map/ppermute | solution.py:530
  31.2 0.0 collective-permute-done.8
  31.2 0.1 collective-permute-start.9
  31.3 1.2 %collective-permute-done.9.other_ref = f32[80,128]{1,0:T(8,128)S(1)} collective-permute-done((f32[80,128]{1,0:T(8,128)S(1)}, f32[80,128]{1,0:T(8,128)S(1)}, u32[]{:S(2)}, u32[]{:S(2)}) %collective-permute-start.9) | collective-permute-done | bytes 40992 | tf_op jit(solution)/shard_map/ppermute | solution.py:530
  32.5 0.8 %shard_map.81 = (f32[128,128]{1,0:T(8,128)}, f32[1,128]{1,0:T(1,128)}) custom-call(f32[80,128]{1,0:T(8,128)S(1)} %add_add_fusion.mine_ref, f32[80,128]{1,0:T(8,128)S(1)} %collective-permute-done.9.other_ref), custom_call_target="tpu_custom_call" | custom-call | tf_op jit(solution)/shard_map/pallas_call | solution.py:515
  (3 shorter events, 0.0 us)
Async XLA Ops:
  0.6 13.5 %copy-start = (bf16[1,8,3,128,128]{4,3,2,1,0:T(8,128)(2,1)S(1)}, bf16[1,8,3,128,128]{4,3,2,1,0:T(8,128)(2,1)}, u32[]{:S(2)}) copy-start(bf16[1,8,3,128,128]{4,3,2,1,0:T(8,128)(2,1)} %param.6) | copy-start | bytes 2359300
  0.6 14.4 %collective-permute-start.2 = (bf16[8,384,128]{2,1,0:T(8,128)(2,1)}, bf16[8,384,128]{2,1,0:T(8,128)(2,1)S(1)}, u32[]{:S(2)}, u32[]{:S(2)}) collective-permute-start(bf16[8,384,128]{2,1,0:T(8,128)(2,1)} %bitcast.8), channel_id=1, source_target_pairs={{0,7},{1,0},{2,1},{3,2},{4,3},{5,4},{6,5},{7,6},{8,15},{9,8},{10,9... | collective-permute-start | bytes 2359304 | tf_op jit(solution)/shard_map/ppermute | solution.py:438
  6.1 11.1 %collective-permute-start = (bf16[1,384,128]{2,1,0:T(8,128)(2,1)S(1)}, bf16[1,384,128]{2,1,0:T(8,128)(2,1)S(1)}, u32[]{:S(2)}, u32[]{:S(2)}) collective-permute-start(bf16[1,384,128]{2,1,0:T(8,128)(2,1)S(1)} %bitcast.12), channel_id=1, source_target_pairs={{0,24},{8,0},{16,8},{24,16},{1,25},{9,1},{17,9},{25,17},{2,26},{10... | collective-permute-start | bytes 294920 | tf_op jit(solution)/shard_map/ppermute | solution.py:449
  8.6 8.7 %collective-permute-start.1 = (bf16[1,384,128]{2,1,0:T(8,128)(2,1)S(1)}, bf16[1,384,128]{2,1,0:T(8,128)(2,1)S(1)}, u32[]{:S(2)}, u32[]{:S(2)}) collective-permute-start(bf16[1,384,128]{2,1,0:T(8,128)(2,1)S(1)} %bitcast.13), channel_id=1, source_target_pairs={{0,31},{1,24},{2,25},{3,26},{4,27},{5,28},{6,29},{7,30},{8,7},{9,0... | collective-permute-start | bytes 294920 | tf_op jit(solution)/shard_map/ppermute | solution.py:440
  17.9 5.1 %collective-permute-start.3 = (f32[80,128]{1,0:T(8,128)S(1)}, f32[80,128]{1,0:T(8,128)S(1)}, u32[]{:S(2)}, u32[]{:S(2)}) collective-permute-start(f32[80,128]{1,0:T(8,128)S(1)} %shard_map.80), channel_id=1, source_target_pairs={{0,24},{8,16},{16,8},{24,0},{1,25},{9,17},{17,9},{25,1},{2,26},{10... | collective-permute-start | bytes 122888 | tf_op jit(solution)/shard_map/ppermute | solution.py:530
  20.4 4.0 %collective-permute-start.4 = (f32[80,128]{1,0:T(8,128)S(1)}, f32[80,128]{1,0:T(8,128)S(1)}, u32[]{:S(2)}, u32[]{:S(2)}) collective-permute-start(f32[80,128]{1,0:T(8,128)S(1)} %shard_map.80), channel_id=1, source_target_pairs={{0,8},{8,0},{16,24},{24,16},{1,9},{9,1},{17,25},{25,17},{2,10},{10... | collective-permute-start | bytes 122888 | tf_op jit(solution)/shard_map/ppermute | solution.py:530
  20.9 4.0 %collective-permute-start.5 = (f32[80,128]{1,0:T(8,128)S(1)}, f32[80,128]{1,0:T(8,128)S(1)}, u32[]{:S(2)}, u32[]{:S(2)}) collective-permute-start(f32[80,128]{1,0:T(8,128)S(1)} %shard_map.80), channel_id=1, source_target_pairs={{0,16},{8,24},{16,0},{24,8},{1,17},{9,25},{17,1},{25,9},{2,18},{10... | collective-permute-start | bytes 122888 | tf_op jit(solution)/shard_map/ppermute | solution.py:530
  24.9 5.4 %collective-permute-start.6 = (f32[80,128]{1,0:T(8,128)S(1)}, f32[80,128]{1,0:T(8,128)S(1)}, u32[]{:S(2)}, u32[]{:S(2)}) collective-permute-start(f32[80,128]{1,0:T(8,128)S(1)} %add_add_fusion.1), channel_id=1, source_target_pairs={{0,4},{1,5},{2,6},{3,7},{4,0},{5,1},{6,2},{7,3},{8,12},{9,13},{10,... | collective-permute-start | bytes 122888 | tf_op jit(solution)/shard_map/ppermute | solution.py:530
  25.0 6.2 %collective-permute-start.7 = (f32[80,128]{1,0:T(8,128)S(1)}, f32[80,128]{1,0:T(8,128)S(1)}, u32[]{:S(2)}, u32[]{:S(2)}) collective-permute-start(f32[80,128]{1,0:T(8,128)S(1)} %add_add_fusion.1), channel_id=1, source_target_pairs={{0,6},{1,7},{2,4},{3,5},{4,2},{5,3},{6,0},{7,1},{8,14},{9,15},{10,... | collective-permute-start | bytes 122888 | tf_op jit(solution)/shard_map/ppermute | solution.py:530
  26.1 5.1 %collective-permute-start.8 = (f32[80,128]{1,0:T(8,128)S(1)}, f32[80,128]{1,0:T(8,128)S(1)}, u32[]{:S(2)}, u32[]{:S(2)}) collective-permute-start(f32[80,128]{1,0:T(8,128)S(1)} %add_add_fusion.1), channel_id=1, source_target_pairs={{0,2},{1,3},{2,0},{3,1},{4,6},{5,7},{6,4},{7,5},{8,10},{9,11},{10,... | collective-permute-start | bytes 122888 | tf_op jit(solution)/shard_map/ppermute | solution.py:530
  31.2 1.3 %collective-permute-start.9 = (f32[80,128]{1,0:T(8,128)S(1)}, f32[80,128]{1,0:T(8,128)S(1)}, u32[]{:S(2)}, u32[]{:S(2)}) collective-permute-start(f32[80,128]{1,0:T(8,128)S(1)} %add_add_fusion.mine_ref), channel_id=1, source_target_pairs={{0,1},{1,0},{2,3},{3,2},{4,5},{5,4},{6,7},{7,6},{8,9},{9,8},{10,11... | collective-permute-start | bytes 122888 | tf_op jit(solution)/shard_map/ppermute | solution.py:530
